TPU v7x, 32 devices: a whole 2x2x4 slice. The times are simulated.
32 devices in a mesh: aa: 4 (over x, core), ba: 2 (over y), col: 4 (over z).
Axes of the slice: x: 2, y: 2, z: 4, core: 2. Of those that a mesh axis runs over, the one named last changes fastest.
Arguments:
- field: float32 [96, 1024, 1024], P('col', 'aa', 'ba'), may hold values from -6 to 6
- factor: float32 [1024, 256], P('aa'), may hold values from -0.1875 to 0.1875
Outputs:
- gram: float32 [1024, 1024], P('ba', ('aa', 'col'))
All inputs are finite; a program needn't handle non-finite values.
Results may differ from a plain program's by a relative error of at most 0.000076.
Values sent between devices are 32-bit elements; how exact they have to be, the bound alone decides.
No kernel may reach another device: no remote copies, remote signals or barrier semaphores. Data moves between devices by JAX's collectives and lax.ppermute only.
A program may use at most 64 MiB of HBM per device.

v0:
```python
import jax
import jax.numpy as jnp
from jax import lax
from jax.sharding import PartitionSpec as P


def shards(field, factor):
    ranks = factor.shape[1]
    depth = field.shape[0] * lax.axis_size("col")
    partial_core = jnp.einsum("kab,ar->krb", field, factor, precision=lax.Precision.HIGHEST)
    core = lax.psum_scatter(partial_core, "aa", scatter_dimension=1, tiled=True)
    block = jnp.einsum(
        "krb,krc->bc",
        core,
        lax.all_gather(core, "ba", axis=2, tiled=True),
        precision=lax.Precision.HIGHEST,
    )
    halfway = lax.psum_scatter(block, "aa", scatter_dimension=1, tiled=True)
    summed = lax.psum_scatter(halfway, "col", scatter_dimension=1, tiled=True)
    return summed / jnp.sqrt(jnp.float32(ranks * depth))


def solution(mesh):
    placed = (P("col", "aa", "ba"), P("aa", None))
    return jax.shard_map(
        shards, mesh=mesh, in_specs=placed, out_specs=P("ba", ("aa", "col")), check_vma=False
    )
```

profile of v0, /device:TPU:0, one launch (start us, length us, event | category | flops | bytes accessed | tf_op | source)
XLA Modules:
  0.0 286.2 jit_solution(2328400789818356903)
XLA Ops:
  6.5 0.0 copy-start
  6.5 0.0 reduce-scatter.6.cloned.1.call-start
  6.5 0.9 copy-done
  7.5 17.1 %convolution_bitcast_fusion = f32[24,256,512]{2,1,0:T(8,128)} fusion(f32[24,256,512]{2,1,0:T(8,128)} %param.2, f32[256,256]{1,0:T(8,128)S(1)} %copy-done), kind=kOutput, calls=%fused_computation | convolution fusion | flops 9663676416 | bytes 25427968 | tf_op jit(solution)/shard_map/kab,ar->krb/dot_general | solution.py:10
  24.5 0.0 reduce-scatter.6.cloned.1.call-update
  24.6 0.0 all-gather.2.cloned.1.call-start
  24.6 101.8 %reduce-scatter.6.cloned.1.call-done = f32[24,64,512]{2,1,0:T(8,128)} async-done(((f32[24,256,512]{2,1,0:T(8,128)}), f32[24,64,512]{2,1,0:T(8,128)}) %reduce-scatter.6.cloned.1.call-update) | async-done | bytes 3145744 | tf_op jit(solution)/shard_map/reduce_scatter | solution.py:11
  126.4 0.0 all-gather.2.cloned.1.call-update
  126.5 0.0 reduce-scatter.8.cloned.1.call-start
  126.5 81.9 %all-gather.2.cloned.1.call-done = f32[24,64,1024]{2,1,0:T(8,128)} async-done(((f32[24,64,512]{2,1,0:T(8,128)}), f32[24,64,1024]{2,1,0:T(8,128)}) %all-gather.2.cloned.1.call-update) | async-done | bytes 6291472 | tf_op jit(solution)/shard_map/all_gather | solution.py:15
  208.4 14.2 %convolution_bitcast_fusion.1 = f32[512,1024]{1,0:T(8,128)} fusion(f32[24,64,512]{2,1,0:T(8,128)} %reduce-scatter.6.cloned.1.call-done, f32[24,64,1024]{2,1,0:T(8,128)} %all-gather.2.cloned.1.call-done), kind=kOutput, calls=%fused_computation.1 | convolution fusion | flops 9663676416 | bytes 11534336 | tf_op jit(solution)/shard_map/krb,krc->bc/dot_general | solution.py:12
  222.6 0.0 reduce-scatter.8.cloned.1.call-update
  222.6 0.0 reduce-scatter.10.cloned.1.call-start
  222.6 31.5 %reduce-scatter.8.cloned.1.call-done = f32[512,256]{1,0:T(8,128)} async-done(((f32[512,1024]{1,0:T(8,128)}), f32[512,256]{1,0:T(8,128)}) %reduce-scatter.8.cloned.1.call-update) | async-done | bytes 524304 | tf_op jit(solution)/shard_map/reduce_scatter | solution.py:18
  254.2 2.0 copy.11
  256.2 0.0 reduce-scatter.10.cloned.1.call-update
  256.2 21.8 %reduce-scatter.10.cloned.1.call-done = f32[64,512]{1,0:T(8,128)} async-done(((f32[256,512]{1,0:T(8,128)}), f32[64,512]{1,0:T(8,128)}) %reduce-scatter.10.cloned.1.call-update) | async-done | bytes 131088
  278.1 1.6 bitcast_multiply_fusion
Async XLA Ops:
  6.5 1.0 copy-start
  6.5 119.9 %reduce-scatter.6.cloned.1.call-start = ((), (), s32[]{:S(2)}) async-start(), calls=%async_computation.3 | async-start | bytes 15728640 | tf_op jit(solution)/shard_map/reduce_scatter | solution.py:11
  24.6 183.9 %all-gather.2.cloned.1.call-start = ((), (), s32[]{:S(2)}) async-start(), calls=%async_computation.4 | async-start | bytes 9437184 | tf_op jit(solution)/shard_map/all_gather | solution.py:15
  126.5 127.7 %reduce-scatter.8.cloned.1.call-start = ((), (), s32[]{:S(2)}) async-start(), calls=%async_computation.5 | async-start | bytes 2621440 | tf_op jit(solution)/shard_map/reduce_scatter | solution.py:18
  222.6 55.5 %reduce-scatter.10.cloned.1.call-start = ((), (), s32[]{:S(2)}) async-start(), calls=%async_computation.6 | async-start | bytes 655360
Sparse Core Ops, SparseCore 0:
  24.7 101.7 reduce-scatter.5
  128.0 80.3 all-gather.1
  222.7 31.4 reduce-scatter.7
  256.4 21.6 reduce-scatter.9
where the time goes:
time: 286 us
  waiting for transfers between devices  237 us (83%)
  matrix products  31.2 us (11%)
  between operations  13.1 us (5%)
  local copies, waits for them, and re-layouts  2.99 us (1%)
    reduce_scatter x1, waiting for transfers between devices, shards(): core = lax.psum_scatter(partial_core, 'aa', scatter_dimension=1, tiled=True)  102 us
    all_gather x1, waiting for transfers between devices, shards(): lax.all_gather(core, 'ba', axis=2, tiled=True)  81.9 us
    reduce_scatter x1, waiting for transfers between devices, shards(): halfway = lax.psum_scatter(block, 'aa', scatter_dimension=1, tiled=True)  31.5 us
    unnamed x5, waiting for transfers between devices  21.9 us
    dot_general x1, matrix products, shards(): jnp.einsum('kab,ar->krb', field, factor, precision=lax.Precision.HIGHEST)  17.1 us
    dot_general x1, matrix products, shards(): jnp.einsum('krb,krc->bc', core, lax.all_gather(core, 'ba', axis=2, tiled=...  14.2 us
  transfers between devices with their start and end apart: 4, of which 4 were waited for; matrix products, arithmetic and copies ran while one was open for 0% of the time, Pallas kernels for 0%

commit v1 on v0

v1 whole, which is shorter than its diff:
```python
import jax
import jax.numpy as jnp
from jax import lax
from jax.sharding import PartitionSpec as P

MULTIPLY = lax.Precision.HIGH


def swap(x, axis, bit):
    size = lax.axis_size(axis)
    return lax.ppermute(x, axis, [(i, i ^ bit) for i in range(size)])


def bits_of(size):
    return [1 << n for n in range(size.bit_length() - 1)]


def summed_over_aa(parts, bits):
    for bit in bits:
        kept = {d: p for d, p in parts.items() if not d & bit}
        for d in reversed(sorted(kept)):
            kept[d] = kept[d] + swap(parts[d | bit], "aa", bit)
        parts = kept
    return parts[0]


def shards(field, factor):
    aa, ba, col = (lax.axis_size(n) for n in ("aa", "ba", "col"))
    me_a, me_b, me_c = (lax.axis_index(n) for n in ("aa", "ba", "col"))
    ranks = factor.shape[1]
    depth = field.shape[0] * col
    each = field.shape[0] // aa
    width = field.shape[2]
    gram = jnp.zeros((ba * width, width), jnp.float32)
    for step in range(each):
        terms = {}
        for d in reversed(range(aa)):
            layer = lax.dynamic_index_in_dim(field, (me_a ^ d) * each + step, 0, keepdims=False)
            terms[d] = jnp.einsum("ab,ar->rb", layer, factor, precision=MULTIPLY)
        core = summed_over_aa(terms, bits_of(aa))
        others = {0: core}
        for d in range(1, ba):
            others[d] = swap(core, "ba", d)
        stacked = jnp.stack([others[d] for d in range(ba)])
        ordered = jnp.concatenate(
            [lax.dynamic_index_in_dim(stacked, me_b ^ y, 0, keepdims=False) for y in range(ba)], axis=1
        )
        gram = gram + jnp.einsum("rc,rb->cb", ordered, core, precision=MULTIPLY)
    rest = ba * width // (aa * col)
    gram = gram.reshape(aa, col, rest, width)
    pieces = {d: lax.dynamic_index_in_dim(gram, me_a ^ d, 0, keepdims=False) for d in range(aa)}
    low = {d: pieces[d] + swap(pieces[d | 1], "aa", 1) for d in pieces if not d & 1}
    tall = jnp.stack([low[d] for d in sorted(low)], axis=1)
    total = lax.dynamic_index_in_dim(tall, me_c, 0, keepdims=False)
    for d in range(1, col):
        total = total + swap(lax.dynamic_index_in_dim(tall, me_c ^ d, 0, keepdims=False), "col", d)
    mine = summed_over_aa({d: total[n] for n, d in enumerate(sorted(low))}, bits_of(aa)[1:])
    return mine.T / jnp.sqrt(jnp.float32(ranks * depth))


def solution(mesh):
    placed = (P("col", "aa", "ba"), P("aa", None))
    return jax.shard_map(
        shards, mesh=mesh, in_specs=placed, out_specs=P("ba", ("aa", "col")), check_vma=False
    )
```

time: 286 us -> 193 us (0.67); the launches traced: 286 us -> 190 us
  waiting for transfers between devices: 237 us -> 105 us
  starting transfers between devices: 0.12 us -> 25.6 us
  matrix products: 31.2 us -> 53.2 us
  between operations: 13.1 us -> 0.46 us
    reduce_scatter x2 -> x0, waiting for transfers between devices: 133 us -> none  [the longest x1 102 us: shards(): core = lax.psum_scatter(partial_core, 'aa', scatter_dimension=1, tiled=True)]
    ppermute x0 -> x30, waiting for transfers between devices: none -> 105 us  [swap(): return lax.ppermute(x, axis, [(i, i ^ bit) for i in range(size)])]
    all_gather x1 -> x0, waiting for transfers between devices: 81.9 us -> none  [shards(): lax.all_gather(core, 'ba', axis=2, tiled=True)]
    ppermute x0 -> x30, starting transfers between devices: none -> 25.6 us  [swap(): return lax.ppermute(x, axis, [(i, i ^ bit) for i in range(size)])]
    dot_general x2 -> x30, matrix products: 31.2 us -> 53.2 us  [the longest x24 46.7 us: shards(): terms[d] = jnp.einsum('ab,ar->rb', layer, factor, precision=MULTIPLY)]
    unnamed x5 -> x0, waiting for transfers between devices: 21.9 us -> none
  transfers between devices with their start and end apart: 4 -> 30, of which waited for: 4 -> 15; matrix products, arithmetic and copies ran while one was open for 0% -> 27% of each run, Pallas kernels for 0% -> 0%
where the time goes in v1:
time: 193 us; the launch traced here: 190 us
  waiting for transfers between devices  105 us (54%)
  matrix products  53.2 us (28%)
  starting transfers between devices  25.6 us (13%)
  other arithmetic  3.48 us (2%)
  local copies, waits for them, and re-layouts  2.66 us (1%)
    ppermute x30, waiting for transfers between devices, swap(): return lax.ppermute(x, axis, [(i, i ^ bit) for i in range(size)])  105 us
    dot_general x24, matrix products, shards(): terms[d] = jnp.einsum('ab,ar->rb', layer, factor, precision=MULTIPLY)  46.7 us
    ppermute x30, starting transfers between devices, swap(): return lax.ppermute(x, axis, [(i, i ^ bit) for i in range(size)])  25.6 us
    dot_general x6, matrix products, shards(): gram = gram + jnp.einsum('rc,rb->cb', ordered, core, precision=MULTIPLY)  6.5 us
  transfers between devices with their start and end apart: 30, of which 15 were waited for; matrix products, arithmetic and copies ran while one was open for 27% of the time, Pallas kernels for 0%

profile of v1, /device:TPU:0, one launch (start us, length us, event | category | flops | bytes accessed | tf_op | source)
XLA Modules:
  0.0 189.9 jit_solution(11136385362315470761)
XLA Ops:
  1.0 2.5 %convolution_bitcast_fusion.12 = f32[256,512]{0,1:T(8,128)} fusion(f32[256,256]{1,0:T(8,128)S(1)} %copy-done, f32[24,256,512]{2,1,0:T(8,128)} %param.2, s32[]{:T(128)S(6)} %select_n.129), kind=kOutput, calls=%fused_computation.45 | convolution fusion | flops 201326592 | bytes 1310724 | tf_op jit(solution)/shard_map/ab,ar->rb/dot_general | solution.py:39
  5.7 2.5 %convolution_bitcast_fusion.8 = f32[256,512]{0,1:T(8,128)} fusion(f32[256,256]{1,0:T(8,128)S(1)} %copy-done, f32[24,256,512]{2,1,0:T(8,128)} %param.2, s32[]{:T(128)S(6)} %select_n.133), kind=kOutput, calls=%fused_computation.41 | convolution fusion | flops 201326592 | bytes 1310724 | tf_op jit(solution)/shard_map/ab,ar->rb/dot_general | solution.py:39
  10.4 2.5 %convolution_bitcast_fusion.16 = f32[256,512]{0,1:T(8,128)} fusion(f32[256,256]{1,0:T(8,128)S(1)} %copy-done, f32[24,256,512]{2,1,0:T(8,128)} %param.2, s32[]{:T(128)S(6)} %select_n.125), kind=kOutput, calls=%fused_computation.49 | convolution fusion | flops 201326592 | bytes 1310724 | tf_op jit(solution)/shard_map/ab,ar->rb/dot_general | solution.py:39
  13.3 2.5 %convolution_bitcast_fusion.18 = f32[256,512]{0,1:T(8,128)} fusion(f32[256,256]{1,0:T(8,128)S(1)} %copy-done, f32[24,256,512]{2,1,0:T(8,128)} %param.2, s32[]{:T(128)S(6)} %select_n.123), kind=kOutput, calls=%fused_computation.51 | convolution fusion | flops 201326592 | bytes 1310724 | tf_op jit(solution)/shard_map/ab,ar->rb/dot_general | solution.py:39
  15.7 2.5 %convolution_bitcast_fusion.4 = f32[256,512]{0,1:T(8,128)} fusion(f32[256,256]{1,0:T(8,128)S(1)} %copy-done, f32[24,256,512]{2,1,0:T(8,128)} %param.2, s32[]{:T(128)S(6)} %select_n.137), kind=kOutput, calls=%fused_computation.37 | convolution fusion | flops 201326592 | bytes 1310724 | tf_op jit(solution)/shard_map/ab,ar->rb/dot_general | solution.py:39
  18.2 2.5 %convolution_bitcast_fusion.6 = f32[256,512]{0,1:T(8,128)} fusion(f32[256,256]{1,0:T(8,128)S(1)} %copy-done, f32[24,256,512]{2,1,0:T(8,128)} %param.2, s32[]{:T(128)S(6)} %select_n.135), kind=kOutput, calls=%fused_computation.39 | convolution fusion | flops 201326592 | bytes 1310724 | tf_op jit(solution)/shard_map/ab,ar->rb/dot_general | solution.py:39
  20.6 2.5 %convolution_bitcast_fusion = f32[256,512]{0,1:T(8,128)} fusion(f32[256,256]{1,0:T(8,128)S(1)} %copy-done, f32[24,256,512]{2,1,0:T(8,128)} %param.2, s32[]{:T(128)S(6)} %select_n.141), kind=kOutput, calls=%fused_computation.33 | convolution fusion | flops 201326592 | bytes 1310724 | tf_op jit(solution)/shard_map/ab,ar->rb/dot_general | solution.py:39
  24.8 2.5 %convolution_bitcast_fusion.20 = f32[256,512]{0,1:T(8,128)} fusion(f32[256,256]{1,0:T(8,128)S(1)} %copy-done, f32[24,256,512]{2,1,0:T(8,128)} %param.2, s32[]{:T(128)S(6)} %select_n.119), kind=kOutput, calls=%fused_computation.53 | convolution fusion | flops 201326592 | bytes 1310724 | tf_op jit(solution)/shard_map/ab,ar->rb/dot_general | solution.py:39
  29.1 1.8 fusion.8
  31.4 1.8 fusion.11
  33.4 1.8 fusion.5
  35.2 3.0 %collective-permute-start.10 = (f32[256,512]{0,1:T(8,128)S(1)}, f32[256,512]{0,1:T(8,128)S(1)}, u32[]{:S(2)}, u32[]{:S(2)}) collective-permute-start(f32[256,512]{0,1:T(8,128)S(1)} %fusion.8), channel_id=1, source_target_pairs={{0,16},{8,24},{16,0},{24,8},{1,17},{9,25},{17,1},{25,9},{2,18},{10... | collective-permute-start | bytes 1572872 | tf_op jit(solution)/shard_map/ppermute | solution.py:11
  43.9 7.0 %collective-permute-done.10 = f32[256,512]{0,1:T(8,128)S(1)} collective-permute-done((f32[256,512]{0,1:T(8,128)S(1)}, f32[256,512]{0,1:T(8,128)S(1)}, u32[]{:S(2)}, u32[]{:S(2)}) %collective-permute-start.10) | collective-permute-done | bytes 524320 | tf_op jit(solution)/shard_map/ppermute | solution.py:11
  50.9 2.1 %collective-permute-start.6 = (f32[256,512]{0,1:T(8,128)S(1)}, f32[256,512]{0,1:T(8,128)S(1)}, u32[]{:S(2)}, u32[]{:S(2)}) collective-permute-start(f32[256,512]{0,1:T(8,128)S(1)} %fusion.5), channel_id=1, source_target_pairs={{0,16},{8,24},{16,0},{24,8},{1,17},{9,25},{17,1},{25,9},{2,18},{10... | collective-permute-start | bytes 1572872 | tf_op jit(solution)/shard_map/ppermute | solution.py:11
  54.9 7.2 %collective-permute-done.14 = f32[256,512]{0,1:T(8,128)S(1)} collective-permute-done((f32[256,512]{0,1:T(8,128)S(1)}, f32[256,512]{0,1:T(8,128)S(1)}, u32[]{:S(2)}, u32[]{:S(2)}) %collective-permute-start.14) | collective-permute-done | bytes 524320 | tf_op jit(solution)/shard_map/ppermute | solution.py:11
  62.2 2.1 %collective-permute-start.18 = (f32[256,512]{0,1:T(8,128)S(1)}, f32[256,512]{0,1:T(8,128)S(1)}, u32[]{:S(2)}, u32[]{:S(2)}) collective-permute-start(f32[256,512]{0,1:T(8,128)S(1)} %fusion.14), channel_id=1, source_target_pairs={{0,16},{8,24},{16,0},{24,8},{1,17},{9,25},{17,1},{25,9},{2,18},{10... | collective-permute-start | bytes 1572872 | tf_op jit(solution)/shard_map/ppermute | solution.py:11
  66.0 7.4 %collective-permute-done.6 = f32[256,512]{0,1:T(8,128)S(1)} collective-permute-done((f32[256,512]{0,1:T(8,128)S(1)}, f32[256,512]{0,1:T(8,128)S(1)}, u32[]{:S(2)}, u32[]{:S(2)}) %collective-permute-start.6) | collective-permute-done | bytes 524320 | tf_op jit(solution)/shard_map/ppermute | solution.py:11
  73.4 2.1 %collective-permute-start.22 = (f32[256,512]{0,1:T(8,128)S(1)}, f32[256,512]{0,1:T(8,128)S(1)}, u32[]{:S(2)}, u32[]{:S(2)}) collective-permute-start(f32[256,512]{0,1:T(8,128)S(1)} %fusion.17), channel_id=1, source_target_pairs={{0,16},{8,24},{16,0},{24,8},{1,17},{9,25},{17,1},{25,9},{2,18},{10... | collective-permute-start | bytes 1572872 | tf_op jit(solution)/shard_map/ppermute | solution.py:11
  77.2 7.4 %collective-permute-done.18 = f32[256,512]{0,1:T(8,128)S(1)} collective-permute-done((f32[256,512]{0,1:T(8,128)S(1)}, f32[256,512]{0,1:T(8,128)S(1)}, u32[]{:S(2)}, u32[]{:S(2)}) %collective-permute-start.18) | collective-permute-done | bytes 524320 | tf_op jit(solution)/shard_map/ppermute | solution.py:11
  84.6 2.1 %collective-permute-start.11 = (f32[256,512]{0,1:T(8,128)S(1)}, f32[256,512]{0,1:T(8,128)S(1)}, u32[]{:S(2)}, u32[]{:S(2)}) collective-permute-start(f32[256,512]{0,1:T(8,128)S(1)} %fusion.7), channel_id=1, source_target_pairs={{0,4},{4,0},{1,5},{5,1},{2,6},{6,2},{3,7},{7,3},{8,12},{12,8},{9,1... | collective-permute-start | bytes 1572872 | tf_op jit(solution)/shard_map/ppermute | solution.py:11
  88.5 7.4 %collective-permute-done.22 = f32[256,512]{0,1:T(8,128)S(1)} collective-permute-done((f32[256,512]{0,1:T(8,128)S(1)}, f32[256,512]{0,1:T(8,128)S(1)}, u32[]{:S(2)}, u32[]{:S(2)}) %collective-permute-start.22) | collective-permute-done | bytes 524320 | tf_op jit(solution)/shard_map/ppermute | solution.py:11
  95.9 2.1 %collective-permute-start.7 = (f32[256,512]{0,1:T(8,128)S(1)}, f32[256,512]{0,1:T(8,128)S(1)}, u32[]{:S(2)}, u32[]{:S(2)}) collective-permute-start(f32[256,512]{0,1:T(8,128)S(1)} %fusion.4), channel_id=1, source_target_pairs={{0,4},{4,0},{1,5},{5,1},{2,6},{6,2},{3,7},{7,3},{8,12},{12,8},{9,1... | collective-permute-start | bytes 1572872 | tf_op jit(solution)/shard_map/ppermute | solution.py:11
  99.7 6.8 %collective-permute-done.2 = f32[256,512]{0,1:T(8,128)S(1)} collective-permute-done((f32[256,512]{0,1:T(8,128)S(1)}, f32[256,512]{0,1:T(8,128)S(1)}, u32[]{:S(2)}, u32[]{:S(2)}) %collective-permute-start.2) | collective-permute-done | bytes 524320 | tf_op jit(solution)/shard_map/ppermute | solution.py:11
  112.2 9.8 %collective-permute-done.7 = f32[256,512]{0,1:T(8,128)S(1)} collective-permute-done((f32[256,512]{0,1:T(8,128)S(1)}, f32[256,512]{0,1:T(8,128)S(1)}, u32[]{:S(2)}, u32[]{:S(2)}) %collective-permute-start.7) | collective-permute-done | bytes 524320 | tf_op jit(solution)/shard_map/ppermute | solution.py:11
  124.3 9.0 %collective-permute-done.19 = f32[256,512]{0,1:T(8,128)S(1)} collective-permute-done((f32[256,512]{0,1:T(8,128)S(1)}, f32[256,512]{0,1:T(8,128)S(1)}, u32[]{:S(2)}, u32[]{:S(2)}) %collective-permute-start.19) | collective-permute-done | bytes 524320 | tf_op jit(solution)/shard_map/ppermute | solution.py:11
  133.3 11.2 %collective-permute-done.23 = f32[256,512]{0,1:T(8,128)S(1)} collective-permute-done((f32[256,512]{0,1:T(8,128)S(1)}, f32[256,512]{0,1:T(8,128)S(1)}, u32[]{:S(2)}, u32[]{:S(2)}) %collective-permute-start.23) | collective-permute-done | bytes 524320 | tf_op jit(solution)/shard_map/ppermute | solution.py:11
  147.0 6.6 %collective-permute-done.3 = f32[256,512]{0,1:T(8,128)S(1)} collective-permute-done((f32[256,512]{0,1:T(8,128)S(1)}, f32[256,512]{0,1:T(8,128)S(1)}, u32[]{:S(2)}, u32[]{:S(2)}) %collective-permute-start.3) | collective-permute-done | bytes 524320 | tf_op jit(solution)/shard_map/ppermute | solution.py:11
  156.6 2.3 %collective-permute-done.24 = f32[4,64,512]{2,1,0:T(8,128)S(1)} collective-permute-done((f32[4,64,512]{2,1,0:T(8,128)}, f32[4,64,512]{2,1,0:T(8,128)S(1)}, u32[]{:S(2)}, u32[]{:S(2)}) %collective-permute-start.24) | collective-permute-done | bytes 524320 | tf_op jit(solution)/shard_map/ppermute | solution.py:11
  162.8 2.6 %collective-permute-start.27 = (f32[2,64,512]{2,1,0:T(8,128)S(1)}, f32[2,64,512]{2,1,0:T(8,128)S(1)}, u32[]{:S(2)}, u32[]{:S(2)}) collective-permute-start(f32[2,64,512]{2,1,0:T(8,128)S(1)} %get-tuple-element.10), channel_id=1, source_target_pairs={{0,2},{1,3},{2,0},{3,1},{4,6},{5,7},{6,4},{7,5},{8,10},{9,11},{10,... | collective-permute-start | bytes 786440 | tf_op jit(solution)/shard_map/ppermute | solution.py:11
  165.7 9.0 %collective-permute-done.26 = f32[2,64,512]{2,1,0:T(8,128)S(1)} collective-permute-done((f32[2,64,512]{2,1,0:T(8,128)S(1)}, f32[2,64,512]{2,1,0:T(8,128)S(1)}, u32[]{:S(2)}, u32[]{:S(2)}) %collective-permute-start.26) | collective-permute-done | bytes 262176 | tf_op jit(solution)/shard_map/ppermute | solution.py:11
  174.6 9.5 %collective-permute-done.27 = f32[2,64,512]{2,1,0:T(8,128)S(1)} collective-permute-done((f32[2,64,512]{2,1,0:T(8,128)S(1)}, f32[2,64,512]{2,1,0:T(8,128)S(1)}, u32[]{:S(2)}, u32[]{:S(2)}) %collective-permute-start.27) | collective-permute-done | bytes 262176 | tf_op jit(solution)/shard_map/ppermute | solution.py:11
  185.8 3.5 %collective-permute-done.29 = f32[64,512]{1,0:T(8,128)S(1)} collective-permute-done((f32[64,512]{1,0:T(8,128)S(1)}, f32[64,512]{1,0:T(8,128)S(1)}, u32[]{:S(2)}, u32[]{:S(2)}) %collective-permute-start.29) | collective-permute-done | bytes 131104 | tf_op jit(solution)/shard_map/ppermute | solution.py:11
  (72 shorter events, 44.4 us)
Async XLA Ops:
  0.0 1.0 copy-start
  3.4 25.5 %collective-permute-start.9 = (f32[256,512]{0,1:T(8,128)}, f32[256,512]{0,1:T(8,128)}, u32[]{:S(2)}, u32[]{:S(2)}) collective-permute-start(f32[256,512]{0,1:T(8,128)} %convolution_bitcast_fusion.12), channel_id=1, source_target_pairs={{0,8},{8,0},{16,24},{24,16},{1,9},{9,1},{17,25},{25,17},{2,10},{10... | collective-permute-start | bytes 1572872 | tf_op jit(solution)/shard_map/ppermute | solution.py:11
  5.5 37.9 %collective-permute-start.8 = (f32[256,512]{0,1:T(8,128)S(1)}, f32[256,512]{0,1:T(8,128)S(1)}, u32[]{:S(2)}, u32[]{:S(2)}) collective-permute-start(f32[256,512]{0,1:T(8,128)S(1)} %convolution_bitcast_fusion.14), channel_id=1, source_target_pairs={{0,8},{8,0},{16,24},{24,16},{1,9},{9,1},{17,25},{25,17},{2,10},{10... | collective-permute-start | bytes 1572872 | tf_op jit(solution)/shard_map/ppermute | solution.py:11
  8.1 22.8 %collective-permute-start.13 = (f32[256,512]{0,1:T(8,128)}, f32[256,512]{0,1:T(8,128)}, u32[]{:S(2)}, u32[]{:S(2)}) collective-permute-start(f32[256,512]{0,1:T(8,128)} %convolution_bitcast_fusion.8), channel_id=1, source_target_pairs={{0,8},{8,0},{16,24},{24,16},{1,9},{9,1},{17,25},{25,17},{2,10},{10... | collective-permute-start | bytes 1572872 | tf_op jit(solution)/shard_map/ppermute | solution.py:11
  10.2 44.4 %collective-permute-start.12 = (f32[256,512]{0,1:T(8,128)S(1)}, f32[256,512]{0,1:T(8,128)S(1)}, u32[]{:S(2)}, u32[]{:S(2)}) collective-permute-start(f32[256,512]{0,1:T(8,128)S(1)} %convolution_bitcast_fusion.10), channel_id=1, source_target_pairs={{0,8},{8,0},{16,24},{24,16},{1,9},{9,1},{17,25},{25,17},{2,10},{10... | collective-permute-start | bytes 1572872 | tf_op jit(solution)/shard_map/ppermute | solution.py:11
  12.8 20.4 %collective-permute-start.5 = (f32[256,512]{0,1:T(8,128)}, f32[256,512]{0,1:T(8,128)}, u32[]{:S(2)}, u32[]{:S(2)}) collective-permute-start(f32[256,512]{0,1:T(8,128)} %convolution_bitcast_fusion.16), channel_id=1, source_target_pairs={{0,8},{8,0},{16,24},{24,16},{1,9},{9,1},{17,25},{25,17},{2,10},{10... | collective-permute-start | bytes 1572872 | tf_op jit(solution)/shard_map/ppermute | solution.py:11
  28.9 6.3 %collective-permute-start.17 = (f32[256,512]{0,1:T(8,128)}, f32[256,512]{0,1:T(8,128)S(1)}, u32[]{:S(2)}, u32[]{:S(2)}) collective-permute-start(f32[256,512]{0,1:T(8,128)} %convolution_bitcast_fusion.4), channel_id=1, source_target_pairs={{0,8},{8,0},{16,24},{24,16},{1,9},{9,1},{17,25},{25,17},{2,10},{10... | collective-permute-start | bytes 1572872 | tf_op jit(solution)/shard_map/ppermute | solution.py:11
  30.9 9.0 %collective-permute-start.21 = (f32[256,512]{0,1:T(8,128)}, f32[256,512]{0,1:T(8,128)S(1)}, u32[]{:S(2)}, u32[]{:S(2)}) collective-permute-start(f32[256,512]{0,1:T(8,128)} %convolution_bitcast_fusion), channel_id=1, source_target_pairs={{0,8},{8,0},{16,24},{24,16},{1,9},{9,1},{17,25},{25,17},{2,10},{10... | collective-permute-start | bytes 1572872 | tf_op jit(solution)/shard_map/ppermute | solution.py:11
  33.2 8.4 %collective-permute-start.1 = (f32[256,512]{0,1:T(8,128)}, f32[256,512]{0,1:T(8,128)S(1)}, u32[]{:S(2)}, u32[]{:S(2)}) collective-permute-start(f32[256,512]{0,1:T(8,128)} %convolution_bitcast_fusion.20), channel_id=1, source_target_pairs={{0,8},{8,0},{16,24},{24,16},{1,9},{9,1},{17,25},{25,17},{2,10},{10... | collective-permute-start | bytes 1572872 | tf_op jit(solution)/shard_map/ppermute | solution.py:11
  35.2 15.7 %collective-permute-start.10 = (f32[256,512]{0,1:T(8,128)S(1)}, f32[256,512]{0,1:T(8,128)S(1)}, u32[]{:S(2)}, u32[]{:S(2)}) collective-permute-start(f32[256,512]{0,1:T(8,128)S(1)} %fusion.8), channel_id=1, source_target_pairs={{0,16},{8,24},{16,0},{24,8},{1,17},{9,25},{17,1},{25,9},{2,18},{10... | collective-permute-start | bytes 1572872 | tf_op jit(solution)/shard_map/ppermute | solution.py:11
  39.9 26.0 %collective-permute-start.4 = (f32[256,512]{0,1:T(8,128)}, f32[256,512]{0,1:T(8,128)S(1)}, u32[]{:S(2)}, u32[]{:S(2)}) collective-permute-start(f32[256,512]{0,1:T(8,128)} %convolution_bitcast_fusion.18), channel_id=1, source_target_pairs={{0,8},{8,0},{16,24},{24,16},{1,9},{9,1},{17,25},{25,17},{2,10},{10... | collective-permute-start | bytes 1572872 | tf_op jit(solution)/shard_map/ppermute | solution.py:11
  41.6 20.5 %collective-permute-start.14 = (f32[256,512]{0,1:T(8,128)S(1)}, f32[256,512]{0,1:T(8,128)S(1)}, u32[]{:S(2)}, u32[]{:S(2)}) collective-permute-start(f32[256,512]{0,1:T(8,128)S(1)} %fusion.11), channel_id=1, source_target_pairs={{0,16},{8,24},{16,0},{24,8},{1,17},{9,25},{17,1},{25,9},{2,18},{10... | collective-permute-start | bytes 1572872 | tf_op jit(solution)/shard_map/ppermute | solution.py:11
  43.4 33.7 %collective-permute-start.16 = (f32[256,512]{0,1:T(8,128)}, f32[256,512]{0,1:T(8,128)S(1)}, u32[]{:S(2)}, u32[]{:S(2)}) collective-permute-start(f32[256,512]{0,1:T(8,128)} %convolution_bitcast_fusion.6), channel_id=1, source_target_pairs={{0,8},{8,0},{16,24},{24,16},{1,9},{9,1},{17,25},{25,17},{2,10},{10... | collective-permute-start | bytes 1572872 | tf_op jit(solution)/shard_map/ppermute | solution.py:11
  50.9 22.5 %collective-permute-start.6 = (f32[256,512]{0,1:T(8,128)S(1)}, f32[256,512]{0,1:T(8,128)S(1)}, u32[]{:S(2)}, u32[]{:S(2)}) collective-permute-start(f32[256,512]{0,1:T(8,128)S(1)} %fusion.5), channel_id=1, source_target_pairs={{0,16},{8,24},{16,0},{24,8},{1,17},{9,25},{17,1},{25,9},{2,18},{10... | collective-permute-start | bytes 1572872 | tf_op jit(solution)/shard_map/ppermute | solution.py:11
  54.7 33.7 %collective-permute-start.20 = (f32[256,512]{0,1:T(8,128)S(1)}, f32[256,512]{0,1:T(8,128)S(1)}, u32[]{:S(2)}, u32[]{:S(2)}) collective-permute-start(f32[256,512]{0,1:T(8,128)S(1)} %convolution_bitcast_fusion.2), channel_id=1, source_target_pairs={{0,8},{8,0},{16,24},{24,16},{1,9},{9,1},{17,25},{25,17},{2,10},{10... | collective-permute-start | bytes 1572872 | tf_op jit(solution)/shard_map/ppermute | solution.py:11
  62.2 22.5 %collective-permute-start.18 = (f32[256,512]{0,1:T(8,128)S(1)}, f32[256,512]{0,1:T(8,128)S(1)}, u32[]{:S(2)}, u32[]{:S(2)}) collective-permute-start(f32[256,512]{0,1:T(8,128)S(1)} %fusion.14), channel_id=1, source_target_pairs={{0,16},{8,24},{16,0},{24,8},{1,17},{9,25},{17,1},{25,9},{2,18},{10... | collective-permute-start | bytes 1572872 | tf_op jit(solution)/shard_map/ppermute | solution.py:11
  65.9 33.7 %collective-permute-start = (f32[256,512]{0,1:T(8,128)S(1)}, f32[256,512]{0,1:T(8,128)S(1)}, u32[]{:S(2)}, u32[]{:S(2)}) collective-permute-start(f32[256,512]{0,1:T(8,128)S(1)} %convolution_bitcast_fusion.22), channel_id=1, source_target_pairs={{0,8},{8,0},{16,24},{24,16},{1,9},{9,1},{17,25},{25,17},{2,10},{10... | collective-permute-start | bytes 1572872 | tf_op jit(solution)/shard_map/ppermute | solution.py:11
  73.4 22.5 %collective-permute-start.22 = (f32[256,512]{0,1:T(8,128)S(1)}, f32[256,512]{0,1:T(8,128)S(1)}, u32[]{:S(2)}, u32[]{:S(2)}) collective-permute-start(f32[256,512]{0,1:T(8,128)S(1)} %fusion.17), channel_id=1, source_target_pairs={{0,16},{8,24},{16,0},{24,8},{1,17},{9,25},{17,1},{25,9},{2,18},{10... | collective-permute-start | bytes 1572872 | tf_op jit(solution)/shard_map/ppermute | solution.py:11
  77.1 29.4 %collective-permute-start.2 = (f32[256,512]{0,1:T(8,128)S(1)}, f32[256,512]{0,1:T(8,128)S(1)}, u32[]{:S(2)}, u32[]{:S(2)}) collective-permute-start(f32[256,512]{0,1:T(8,128)S(1)} %fusion.2), channel_id=1, source_target_pairs={{0,16},{8,24},{16,0},{24,8},{1,17},{9,25},{17,1},{25,9},{2,18},{10... | collective-permute-start | bytes 1572872 | tf_op jit(solution)/shard_map/ppermute | solution.py:11
  84.6 25.3 %collective-permute-start.11 = (f32[256,512]{0,1:T(8,128)S(1)}, f32[256,512]{0,1:T(8,128)S(1)}, u32[]{:S(2)}, u32[]{:S(2)}) collective-permute-start(f32[256,512]{0,1:T(8,128)S(1)} %fusion.7), channel_id=1, source_target_pairs={{0,4},{4,0},{1,5},{5,1},{2,6},{6,2},{3,7},{7,3},{8,12},{12,8},{9,1... | collective-permute-start | bytes 1572872 | tf_op jit(solution)/shard_map/ppermute | solution.py:11
  88.4 22.4 %collective-permute-start.15 = (f32[256,512]{0,1:T(8,128)S(1)}, f32[256,512]{0,1:T(8,128)S(1)}, u32[]{:S(2)}, u32[]{:S(2)}) collective-permute-start(f32[256,512]{0,1:T(8,128)S(1)} %fusion.10), channel_id=1, source_target_pairs={{0,4},{4,0},{1,5},{5,1},{2,6},{6,2},{3,7},{7,3},{8,12},{12,8},{9,1... | collective-permute-start | bytes 1572872 | tf_op jit(solution)/shard_map/ppermute | solution.py:11
  95.9 26.2 %collective-permute-start.7 = (f32[256,512]{0,1:T(8,128)S(1)}, f32[256,512]{0,1:T(8,128)S(1)}, u32[]{:S(2)}, u32[]{:S(2)}) collective-permute-start(f32[256,512]{0,1:T(8,128)S(1)} %fusion.4), channel_id=1, source_target_pairs={{0,4},{4,0},{1,5},{5,1},{2,6},{6,2},{3,7},{7,3},{8,12},{12,8},{9,1... | collective-permute-start | bytes 1572872 | tf_op jit(solution)/shard_map/ppermute | solution.py:11
  99.6 33.6 %collective-permute-start.19 = (f32[256,512]{0,1:T(8,128)S(1)}, f32[256,512]{0,1:T(8,128)S(1)}, u32[]{:S(2)}, u32[]{:S(2)}) collective-permute-start(f32[256,512]{0,1:T(8,128)S(1)} %fusion.13), channel_id=1, source_target_pairs={{0,4},{4,0},{1,5},{5,1},{2,6},{6,2},{3,7},{7,3},{8,12},{12,8},{9,1... | collective-permute-start | bytes 1572872 | tf_op jit(solution)/shard_map/ppermute | solution.py:11
  106.5 38.0 %collective-permute-start.23 = (f32[256,512]{0,1:T(8,128)S(1)}, f32[256,512]{0,1:T(8,128)S(1)}, u32[]{:S(2)}, u32[]{:S(2)}) collective-permute-start(f32[256,512]{0,1:T(8,128)S(1)} %fusion.16), channel_id=1, source_target_pairs={{0,4},{4,0},{1,5},{5,1},{2,6},{6,2},{3,7},{7,3},{8,12},{12,8},{9,1... | collective-permute-start | bytes 1572872 | tf_op jit(solution)/shard_map/ppermute | solution.py:11
  110.0 43.6 %collective-permute-start.3 = (f32[256,512]{0,1:T(8,128)S(1)}, f32[256,512]{0,1:T(8,128)S(1)}, u32[]{:S(2)}, u32[]{:S(2)}) collective-permute-start(f32[256,512]{0,1:T(8,128)S(1)} %fusion.1), channel_id=1, source_target_pairs={{0,4},{4,0},{1,5},{5,1},{2,6},{6,2},{3,7},{7,3},{8,12},{12,8},{9,1... | collective-permute-start | bytes 1572872 | tf_op jit(solution)/shard_map/ppermute | solution.py:11
  156.1 2.8 %collective-permute-start.24 = (f32[4,64,512]{2,1,0:T(8,128)}, f32[4,64,512]{2,1,0:T(8,128)S(1)}, u32[]{:S(2)}, u32[]{:S(2)}) collective-permute-start(f32[4,64,512]{2,1,0:T(8,128)} %get-tuple-element.8), channel_id=1, source_target_pairs={{0,8},{8,0},{16,24},{24,16},{1,9},{9,1},{17,25},{25,17},{2,10},{10... | collective-permute-start | bytes 1572872 | tf_op jit(solution)/shard_map/ppermute | solution.py:11
  156.1 3.6 %collective-permute-start.25 = (f32[4,64,512]{2,1,0:T(8,128)S(1)}, f32[4,64,512]{2,1,0:T(8,128)}, u32[]{:S(2)}, u32[]{:S(2)}) collective-permute-start(f32[4,64,512]{2,1,0:T(8,128)S(1)} %get-tuple-element.7), channel_id=1, source_target_pairs={{0,8},{8,0},{16,24},{24,16},{1,9},{9,1},{17,25},{25,17},{2,10},{10... | collective-permute-start | bytes 1572872 | tf_op jit(solution)/shard_map/ppermute | solution.py:11
  158.9 0.8 copy-start.1
  161.2 13.4 %collective-permute-start.26 = (f32[2,64,512]{2,1,0:T(8,128)S(1)}, f32[2,64,512]{2,1,0:T(8,128)S(1)}, u32[]{:S(2)}, u32[]{:S(2)}) collective-permute-start(f32[2,64,512]{2,1,0:T(8,128)S(1)} %get-tuple-element.9), channel_id=1, source_target_pairs={{0,1},{1,0},{2,3},{3,2},{4,5},{5,4},{6,7},{7,6},{8,9},{9,8},{10,11... | collective-permute-start | bytes 786440 | tf_op jit(solution)/shard_map/ppermute | solution.py:11
  162.8 21.3 %collective-permute-start.27 = (f32[2,64,512]{2,1,0:T(8,128)S(1)}, f32[2,64,512]{2,1,0:T(8,128)S(1)}, u32[]{:S(2)}, u32[]{:S(2)}) collective-permute-start(f32[2,64,512]{2,1,0:T(8,128)S(1)} %get-tuple-element.10), channel_id=1, source_target_pairs={{0,2},{1,3},{2,0},{3,1},{4,6},{5,7},{6,4},{7,5},{8,10},{9,11},{10,... | collective-permute-start | bytes 786440 | tf_op jit(solution)/shard_map/ppermute | solution.py:11
  165.3 18.8 %collective-permute-start.28 = (f32[2,64,512]{2,1,0:T(8,128)S(1)}, f32[2,64,512]{2,1,0:T(8,128)S(1)}, u32[]{:S(2)}, u32[]{:S(2)}) collective-permute-start(f32[2,64,512]{2,1,0:T(8,128)S(1)} %get-tuple-element.11), channel_id=1, source_target_pairs={{0,3},{1,2},{2,1},{3,0},{4,7},{5,6},{6,5},{7,4},{8,11},{9,10},{10,... | collective-permute-start | bytes 786440 | tf_op jit(solution)/shard_map/ppermute | solution.py:11
  184.2 5.0 %collective-permute-start.29 = (f32[64,512]{1,0:T(8,128)S(1)}, f32[64,512]{1,0:T(8,128)S(1)}, u32[]{:S(2)}, u32[]{:S(2)}) collective-permute-start(f32[64,512]{1,0:T(8,128)S(1)} %slice_bitcast_fusion), channel_id=1, source_target_pairs={{0,16},{8,24},{16,0},{24,8},{1,17},{9,25},{17,1},{25,9},{2,18},{10... | collective-permute-start | bytes 393224 | tf_op jit(solution)/shard_map/ppermute | solution.py:11

commit v2 on v0

v2 whole, which is shorter than its diff:
```python
import functools

import jax
import jax.numpy as jnp
from jax import lax
from jax.experimental import pallas as pl
from jax.experimental.pallas import tpu as pltpu
from jax.sharding import PartitionSpec as P

VMEM_LIMIT = 48 << 20
LAG = 3


def swap(x, axis, bit):
    return lax.ppermute(x, axis, [(i, i ^ bit) for i in range(lax.axis_size(axis))])


def tie(x, *after):
    return lax.optimization_barrier((x, *after))[0]


def split(x):
    high = x.astype(jnp.bfloat16)
    return high, (x - high.astype(jnp.float32)).astype(jnp.bfloat16)


def product(a, b, dims):
    dot = functools.partial(lax.dot_general, dimension_numbers=(dims, ((), ())), preferred_element_type=jnp.float32)
    return dot(a[0], b[0]) + (dot(a[0], b[1]) + dot(a[1], b[0]))


def truncate_kernel(_, layer_ref, factor_ref, out_ref):
    out_ref[0] = product(split(layer_ref[0]), split(factor_ref[...]), ((0,), (0,)))


def truncated(layers, field, factor):
    count = layers.shape[0]
    _, rows, width = field.shape
    ranks = factor.shape[1]
    return pl.pallas_call(
        truncate_kernel,
        grid_spec=pltpu.PrefetchScalarGridSpec(
            num_scalar_prefetch=1,
            grid=(count,),
            in_specs=[
                pl.BlockSpec((1, rows, width), lambda i, n: (n[i], 0, 0)),
                pl.BlockSpec((rows, ranks), lambda i, n: (0, 0)),
            ],
            out_specs=pl.BlockSpec((1, width, ranks), lambda i, n: (i, 0, 0)),
        ),
        out_shape=jax.ShapeDtypeStruct((count, width, ranks), jnp.float32),
        compiler_params=pltpu.CompilerParams(vmem_limit_bytes=VMEM_LIMIT),
        cost_estimate=pl.CostEstimate(
            flops=6 * count * rows * width * ranks, bytes_accessed=4 * count * width * (rows + ranks), transcendentals=0
        ),
    )(layers, field, factor)


def gram_kernel(ba, widths, counts, unit, added, me_ref, *refs):
    strips, total = len(widths), ba * sum(counts)
    pieces, out_ref = refs[:total], refs[-1]
    old_ref = refs[total] if added else None
    owners, ranks = pieces[0].shape[1], pieces[0].shape[3]

    def pair(d, i):
        first = d * sum(counts) + sum(counts[:i])
        found = []
        for piece in pieces[first : first + counts[i]]:
            found += [split(piece[k].reshape(owners * widths[i], ranks)) for k in range(piece.shape[0])]
        return tuple(jnp.concatenate([x[n] for x in found], axis=1) for n in range(2))

    def put(block, row, size, value):
        value = value.reshape(owners, size, owners * unit)
        if added:
            value = value + old_ref[block, :, row : row + size, :]
        out_ref[block, :, row : row + size, :] = value

    pairs = {(d, i): pair(d, i) for d in range(ba) for i in range(strips)}
    lanes, wide = owners * unit, widths[-1]
    for d in range(ba):
        block = me_ref[0] ^ d
        row = 0
        for i, w in enumerate(widths):
            got = product(pairs[d, strips - 1], pairs[0, i], ((1,), (1,)))
            for n in range(w // unit):
                put(block, row, wide, got[:, n * lanes : (n + 1) * lanes])
                row += wide
        for n in range(wide // unit):
            mine = tuple(x[n * lanes : (n + 1) * lanes, :] for x in pairs[0, strips - 1])
            for i, w in enumerate(widths[:-1]):
                put(block, row, w, product(pairs[d, i], mine, ((1,), (1,))))
                row += w


def gram_strip(me, pieces, widths, unit, old):
    ba, counts = len(pieces), [len(x) for x in pieces[0]]
    owners, ranks = pieces[0][0][0].shape[1], pieces[0][0][0].shape[3]
    rows = (sum(widths) * widths[-1] + sum(widths[:-1]) * widths[-1]) // unit
    flat = [x for by_strip in pieces for by_chunk in by_strip for x in by_chunk]
    inner = ranks * sum(x.shape[0] for x in pieces[0][0])
    olds = [] if old is None else [old]
    full = pl.BlockSpec(memory_space=pltpu.VMEM)
    return pl.pallas_call(
        functools.partial(gram_kernel, ba, widths, counts, unit, len(olds)),
        in_specs=[pl.BlockSpec(memory_space=pltpu.SMEM)] + [full] * (len(flat) + len(olds)),
        out_specs=full,
        out_shape=jax.ShapeDtypeStruct((ba, owners, rows, owners * unit), jnp.float32),
        input_output_aliases={1 + len(flat): 0} if olds else {},
        compiler_params=pltpu.CompilerParams(vmem_limit_bytes=VMEM_LIMIT),
        cost_estimate=pl.CostEstimate(
            flops=6 * ba * owners * owners * rows * unit * inner, bytes_accessed=4 * sum(x.size for x in flat), transcendentals=0
        ),
    )(me.reshape(1).astype(jnp.int32), *flat, *olds)


def order_of(bits):
    if not bits:
        return [0]
    rest = order_of(bits[1:])
    return [d | bits[0] for d in rest] + rest


def strips_of(rest):
    widths = []
    while rest > 16 and rest % 2 == 0 and len(widths) < 2:
        rest //= 2
        widths.append(rest)
    return widths + [rest]


def summed_over_core(region):
    aa = region.shape[0]
    core = lax.axis_index("aa") & 1
    pairs = region.reshape(aa // 2, 2, *region.shape[1:])
    send = lax.dynamic_index_in_dim(pairs, core ^ 1, 1, keepdims=False)
    return lax.dynamic_index_in_dim(pairs, core, 1, keepdims=False) + swap(send, "aa", 1)


def block_by_permutes(region):
    t = summed_over_core(region)
    me_x, me_c = lax.axis_index("aa") >> 1, lax.axis_index("col")
    total = lax.dynamic_index_in_dim(t, me_c, 1, keepdims=False)
    for d in range(1, region.shape[1]):
        total = total + swap(lax.dynamic_index_in_dim(t, me_c ^ d, 1, keepdims=False), "col", d)
    places = total.shape[0]
    mine = lax.dynamic_index_in_dim(total, me_x, 0, keepdims=False)
    for d in range(1, places):
        mine = mine + swap(lax.dynamic_index_in_dim(total, me_x ^ d, 0, keepdims=False), "aa", 2 * d)
    return mine


def block_by_all_to_all(region):
    aa, col = region.shape[:2]
    t = summed_over_core(region)
    groups = [[(x * 2 + c) * col + z for x in range(aa // 2) for z in range(col)] for c in range(2)]
    t = t.reshape(aa // 2 * col, *t.shape[2:])
    return jnp.sum(lax.all_to_all(t, ("aa", "col"), 0, 0, tiled=True, axis_index_groups=groups), axis=0)


def shards(field, factor):
    aa, ba, col = (lax.axis_size(n) for n in ("aa", "ba", "col"))
    me_a, me_b = lax.axis_index("aa"), lax.axis_index("ba")
    ranks, width = factor.shape[1], field.shape[2]
    depth = field.shape[0] * col
    each = field.shape[0] // aa
    rest = ba * width // (aa * col)
    owners = width // rest
    widths = strips_of(rest)
    unit = widths[-1]
    bits = [1 << n for n in range(aa.bit_length() - 1)]
    keep = order_of(bits[1:])
    send = [d | 1 for d in keep]

    def layers(places, c):
        return jnp.concatenate([((me_a ^ d) * each + c).reshape(1) for d in places])

    def groups_of(i):
        size = 1 if i == 0 else 2 if each % 2 == 0 else 1
        return [range(c, c + size) for c in range(0, each, size)]

    def parts_of(c, i):
        first = sum(widths[:i])
        kept, came = kept_of[c], came_of[c]
        kept, came = (x.reshape(len(keep), 1, owners, rest, ranks)[:, :, :, first : first + widths[i]] for x in (kept, came))
        return kept + came

    kept_of, came_of = {}, {}

    def send_core(c, *after):
        out = truncated(tie(layers(send, c), *after), field, factor)
        came_of[c] = swap(out, "aa", 1)
        return out

    def keep_core(c, *after):
        kept_of[c] = truncated(tie(layers(keep, c), *after), field, factor)

    steps = [(i, group) for i in range(len(widths)) for group in groups_of(i)]
    pieces = {}
    regions, blocks = [None] * len(widths), []
    arrived, passed, waiting, leaving_of = [], [], [], {}

    def add_gram(i, group, *after):
        used = [
            [[pieces[d, s, g] for g in groups_of(s) if g[0] in group] for s in range(i + 1)] for d in range(ba)
        ]
        regions[i] = gram_strip(tie(me_b, *after), used, widths[: i + 1], unit, regions[i])
        if group[-1] == each - 1:
            region = regions[i].reshape(aa, col, *regions[i].shape[2:])
            blocks.append(block_by_permutes(region) if i < len(widths) - 1 else block_by_all_to_all(region))

    keep_core(0, send_core(0))
    out = send_core(1, kept_of[0]) if each > 1 else None
    for n, (i, group) in enumerate(steps):
        t = jnp.concatenate([parts_of(c, i) for c in group], axis=1)
        half = t.shape[0] // 2
        leaving, t = (t[:half], t[half:]) if bits[1:] else (t, t)
        if i == 0 and n + 1 < each:
            keep_core(n + 1, leaving, out)
            if n + 2 < each:
                out = send_core(n + 2, kept_of[n + 1])
        after = ([arrived[n - 2]] if n >= 2 else []) + (passed[n - 4] if n >= 4 else [])
        if after:
            leaving = tie(leaving, *after)
        leaving_of[n] = leaving
        for bit in bits[1:]:
            t = t + swap(leaving, "aa", bit)
            half = t.shape[0] // 2
            leaving, t = (t[:half], t[half:]) if half else (t, t)
        t = t[0]
        arrived.append(t)
        passed.append([swap(t, "ba", d) for d in range(1, ba)])
        for d, x in enumerate([t] + passed[-1]):
            pieces[d, i, group] = x
        waiting.append((i, group))
        if len(waiting) > LAG:
            add_gram(*waiting.pop(0), leaving_of[n])
    while waiting:
        add_gram(*waiting.pop(0))

    lanes = owners * unit
    columns = [[None] * len(widths) for _ in widths]
    for j, wide in enumerate(widths):
        row = 0
        for i in range(j + 1):
            n = widths[i] // unit
            columns[i][j] = blocks[j][row : row + n * wide].reshape(n, wide, lanes).swapaxes(1, 2).reshape(n * lanes, wide)
            row += n * wide
        n, before = wide // unit, sum(widths[:j])
        if j:
            earlier = blocks[j][row:].reshape(n, before, lanes).swapaxes(1, 2).reshape(n * lanes, before)
            for i in range(j):
                at = sum(widths[:i])
                columns[j][i] = earlier[:, at : at + widths[i]]
    parts = [jnp.concatenate(columns[i], axis=1).reshape(owners, widths[i], rest) for i in range(len(widths))]
    return jnp.concatenate(parts, axis=1).reshape(width, rest) / jnp.sqrt(jnp.float32(ranks * depth))


def solution(mesh):
    placed = (P("col", "aa", "ba"), P("aa", None))
    return jax.shard_map(
        shards, mesh=mesh, in_specs=placed, out_specs=P("ba", ("aa", "col")), check_vma=False
    )
```

time: 286 us -> 152 us (0.53)
  waiting for transfers between devices: 237 us -> 51.1 us
  starting transfers between devices: 0.12 us -> 48.3 us
  Pallas kernels: 0 us -> 41.1 us
  matrix products: 31.2 us -> 0 us
  between operations: 13.1 us -> 0.84 us
  other arithmetic: 1.57 us -> 7.32 us
    reduce_scatter x2 -> x0, waiting for transfers between devices: 133 us -> none  [the longest x1 102 us: shards(): core = lax.psum_scatter(partial_core, 'aa', scatter_dimension=1, tiled=True)]
    all_gather x1 -> x0, waiting for transfers between devices: 81.9 us -> none  [shards(): lax.all_gather(core, 'ba', axis=2, tiled=True)]
    ppermute x0 -> x41, starting transfers between devices: none -> 44.8 us  [swap(): lax.ppermute(x, axis, [(i, i ^ bit) for i in range(lax.axis_size(axis))])]
    pallas_call x0 -> x24, Pallas kernels: none -> 41.1 us  [the longest x12 29.8 us: truncated(): pl.pallas_call(truncate_kernel, grid_spec=pltpu.PrefetchScalarGridSpec(nu...]
    ppermute x0 -> x41, waiting for transfers between devices: none -> 37.9 us  [swap(): lax.ppermute(x, axis, [(i, i ^ bit) for i in range(lax.axis_size(axis))])]
    dot_general x2 -> x0, matrix products: 31.2 us -> none  [the longest x1 17.1 us: shards(): jnp.einsum('kab,ar->krb', field, factor, precision=lax.Precision.HIGHEST)]
    unnamed x5 -> x0, waiting for transfers between devices: 21.9 us -> none
    all_to_all x0 -> x1, waiting for transfers between devices: none -> 13.2 us  [block_by_all_to_all(): lax.all_to_all(t, ('aa', 'col'), 0, 0, tiled=True, axis_index_groups=groups)]
  transfers between devices with their start and end apart: 4 -> 42, of which waited for: 4 -> 11; matrix products, arithmetic and copies ran while one was open for 0% -> 5% of each run, Pallas kernels for 0% -> 25%
where the time goes in v2:
time: 152 us
  waiting for transfers between devices  51.1 us (34%)
  starting transfers between devices  48.3 us (32%)
  Pallas kernels  41.1 us (27%)
  other arithmetic  7.32 us (5%)
  local copies, waits for them, and re-layouts  3.02 us (2%)
    ppermute x41, starting transfers between devices, swap(): lax.ppermute(x, axis, [(i, i ^ bit) for i in range(lax.axis_size(axis))])  44.8 us
    ppermute x41, waiting for transfers between devices, swap(): lax.ppermute(x, axis, [(i, i ^ bit) for i in range(lax.axis_size(axis))])  37.9 us
    pallas_call x12, Pallas kernels, truncated(): pl.pallas_call(truncate_kernel, grid_spec=pltpu.PrefetchScalarGridSpec(nu...  29.8 us
    all_to_all x1, waiting for transfers between devices, block_by_all_to_all(): lax.all_to_all(t, ('aa', 'col'), 0, 0, tiled=True, axis_index_groups=groups)  13.2 us
    pallas_call x12, Pallas kernels, gram_strip(): pl.pallas_call(functools.partial(gram_kernel, ba, widths, counts, unit, l...  11.3 us
    add x12, other arithmetic, parts_of(): return kept + came  5.1 us
    all_to_all x1, starting transfers between devices, block_by_all_to_all(): lax.all_to_all(t, ('aa', 'col'), 0, 0, tiled=True, axis_index_groups=groups)  3.47 us
  transfers between devices with their start and end apart: 42, of which 11 were waited for; matrix products, arithmetic and copies ran while one was open for 5% of the time, Pallas kernels for 25%

profile of v2, /device:TPU:0, one launch (start us, length us, event | category | flops | bytes accessed | tf_op | source)
XLA Modules:
  0.0 151.7 jit_solution(15575623077618906898)
XLA Ops:
  1.0 2.5 %shard_map.28 = f32[2,512,256]{2,1,0:T(8,128)S(1)} custom-call(s32[2]{0:T(128)S(1)} %get-tuple-element.92._, f32[24,256,512]{2,1,0:T(8,128)} %layer_ref.23, f32[256,256]{1,0:T(8,128)S(1)} %copy-done), custom_call_target="tpu_custom_call" | custom-call | flops 402653184 | bytes 2097152 | tf_op jit(solution)/shard_map/pallas_call | solution.py:40
  4.0 2.5 %shard_map.29 = f32[2,512,256]{2,1,0:T(8,128)S(1)} custom-call(s32[2]{0:T(128)S(1)} %get-tuple-element.35._, f32[24,256,512]{2,1,0:T(8,128)} %layer_ref.23, f32[256,256]{1,0:T(8,128)S(1)} %copy-done.1), custom_call_target="tpu_custom_call" | custom-call | flops 402653184 | bytes 2097152 | tf_op jit(solution)/shard_map/pallas_call | solution.py:40
  6.6 2.5 %shard_map.30 = f32[2,512,256]{2,1,0:T(8,128)S(1)} custom-call(s32[2]{0:T(128)S(1)} %get-tuple-element.36._, f32[24,256,512]{2,1,0:T(8,128)} %layer_ref.23, f32[256,256]{1,0:T(8,128)S(1)} %copy-done.1), custom_call_target="tpu_custom_call" | custom-call | flops 402653184 | bytes 2097152 | tf_op jit(solution)/shard_map/pallas_call | solution.py:40
  10.6 3.0 %collective-permute-start.6 = (f32[1,1,8,32,256]{4,3,2,1,0:T(8,128)S(1)}, f32[1,1,8,32,256]{4,3,2,1,0:T(8,128)S(1)}, u32[]{:S(2)}, u32[]{:S(2)}) collective-permute-start(f32[1,1,8,32,256]{4,3,2,1,0:T(8,128)S(1)} %slice.273), channel_id=1, source_target_pairs={{0,16},{8,24},{16,0},{24,8},{1,17},{9,25},{17,1},{25,9},{2,18},{10... | collective-permute-start | bytes 786440 | tf_op jit(solution)/shard_map/ppermute | solution.py:15
  13.6 2.5 %shard_map.31 = f32[2,512,256]{2,1,0:T(8,128)S(1)} custom-call(s32[2]{0:T(128)S(1)} %get-tuple-element.37._, f32[24,256,512]{2,1,0:T(8,128)} %layer_ref.23, f32[256,256]{1,0:T(8,128)S(1)} %copy-done.1), custom_call_target="tpu_custom_call" | custom-call | flops 402653184 | bytes 2097152 | tf_op jit(solution)/shard_map/pallas_call | solution.py:40
  18.5 2.5 %shard_map.32 = f32[2,512,256]{2,1,0:T(8,128)S(1)} custom-call(s32[2]{0:T(128)S(1)} %get-tuple-element.38._, f32[24,256,512]{2,1,0:T(8,128)} %layer_ref.23, f32[256,256]{1,0:T(8,128)S(1)} %copy-done.1), custom_call_target="tpu_custom_call" | custom-call | flops 402653184 | bytes 2097152 | tf_op jit(solution)/shard_map/pallas_call | solution.py:40
  21.0 2.5 %shard_map.33 = f32[2,512,256]{2,1,0:T(8,128)S(1)} custom-call(s32[2]{0:T(128)S(1)} %get-tuple-element.39._, f32[24,256,512]{2,1,0:T(8,128)} %layer_ref.23, f32[256,256]{1,0:T(8,128)S(1)} %copy-done.1), custom_call_target="tpu_custom_call" | custom-call | flops 402653184 | bytes 2097152 | tf_op jit(solution)/shard_map/pallas_call | solution.py:40
  24.6 2.5 %shard_map.34 = f32[2,512,256]{2,1,0:T(8,128)S(1)} custom-call(s32[2]{0:T(128)S(1)} %get-tuple-element.40._, f32[24,256,512]{2,1,0:T(8,128)} %layer_ref.23, f32[256,256]{1,0:T(8,128)S(1)} %copy-done.1), custom_call_target="tpu_custom_call" | custom-call | flops 402653184 | bytes 2097152 | tf_op jit(solution)/shard_map/pallas_call | solution.py:40
  27.8 2.1 %collective-permute-start.8 = (f32[1,8,32,256]{3,2,1,0:T(8,128)S(1)}, f32[1,8,32,256]{3,2,1,0:T(8,128)S(1)}, u32[]{:S(2)}, u32[]{:S(2)}) collective-permute-start(f32[1,8,32,256]{3,2,1,0:T(8,128)S(1)} %fusion.21.refs_0_), channel_id=1, source_target_pairs={{0,4},{4,0},{1,5},{5,1},{2,6},{6,2},{3,7},{7,3},{8,12},{12,8},{9,1... | collective-permute-start | bytes 786440 | tf_op jit(solution)/shard_map/ppermute | solution.py:15
  30.1 2.0 %collective-permute-start.7 = (f32[1,1,8,32,256]{4,3,2,1,0:T(8,128)S(1)}, f32[1,1,8,32,256]{4,3,2,1,0:T(8,128)S(1)}, u32[]{:S(2)}, u32[]{:S(2)}) collective-permute-start(f32[1,1,8,32,256]{4,3,2,1,0:T(8,128)S(1)} %slice.279), channel_id=1, source_target_pairs={{0,16},{8,24},{16,0},{24,8},{1,17},{9,25},{17,1},{25,9},{2,18},{10... | collective-permute-start | bytes 786440 | tf_op jit(solution)/shard_map/ppermute | solution.py:15
  32.1 2.5 %shard_map.35 = f32[2,512,256]{2,1,0:T(8,128)S(1)} custom-call(s32[2]{0:T(128)S(1)} %get-tuple-element.41._, f32[24,256,512]{2,1,0:T(8,128)} %layer_ref.23, f32[256,256]{1,0:T(8,128)S(1)} %copy-done.1), custom_call_target="tpu_custom_call" | custom-call | flops 402653184 | bytes 2097152 | tf_op jit(solution)/shard_map/pallas_call | solution.py:40
  34.8 2.5 %shard_map.36 = f32[2,512,256]{2,1,0:T(8,128)S(1)} custom-call(s32[2]{0:T(128)S(1)} %get-tuple-element.42._, f32[24,256,512]{2,1,0:T(8,128)} %layer_ref.23, f32[256,256]{1,0:T(8,128)S(1)} %copy-done.1), custom_call_target="tpu_custom_call" | custom-call | flops 402653184 | bytes 2097152 | tf_op jit(solution)/shard_map/pallas_call | solution.py:40
  37.4 2.5 %shard_map.37 = f32[2,512,256]{2,1,0:T(8,128)S(1)} custom-call(s32[2]{0:T(128)S(1)} %get-tuple-element.43._, f32[24,256,512]{2,1,0:T(8,128)} %layer_ref.23, f32[256,256]{1,0:T(8,128)S(1)} %copy-done.1), custom_call_target="tpu_custom_call" | custom-call | flops 402653184 | bytes 2097152 | tf_op jit(solution)/shard_map/pallas_call | solution.py:40
  39.9 2.5 %shard_map.38 = f32[2,512,256]{2,1,0:T(8,128)S(1)} custom-call(s32[2]{0:T(128)S(1)} %get-tuple-element.44._, f32[24,256,512]{2,1,0:T(8,128)} %layer_ref.23, f32[256,256]{1,0:T(8,128)S(1)} %copy-done.1), custom_call_target="tpu_custom_call" | custom-call | flops 402653184 | bytes 2097152 | tf_op jit(solution)/shard_map/pallas_call | solution.py:40
  43.6 2.1 %collective-permute-start.10 = (f32[1,8,32,256]{3,2,1,0:T(8,128)S(1)}, f32[1,8,32,256]{3,2,1,0:T(8,128)S(1)}, u32[]{:S(2)}, u32[]{:S(2)}) collective-permute-start(f32[1,8,32,256]{3,2,1,0:T(8,128)S(1)} %fusion.22.refs_0_), channel_id=1, source_target_pairs={{0,4},{4,0},{1,5},{5,1},{2,6},{6,2},{3,7},{7,3},{8,12},{12,8},{9,1... | collective-permute-start | bytes 786440 | tf_op jit(solution)/shard_map/ppermute | solution.py:15
  45.7 5.6 %collective-permute-done.14 = f32[1,1,8,32,256]{4,3,2,1,0:T(8,128)S(1)} collective-permute-done((f32[1,1,8,32,256]{4,3,2,1,0:T(8,128)S(1)}, f32[1,1,8,32,256]{4,3,2,1,0:T(8,128)S(1)}, u32[]{:S(2)}, u32[]{:S(2)}) %collective-permute-start.14) | collective-permute-done | bytes 262176 | tf_op jit(solution)/shard_map/ppermute | solution.py:15
  53.7 2.6 %shard_map.39 = f32[2,512,256]{2,1,0:T(8,128)S(1)} custom-call(s32[2]{0:T(128)S(1)} %get-tuple-element.45._, f32[24,256,512]{2,1,0:T(8,128)} %layer_ref.23, f32[256,256]{1,0:T(8,128)S(1)} %copy-done.1), custom_call_target="tpu_custom_call" | custom-call | flops 402653184 | bytes 2097152 | tf_op jit(solution)/shard_map/pallas_call | solution.py:40
  58.7 7.2 %collective-permute-done.16 = f32[1,1,8,32,256]{4,3,2,1,0:T(8,128)S(1)} collective-permute-done((f32[1,1,8,32,256]{4,3,2,1,0:T(8,128)S(1)}, f32[1,1,8,32,256]{4,3,2,1,0:T(8,128)S(1)}, u32[]{:S(2)}, u32[]{:S(2)}) %collective-permute-start.16) | collective-permute-done | bytes 262176 | tf_op jit(solution)/shard_map/ppermute | solution.py:15
  71.1 4.6 %collective-permute-done.24 = f32[1,2,8,16,256]{4,3,2,1,0:T(8,128)S(1)} collective-permute-done((f32[1,2,8,16,256]{4,3,2,1,0:T(8,128)S(1)}, f32[1,2,8,16,256]{4,3,2,1,0:T(8,128)S(1)}, u32[]{:S(2)}, u32[]{:S(2)}) %collective-permute-start.24) | collective-permute-done | bytes 262176 | tf_op jit(solution)/shard_map/ppermute | solution.py:15
  77.9 3.5 %collective-permute-done.11 = f32[1,2,8,16,256]{4,3,2,1,0:T(8,128)S(1)} collective-permute-done((f32[1,2,8,16,256]{4,3,2,1,0:T(8,128)S(1)}, f32[1,2,8,16,256]{4,3,2,1,0:T(8,128)S(1)}, u32[]{:S(2)}, u32[]{:S(2)}) %collective-permute-start.11) | collective-permute-done | bytes 262176 | tf_op jit(solution)/shard_map/ppermute | solution.py:15
  84.5 1.9 %collective-permute-done.25 = f32[1,2,8,16,256]{4,3,2,1,0:T(8,128)S(1)} collective-permute-done((f32[1,2,8,16,256]{4,3,2,1,0:T(8,128)S(1)}, f32[1,2,8,16,256]{4,3,2,1,0:T(8,128)S(1)}, u32[]{:S(2)}, u32[]{:S(2)}) %collective-permute-start.25) | collective-permute-done | bytes 262176 | tf_op jit(solution)/shard_map/ppermute | solution.py:15
  89.1 1.8 %collective-permute-done.27 = f32[1,2,8,16,256]{4,3,2,1,0:T(8,128)S(1)} collective-permute-done((f32[1,2,8,16,256]{4,3,2,1,0:T(8,128)S(1)}, f32[1,2,8,16,256]{4,3,2,1,0:T(8,128)S(1)}, u32[]{:S(2)}, u32[]{:S(2)}) %collective-permute-start.27) | collective-permute-done | bytes 262176 | tf_op jit(solution)/shard_map/ppermute | solution.py:15
  91.8 2.5 %collective-permute-start.28 = (f32[2,8,16,256]{3,2,1,0:T(8,128)S(1)}, f32[2,8,16,256]{3,2,1,0:T(8,128)S(1)}, u32[]{:S(2)}, u32[]{:S(2)}) collective-permute-start(f32[2,8,16,256]{3,2,1,0:T(8,128)S(1)} %fusion.15.refs_2_), channel_id=1, source_target_pairs={{0,4},{4,0},{1,5},{5,1},{2,6},{6,2},{3,7},{7,3},{8,12},{12,8},{9,1... | collective-permute-start | bytes 786440 | tf_op jit(solution)/shard_map/ppermute | solution.py:15
  98.6 2.5 %collective-permute-start.22 = (f32[2,64,128]{2,1,0:T(8,128)S(1)}, f32[2,64,128]{2,1,0:T(8,128)S(1)}, u32[]{:S(2)}, u32[]{:S(2)}) collective-permute-start(f32[2,64,128]{2,1,0:T(8,128)S(1)} %get-tuple-element.81), channel_id=1, source_target_pairs={{0,3},{1,2},{2,1},{3,0},{4,7},{5,6},{6,5},{7,4},{8,11},{9,10},{10,... | collective-permute-start | bytes 196616 | tf_op jit(solution)/shard_map/ppermute | solution.py:15
  101.2 2.0 %collective-permute-start.21 = (f32[2,64,128]{2,1,0:T(8,128)S(1)}, f32[2,64,128]{2,1,0:T(8,128)S(1)}, u32[]{:S(2)}, u32[]{:S(2)}) collective-permute-start(f32[2,64,128]{2,1,0:T(8,128)S(1)} %get-tuple-element.82), channel_id=1, source_target_pairs={{0,2},{1,3},{2,0},{3,1},{4,6},{5,7},{6,4},{7,5},{8,10},{9,11},{10,... | collective-permute-start | bytes 196616 | tf_op jit(solution)/shard_map/ppermute | solution.py:15
  108.8 6.6 %collective-permute-done.38.refs_7_ = f32[2,8,16,256]{3,2,1,0:T(8,128)S(1)} collective-permute-done((f32[2,8,16,256]{3,2,1,0:T(8,128)S(1)}, f32[2,8,16,256]{3,2,1,0:T(8,128)S(1)}, u32[]{:S(2)}, u32[]{:S(2)}) %collective-permute-start.38) | collective-permute-done | bytes 262176 | tf_op jit(solution)/shard_map/ppermute | solution.py:15
  117.1 1.7 %shard_map.51 = f32[2,8,112,128]{3,2,1,0:T(8,128)S(1)} custom-call(s32[1]{0:T(128)} %bitcast.77.me_ref, f32[1,8,32,256]{3,2,1,0:T(8,128)S(1)} %fusion.23.refs_0_, f32[1,8,32,256]{3,2,1,0:T(8,128)S(1)} %fusion.20.refs_0_.refs_1_, f32[2,8,16,256]{3,2,1,0:T(8,128)S(1)} %fusion.15.refs_2_, ...), custom_call_target="tpu_custom_call", output_to_operand_aliasing={{}: (9, {})} | custom-call | flops 704643072 | bytes 2097152 | tf_op jit(solution)/shard_map/pallas_call | solution.py:103
  120.8 1.7 %collective-permute-start.32 = (f32[2,80,128]{2,1,0:T(8,128)S(1)}, f32[2,80,128]{2,1,0:T(8,128)S(1)}, u32[]{:S(2)}, u32[]{:S(2)}) collective-permute-start(f32[2,80,128]{2,1,0:T(8,128)S(1)} %get-tuple-element.79), channel_id=1, source_target_pairs={{0,2},{1,3},{2,0},{3,1},{4,6},{5,7},{6,4},{7,5},{8,10},{9,11},{10,... | collective-permute-start | bytes 245768 | tf_op jit(solution)/shard_map/ppermute | solution.py:15
  124.0 3.7 %collective-permute-done.33 = f32[2,80,128]{2,1,0:T(8,128)S(1)} collective-permute-done((f32[2,80,128]{2,1,0:T(8,128)S(1)}, f32[2,80,128]{2,1,0:T(8,128)S(1)}, u32[]{:S(2)}, u32[]{:S(2)}) %collective-permute-start.33) | collective-permute-done | bytes 81952 | tf_op jit(solution)/shard_map/ppermute | solution.py:15
  127.8 2.5 %collective-permute-done.32 = f32[2,80,128]{2,1,0:T(8,128)S(1)} collective-permute-done((f32[2,80,128]{2,1,0:T(8,128)S(1)}, f32[2,80,128]{2,1,0:T(8,128)S(1)}, u32[]{:S(2)}, u32[]{:S(2)}) %collective-permute-start.32) | collective-permute-done | bytes 81952 | tf_op jit(solution)/shard_map/ppermute | solution.py:15
  132.8 3.5 %all-to-all-start = ((f32[8,112,128]{2,1,0:T(8,128)}), f32[8,112,128]{2,1,0:T(8,128)S(1)}, u32[]{:S(2)}, u32[]{:S(2)}) async-start(f32[8,112,128]{2,1,0:T(8,128)} %bitcast.83), calls=%async_computation | async-start | bytes 917504 | tf_op jit(solution)/shard_map/all_to_all | solution.py:157
  136.9 13.2 %all-to-all-done = f32[8,112,128]{2,1,0:T(8,128)S(1)} async-done(((f32[8,112,128]{2,1,0:T(8,128)}), f32[8,112,128]{2,1,0:T(8,128)S(1)}, u32[]{:S(2)}, u32[]{:S(2)}) %all-to-all-start) | async-done | bytes 458784 | tf_op jit(solution)/shard_map/all_to_all | solution.py:157
  (157 shorter events, 47.3 us)
Async XLA Ops:
  10.6 17.1 %collective-permute-start.6 = (f32[1,1,8,32,256]{4,3,2,1,0:T(8,128)S(1)}, f32[1,1,8,32,256]{4,3,2,1,0:T(8,128)S(1)}, u32[]{:S(2)}, u32[]{:S(2)}) collective-permute-start(f32[1,1,8,32,256]{4,3,2,1,0:T(8,128)S(1)} %slice.273), channel_id=1, source_target_pairs={{0,16},{8,24},{16,0},{24,8},{1,17},{9,25},{17,1},{25,9},{2,18},{10... | collective-permute-start | bytes 786440 | tf_op jit(solution)/shard_map/ppermute | solution.py:15
  18.4 11.5 %collective-permute-start.13 = (f32[1,1,8,32,256]{4,3,2,1,0:T(8,128)S(1)}, f32[1,1,8,32,256]{4,3,2,1,0:T(8,128)S(1)}, u32[]{:S(2)}, u32[]{:S(2)}) collective-permute-start(f32[1,1,8,32,256]{4,3,2,1,0:T(8,128)S(1)} %slice.276), channel_id=1, source_target_pairs={{0,16},{8,24},{16,0},{24,8},{1,17},{9,25},{17,1},{25,9},{2,18},{10... | collective-permute-start | bytes 786440 | tf_op jit(solution)/shard_map/ppermute | solution.py:15
  20.9 9.1 %collective-permute-start.2 = (f32[2,512,256]{2,1,0:T(8,128)S(1)}, f32[2,512,256]{2,1,0:T(8,128)S(1)}, u32[]{:S(2)}, u32[]{:S(2)}) collective-permute-start(f32[2,512,256]{2,1,0:T(8,128)S(1)} %shard_map.32), channel_id=1, source_target_pairs={{0,8},{8,0},{16,24},{24,16},{1,9},{9,1},{17,25},{25,17},{2,10},{10... | collective-permute-start | bytes 3145736 | tf_op jit(solution)/shard_map/ppermute | solution.py:15
  27.8 15.3 %collective-permute-start.8 = (f32[1,8,32,256]{3,2,1,0:T(8,128)S(1)}, f32[1,8,32,256]{3,2,1,0:T(8,128)S(1)}, u32[]{:S(2)}, u32[]{:S(2)}) collective-permute-start(f32[1,8,32,256]{3,2,1,0:T(8,128)S(1)} %fusion.21.refs_0_), channel_id=1, source_target_pairs={{0,4},{4,0},{1,5},{5,1},{2,6},{6,2},{3,7},{7,3},{8,12},{12,8},{9,1... | collective-permute-start | bytes 786440 | tf_op jit(solution)/shard_map/ppermute | solution.py:15
  29.9 26.6 %collective-permute-start.15 = (f32[1,8,32,256]{3,2,1,0:T(8,128)S(1)}, f32[1,8,32,256]{3,2,1,0:T(8,128)S(1)}, u32[]{:S(2)}, u32[]{:S(2)}) collective-permute-start(f32[1,8,32,256]{3,2,1,0:T(8,128)S(1)} %fusion.18.refs_0_.refs_1_), channel_id=1, source_target_pairs={{0,4},{4,0},{1,5},{5,1},{2,6},{6,2},{3,7},{7,3},{8,12},{12,8},{9,1... | collective-permute-start | bytes 786440 | tf_op jit(solution)/shard_map/ppermute | solution.py:15
  30.1 13.5 %collective-permute-start.7 = (f32[1,1,8,32,256]{4,3,2,1,0:T(8,128)S(1)}, f32[1,1,8,32,256]{4,3,2,1,0:T(8,128)S(1)}, u32[]{:S(2)}, u32[]{:S(2)}) collective-permute-start(f32[1,1,8,32,256]{4,3,2,1,0:T(8,128)S(1)} %slice.279), channel_id=1, source_target_pairs={{0,16},{8,24},{16,0},{24,8},{1,17},{9,25},{17,1},{25,9},{2,18},{10... | collective-permute-start | bytes 786440 | tf_op jit(solution)/shard_map/ppermute | solution.py:15
  37.3 15.7 %collective-permute-start.4 = (f32[2,512,256]{2,1,0:T(8,128)S(1)}, f32[2,512,256]{2,1,0:T(8,128)S(1)}, u32[]{:S(2)}, u32[]{:S(2)}) collective-permute-start(f32[2,512,256]{2,1,0:T(8,128)S(1)} %shard_map.36), channel_id=1, source_target_pairs={{0,8},{8,0},{16,24},{24,16},{1,9},{9,1},{17,25},{25,17},{2,10},{10... | collective-permute-start | bytes 3145736 | tf_op jit(solution)/shard_map/ppermute | solution.py:15
  42.3 14.0 %collective-permute-start.5 = (f32[2,512,256]{2,1,0:T(8,128)S(1)}, f32[2,512,256]{2,1,0:T(8,128)S(1)}, u32[]{:S(2)}, u32[]{:S(2)}) collective-permute-start(f32[2,512,256]{2,1,0:T(8,128)S(1)} %shard_map.38), channel_id=1, source_target_pairs={{0,8},{8,0},{16,24},{24,16},{1,9},{9,1},{17,25},{25,17},{2,10},{10... | collective-permute-start | bytes 3145736 | tf_op jit(solution)/shard_map/ppermute | solution.py:15
  43.6 23.4 %collective-permute-start.10 = (f32[1,8,32,256]{3,2,1,0:T(8,128)S(1)}, f32[1,8,32,256]{3,2,1,0:T(8,128)S(1)}, u32[]{:S(2)}, u32[]{:S(2)}) collective-permute-start(f32[1,8,32,256]{3,2,1,0:T(8,128)S(1)} %fusion.22.refs_0_), channel_id=1, source_target_pairs={{0,4},{4,0},{1,5},{5,1},{2,6},{6,2},{3,7},{7,3},{8,12},{12,8},{9,1... | collective-permute-start | bytes 786440 | tf_op jit(solution)/shard_map/ppermute | solution.py:15
  51.4 15.1 %collective-permute-start.18 = (f32[1,8,32,256]{3,2,1,0:T(8,128)S(1)}, f32[1,8,32,256]{3,2,1,0:T(8,128)S(1)}, u32[]{:S(2)}, u32[]{:S(2)}) collective-permute-start(f32[1,8,32,256]{3,2,1,0:T(8,128)S(1)} %fusion.19.refs_0_.refs_1_), channel_id=1, source_target_pairs={{0,4},{4,0},{1,5},{5,1},{2,6},{6,2},{3,7},{7,3},{8,12},{12,8},{9,1... | collective-permute-start | bytes 786440 | tf_op jit(solution)/shard_map/ppermute | solution.py:15
  53.1 14.0 %collective-permute-start.9 = (f32[1,1,8,32,256]{4,3,2,1,0:T(8,128)S(1)}, f32[1,1,8,32,256]{4,3,2,1,0:T(8,128)S(1)}, u32[]{:S(2)}, u32[]{:S(2)}) collective-permute-start(f32[1,1,8,32,256]{4,3,2,1,0:T(8,128)S(1)} %slice.287), channel_id=1, source_target_pairs={{0,16},{8,24},{16,0},{24,8},{1,17},{9,25},{17,1},{25,9},{2,18},{10... | collective-permute-start | bytes 786440 | tf_op jit(solution)/shard_map/ppermute | solution.py:15
  56.5 9.3 %collective-permute-start.16 = (f32[1,1,8,32,256]{4,3,2,1,0:T(8,128)S(1)}, f32[1,1,8,32,256]{4,3,2,1,0:T(8,128)S(1)}, u32[]{:S(2)}, u32[]{:S(2)}) collective-permute-start(f32[1,1,8,32,256]{4,3,2,1,0:T(8,128)S(1)} %slice.304), channel_id=1, source_target_pairs={{0,16},{8,24},{16,0},{24,8},{1,17},{9,25},{17,1},{25,9},{2,18},{10... | collective-permute-start | bytes 786440 | tf_op jit(solution)/shard_map/ppermute | solution.py:15
  65.9 11.4 %collective-permute-start.17 = (f32[1,8,32,256]{3,2,1,0:T(8,128)S(1)}, f32[1,8,32,256]{3,2,1,0:T(8,128)S(1)}, u32[]{:S(2)}, u32[]{:S(2)}) collective-permute-start(f32[1,8,32,256]{3,2,1,0:T(8,128)S(1)} %fusion.20.refs_0_.refs_1_), channel_id=1, source_target_pairs={{0,4},{4,0},{1,5},{5,1},{2,6},{6,2},{3,7},{7,3},{8,12},{12,8},{9,1... | collective-permute-start | bytes 786440 | tf_op jit(solution)/shard_map/ppermute | solution.py:15
  66.5 9.2 %collective-permute-start.24 = (f32[1,2,8,16,256]{4,3,2,1,0:T(8,128)S(1)}, f32[1,2,8,16,256]{4,3,2,1,0:T(8,128)S(1)}, u32[]{:S(2)}, u32[]{:S(2)}) collective-permute-start(f32[1,2,8,16,256]{4,3,2,1,0:T(8,128)S(1)} %fusion.5), channel_id=1, source_target_pairs={{0,16},{8,24},{16,0},{24,8},{1,17},{9,25},{17,1},{25,9},{2,18},{10... | collective-permute-start | bytes 786440 | tf_op jit(solution)/shard_map/ppermute | solution.py:15
  67.1 14.2 %collective-permute-start.11 = (f32[1,2,8,16,256]{4,3,2,1,0:T(8,128)S(1)}, f32[1,2,8,16,256]{4,3,2,1,0:T(8,128)S(1)}, u32[]{:S(2)}, u32[]{:S(2)}) collective-permute-start(f32[1,2,8,16,256]{4,3,2,1,0:T(8,128)S(1)} %pad_maximum_fusion.5), channel_id=1, source_target_pairs={{0,16},{8,24},{16,0},{24,8},{1,17},{9,25},{17,1},{25,9},{2,18},{10... | collective-permute-start | bytes 786440 | tf_op jit(solution)/shard_map/ppermute | solution.py:15
  69.1 13.9 %collective-permute-start.12 = (f32[1,8,32,256]{3,2,1,0:T(8,128)S(1)}, f32[1,8,32,256]{3,2,1,0:T(8,128)S(1)}, u32[]{:S(2)}, u32[]{:S(2)}) collective-permute-start(f32[1,8,32,256]{3,2,1,0:T(8,128)S(1)} %fusion.23.refs_0_), channel_id=1, source_target_pairs={{0,4},{4,0},{1,5},{5,1},{2,6},{6,2},{3,7},{7,3},{8,12},{12,8},{9,1... | collective-permute-start | bytes 786440 | tf_op jit(solution)/shard_map/ppermute | solution.py:15
  75.8 10.7 %collective-permute-start.26 = (f32[2,8,16,256]{3,2,1,0:T(8,128)S(1)}, f32[2,8,16,256]{3,2,1,0:T(8,128)S(1)}, u32[]{:S(2)}, u32[]{:S(2)}) collective-permute-start(f32[2,8,16,256]{3,2,1,0:T(8,128)S(1)} %fusion.17.refs_2_), channel_id=1, source_target_pairs={{0,4},{4,0},{1,5},{5,1},{2,6},{6,2},{3,7},{7,3},{8,12},{12,8},{9,1... | collective-permute-start | bytes 786440 | tf_op jit(solution)/shard_map/ppermute | solution.py:15
  77.3 9.1 %collective-permute-start.25 = (f32[1,2,8,16,256]{4,3,2,1,0:T(8,128)S(1)}, f32[1,2,8,16,256]{4,3,2,1,0:T(8,128)S(1)}, u32[]{:S(2)}, u32[]{:S(2)}) collective-permute-start(f32[1,2,8,16,256]{4,3,2,1,0:T(8,128)S(1)} %pad_maximum_fusion.4), channel_id=1, source_target_pairs={{0,16},{8,24},{16,0},{24,8},{1,17},{9,25},{17,1},{25,9},{2,18},{10... | collective-permute-start | bytes 786440 | tf_op jit(solution)/shard_map/ppermute | solution.py:15
  81.4 9.6 %collective-permute-start.29 = (f32[2,8,16,256]{3,2,1,0:T(8,128)S(1)}, f32[2,8,16,256]{3,2,1,0:T(8,128)S(1)}, u32[]{:S(2)}, u32[]{:S(2)}) collective-permute-start(f32[2,8,16,256]{3,2,1,0:T(8,128)S(1)} %fusion.8.refs_2_), channel_id=1, source_target_pairs={{0,4},{4,0},{1,5},{5,1},{2,6},{6,2},{3,7},{7,3},{8,12},{12,8},{9,1... | collective-permute-start | bytes 786440 | tf_op jit(solution)/shard_map/ppermute | solution.py:15
  84.4 9.9 %collective-permute-start.19 = (f32[2,4,64,128]{3,2,1,0:T(8,128)S(1)}, f32[2,4,64,128]{3,2,1,0:T(8,128)S(1)}, u32[]{:S(2)}, u32[]{:S(2)}) collective-permute-start(f32[2,4,64,128]{3,2,1,0:T(8,128)S(1)} %dynamic-slice_bitcast_fusion.2), channel_id=1, source_target_pairs={{0,8},{8,0},{16,24},{24,16},{1,9},{9,1},{17,25},{25,17},{2,10},{10... | collective-permute-start | bytes 786440 | tf_op jit(solution)/shard_map/ppermute | solution.py:15
  86.5 12.1 %collective-permute-start.35 = (f32[1,2,8,16,256]{4,3,2,1,0:T(8,128)S(1)}, f32[1,2,8,16,256]{4,3,2,1,0:T(8,128)S(1)}, u32[]{:S(2)}, u32[]{:S(2)}) collective-permute-start(f32[1,2,8,16,256]{4,3,2,1,0:T(8,128)S(1)} %fusion.4), channel_id=1, source_target_pairs={{0,16},{8,24},{16,0},{24,8},{1,17},{9,25},{17,1},{25,9},{2,18},{10... | collective-permute-start | bytes 786440 | tf_op jit(solution)/shard_map/ppermute | solution.py:15
  87.6 19.5 %collective-permute-start.39 = (f32[2,8,16,256]{3,2,1,0:T(8,128)S(1)}, f32[2,8,16,256]{3,2,1,0:T(8,128)S(1)}, u32[]{:S(2)}, u32[]{:S(2)}) collective-permute-start(f32[2,8,16,256]{3,2,1,0:T(8,128)S(1)} %fusion.3.refs_3_), channel_id=1, source_target_pairs={{0,4},{4,0},{1,5},{5,1},{2,6},{6,2},{3,7},{7,3},{8,12},{12,8},{9,1... | collective-permute-start | bytes 786440 | tf_op jit(solution)/shard_map/ppermute | solution.py:15
  91.0 10.2 %collective-permute-start.37 = (f32[1,2,8,16,256]{4,3,2,1,0:T(8,128)S(1)}, f32[1,2,8,16,256]{4,3,2,1,0:T(8,128)S(1)}, u32[]{:S(2)}, u32[]{:S(2)}) collective-permute-start(f32[1,2,8,16,256]{4,3,2,1,0:T(8,128)S(1)} %fusion), channel_id=1, source_target_pairs={{0,16},{8,24},{16,0},{24,8},{1,17},{9,25},{17,1},{25,9},{2,18},{10... | collective-permute-start | bytes 786440 | tf_op jit(solution)/shard_map/ppermute | solution.py:15
  91.8 11.4 %collective-permute-start.28 = (f32[2,8,16,256]{3,2,1,0:T(8,128)S(1)}, f32[2,8,16,256]{3,2,1,0:T(8,128)S(1)}, u32[]{:S(2)}, u32[]{:S(2)}) collective-permute-start(f32[2,8,16,256]{3,2,1,0:T(8,128)S(1)} %fusion.15.refs_2_), channel_id=1, source_target_pairs={{0,4},{4,0},{1,5},{5,1},{2,6},{6,2},{3,7},{7,3},{8,12},{12,8},{9,1... | collective-permute-start | bytes 786440 | tf_op jit(solution)/shard_map/ppermute | solution.py:15
  94.4 11.6 %collective-permute-start.20 = (f32[2,64,128]{2,1,0:T(8,128)S(1)}, f32[2,64,128]{2,1,0:T(8,128)S(1)}, u32[]{:S(2)}, u32[]{:S(2)}) collective-permute-start(f32[2,64,128]{2,1,0:T(8,128)S(1)} %get-tuple-element.80), channel_id=1, source_target_pairs={{0,1},{1,0},{2,3},{3,2},{4,5},{5,4},{6,7},{7,6},{8,9},{9,8},{10,11... | collective-permute-start | bytes 196616 | tf_op jit(solution)/shard_map/ppermute | solution.py:15
  103.2 13.8 %collective-permute-start.36 = (f32[2,8,16,256]{3,2,1,0:T(8,128)S(1)}, f32[2,8,16,256]{3,2,1,0:T(8,128)S(1)}, u32[]{:S(2)}, u32[]{:S(2)}) collective-permute-start(f32[2,8,16,256]{3,2,1,0:T(8,128)S(1)} %fusion.13.refs_3_), channel_id=1, source_target_pairs={{0,4},{4,0},{1,5},{5,1},{2,6},{6,2},{3,7},{7,3},{8,12},{12,8},{9,1... | collective-permute-start | bytes 786440 | tf_op jit(solution)/shard_map/ppermute | solution.py:15
  106.0 9.4 %collective-permute-start.38 = (f32[2,8,16,256]{3,2,1,0:T(8,128)S(1)}, f32[2,8,16,256]{3,2,1,0:T(8,128)S(1)}, u32[]{:S(2)}, u32[]{:S(2)}) collective-permute-start(f32[2,8,16,256]{3,2,1,0:T(8,128)S(1)} %fusion.11.refs_3_), channel_id=1, source_target_pairs={{0,4},{4,0},{1,5},{5,1},{2,6},{6,2},{3,7},{7,3},{8,12},{12,8},{9,1... | collective-permute-start | bytes 786440 | tf_op jit(solution)/shard_map/ppermute | solution.py:15
  106.7 12.2 %collective-permute-start.30 = (f32[2,4,80,128]{3,2,1,0:T(8,128)S(1)}, f32[2,4,80,128]{3,2,1,0:T(8,128)S(1)}, u32[]{:S(2)}, u32[]{:S(2)}) collective-permute-start(f32[2,4,80,128]{3,2,1,0:T(8,128)S(1)} %dynamic-slice_bitcast_fusion.1), channel_id=1, source_target_pairs={{0,8},{8,0},{16,24},{24,16},{1,9},{9,1},{17,25},{25,17},{2,10},{10... | collective-permute-start | bytes 983048 | tf_op jit(solution)/shard_map/ppermute | solution.py:15
  118.8 13.2 %collective-permute-start.40 = (f32[2,4,112,128]{3,2,1,0:T(8,128)S(1)}, f32[2,4,112,128]{3,2,1,0:T(8,128)S(1)}, u32[]{:S(2)}, u32[]{:S(2)}) collective-permute-start(f32[2,4,112,128]{3,2,1,0:T(8,128)S(1)} %dynamic-slice_bitcast_fusion), channel_id=1, source_target_pairs={{0,8},{8,0},{16,24},{24,16},{1,9},{9,1},{17,25},{25,17},{2,10},{10... | collective-permute-start | bytes 1376264 | tf_op jit(solution)/shard_map/ppermute | solution.py:15
  120.8 9.5 %collective-permute-start.32 = (f32[2,80,128]{2,1,0:T(8,128)S(1)}, f32[2,80,128]{2,1,0:T(8,128)S(1)}, u32[]{:S(2)}, u32[]{:S(2)}) collective-permute-start(f32[2,80,128]{2,1,0:T(8,128)S(1)} %get-tuple-element.79), channel_id=1, source_target_pairs={{0,2},{1,3},{2,0},{3,1},{4,6},{5,7},{6,4},{7,5},{8,10},{9,11},{10,... | collective-permute-start | bytes 245768 | tf_op jit(solution)/shard_map/ppermute | solution.py:15
  122.5 13.7 %collective-permute-start.23 = (f32[64,128]{1,0:T(8,128)S(1)}, f32[64,128]{1,0:T(8,128)S(1)}, u32[]{:S(2)}, u32[]{:S(2)}) collective-permute-start(f32[64,128]{1,0:T(8,128)S(1)} %dynamic-slice_bitcast_fusion.10), channel_id=1, source_target_pairs={{0,16},{8,24},{16,0},{24,8},{1,17},{9,25},{17,1},{25,9},{2,18},{10... | collective-permute-start | bytes 98312 | tf_op jit(solution)/shard_map/ppermute | solution.py:15
  132.8 17.3 %all-to-all-start = ((f32[8,112,128]{2,1,0:T(8,128)}), f32[8,112,128]{2,1,0:T(8,128)S(1)}, u32[]{:S(2)}, u32[]{:S(2)}) async-start(f32[8,112,128]{2,1,0:T(8,128)} %bitcast.83), calls=%async_computation | async-start | bytes 917504 | tf_op jit(solution)/shard_map/all_to_all | solution.py:157
  (12 other events, 74.4 us)

commit v3 on v2

--- a/solution.py
+++ b/solution.py
@@ -1,4 +1,5 @@
 import functools
+import math
 
 import jax
 import jax.numpy as jnp
@@ -8,7 +9,9 @@
 from jax.sharding import PartitionSpec as P
 
 VMEM_LIMIT = 48 << 20
-LAG = 3
+LAG = 2
+DEEP = 3
+BRIEF = pl.CostEstimate(flops=0, bytes_accessed=0, transcendentals=0)
 
 
 def swap(x, axis, bit):
@@ -29,31 +32,65 @@
     return dot(a[0], b[0]) + (dot(a[0], b[1]) + dot(a[1], b[0]))
 
 
-def truncate_kernel(_, layer_ref, factor_ref, out_ref):
-    out_ref[0] = product(split(layer_ref[0]), split(factor_ref[...]), ((0,), (0,)))
-
-
-def truncated(layers, field, factor):
+def gather_kernel(layers_ref, field_ref, out_ref, held, sems):
+    count = out_ref.shape[0]
+    reads = [pltpu.make_async_copy(field_ref.at[layers_ref[n]], held.at[n], sems.at[0, n]) for n in range(count)]
+    writes = [pltpu.make_async_copy(held.at[n], out_ref.at[n], sems.at[1, n]) for n in range(count)]
+    for read in reads:
+        read.start()
+    for read, write in zip(reads, writes):
+        read.wait()
+        write.start()
+    for write in writes:
+        write.wait()
+
+
+def gathered(layers, field):
+    shape = (layers.shape[0], *field.shape[1:])
+    return pl.pallas_call(
+        gather_kernel,
+        in_specs=[pl.BlockSpec(memory_space=pltpu.SMEM), pl.BlockSpec(memory_space=pl.ANY)],
+        out_specs=pl.BlockSpec(memory_space=pl.ANY),
+        out_shape=jax.ShapeDtypeStruct(shape, field.dtype),
+        scratch_shapes=[pltpu.VMEM(shape, field.dtype), pltpu.SemaphoreType.DMA((2, shape[0]))],
+        compiler_params=pltpu.CompilerParams(vmem_limit_bytes=VMEM_LIMIT),
+        cost_estimate=BRIEF,
+    )(layers, field)
+
+
+def truncate_kernel(cuts, _, *refs):
+    own, came, own_factor, came_factor = refs[:4]
+    layer = jnp.concatenate([own[0], came[0]], axis=0)
+    factor = jnp.concatenate([own_factor[...], came_factor[...]], axis=0)
+    out = product(split(layer), split(factor), ((0,), (0,)))
+    owners = refs[4].shape[1]
+    out = out.reshape(owners, -1, out.shape[1])
+    for ref, (low, high) in zip(refs[4:], cuts):
+        ref[0] = out[:, low:high]
+
+
+def truncated(layers, slots, field, came, factors, owners, cuts):
     count = layers.shape[0]
     _, rows, width = field.shape
-    ranks = factor.shape[1]
+    ranks = factors[0].shape[1]
+    outs = [(owners, high - low, ranks) for low, high in cuts]
     return pl.pallas_call(
-        truncate_kernel,
+        functools.partial(truncate_kernel, cuts),
         grid_spec=pltpu.PrefetchScalarGridSpec(
             num_scalar_prefetch=1,
             grid=(count,),
             in_specs=[
                 pl.BlockSpec((1, rows, width), lambda i, n: (n[i], 0, 0)),
+                pl.BlockSpec((1, rows, width), lambda i, n: (n[count + i], 0, 0)),
+                pl.BlockSpec((rows, ranks), lambda i, n: (0, 0)),
                 pl.BlockSpec((rows, ranks), lambda i, n: (0, 0)),
             ],
-            out_specs=pl.BlockSpec((1, width, ranks), lambda i, n: (i, 0, 0)),
+            out_specs=[pl.BlockSpec((1, *x), lambda i, n: (i, 0, 0, 0)) for x in outs],
         ),
-        out_shape=jax.ShapeDtypeStruct((count, width, ranks), jnp.float32),
+        out_shape=[jax.ShapeDtypeStruct((count, *x), jnp.float32) for x in outs],
         compiler_params=pltpu.CompilerParams(vmem_limit_bytes=VMEM_LIMIT),
-        cost_estimate=pl.CostEstimate(
-            flops=6 * count * rows * width * ranks, bytes_accessed=4 * count * width * (rows + ranks), transcendentals=0
-        ),
-    )(layers, field, factor)
+        cost_estimate=BRIEF,
+    )(jnp.concatenate([layers, slots]), field, came, *factors)
 
 
 def gram_kernel(ba, widths, counts, unit, added, me_ref, *refs):
@@ -107,9 +144,7 @@
         out_shape=jax.ShapeDtypeStruct((ba, owners, rows, owners * unit), jnp.float32),
         input_output_aliases={1 + len(flat): 0} if olds else {},
         compiler_params=pltpu.CompilerParams(vmem_limit_bytes=VMEM_LIMIT),
-        cost_estimate=pl.CostEstimate(
-            flops=6 * ba * owners * owners * rows * unit * inner, bytes_accessed=4 * sum(x.size for x in flat), transcendentals=0
-        ),
+        cost_estimate=BRIEF,
     )(me.reshape(1).astype(jnp.int32), *flat, *olds)
 
 
@@ -136,12 +171,16 @@
     return lax.dynamic_index_in_dim(pairs, core, 1, keepdims=False) + swap(send, "aa", 1)
 
 
-def block_by_permutes(region):
-    t = summed_over_core(region)
+def block_by_permutes(t):
     me_x, me_c = lax.axis_index("aa") >> 1, lax.axis_index("col")
-    total = lax.dynamic_index_in_dim(t, me_c, 1, keepdims=False)
-    for d in range(1, region.shape[1]):
-        total = total + swap(lax.dynamic_index_in_dim(t, me_c ^ d, 1, keepdims=False), "col", d)
+    bit = t.shape[1] // 2
+    while bit:
+        halves = t.reshape(t.shape[0], 2, bit, *t.shape[2:])
+        side = (me_c // bit) & 1
+        leaving = lax.dynamic_index_in_dim(halves, side ^ 1, 1, keepdims=False)
+        t = lax.dynamic_index_in_dim(halves, side, 1, keepdims=False) + swap(leaving, "col", bit)
+        bit //= 2
+    total = t[:, 0]
     places = total.shape[0]
     mine = lax.dynamic_index_in_dim(total, me_x, 0, keepdims=False)
     for d in range(1, places):
@@ -149,9 +188,8 @@
     return mine
 
 
-def block_by_all_to_all(region):
-    aa, col = region.shape[:2]
-    t = summed_over_core(region)
+def block_by_all_to_all(t):
+    aa, col = 2 * t.shape[0], t.shape[1]
     groups = [[(x * 2 + c) * col + z for x in range(aa // 2) for z in range(col)] for c in range(2)]
     t = t.reshape(aa // 2 * col, *t.shape[2:])
     return jnp.sum(lax.all_to_all(t, ("aa", "col"), 0, 0, tiled=True, axis_index_groups=groups), axis=0)
@@ -169,59 +207,83 @@
     unit = widths[-1]
     bits = [1 << n for n in range(aa.bit_length() - 1)]
     keep = order_of(bits[1:])
-    send = [d | 1 for d in keep]
-
-    def layers(places, c):
-        return jnp.concatenate([((me_a ^ d) * each + c).reshape(1) for d in places])
+    middle = each // 2
+    halves = [range(middle), range(middle, each)] if middle else [range(each)]
 
     def groups_of(i):
-        size = 1 if i == 0 else 2 if each % 2 == 0 else 1
-        return [range(c, c + size) for c in range(0, each, size)]
-
-    def parts_of(c, i):
-        first = sum(widths[:i])
-        kept, came = kept_of[c], came_of[c]
-        kept, came = (x.reshape(len(keep), 1, owners, rest, ranks)[:, :, :, first : first + widths[i]] for x in (kept, came))
-        return kept + came
-
-    kept_of, came_of = {}, {}
-
-    def send_core(c, *after):
-        out = truncated(tie(layers(send, c), *after), field, factor)
-        came_of[c] = swap(out, "aa", 1)
-        return out
-
-    def keep_core(c, *after):
-        kept_of[c] = truncated(tie(layers(keep, c), *after), field, factor)
+        if i == 0:
+            return [range(c, c + 1) for c in range(each)]
+        if i == len(widths) - 1 and len(halves[-1]) > 1:
+            return halves[:-1] + [range(middle, each - 1), range(each - 1, each)]
+        return halves
+
+    cuts = [(0, widths[0])] + ([(widths[0], rest)] if len(widths) > 1 else [])
+    trips = [range(c, c + 1) for c in range(min(2, each))] + ([range(2, each)] if each > 2 else [])
+    came_of, terms = {}, {}
+    factors = [factor, swap(factor, "aa", 1)]
+    for n, trip in enumerate(trips):
+        first = (me_a & 1 ^ 1) * each
+        if n:
+            first = tie(first, going, *(factors[1:] if n == 1 else []))
+        going = gathered(jnp.stack([first + 2 * each * x + c for x in range(aa // 2) for c in trip]), field)
+        if n > 1:
+            going = tie(going, came_of[0][0])
+        came = swap(going, "aa", 1)
+        for c in trip:
+            came_of[c] = came, [(me_a ^ d) // 2 * len(trip) + c - trip[0] for d in keep]
+
+    def truncate(c, *after):
+        came, slots = came_of[c]
+        half = len(keep) // 2
+        terms[c] = []
+        for part in (range(half), range(half, len(keep))):
+            if part:
+                layers = jnp.stack([(me_a ^ keep[n]) * each + c for n in part])
+                places = jnp.stack([slots[n] for n in part])
+                after = tie(layers, *after), places
+                terms[c].append(truncated(*after, field, came, factors, owners, cuts))
+                after = terms[c][-1][:1]
+
+    def terms_of(part, group, i):
+        cut = min(i, 1)
+        first = sum(widths[:i]) - cuts[cut][0]
+        found = [terms[c][part][cut] for c in group]
+        found = [x.reshape(x.shape[0], 1, *x.shape[1:])[:, :, :, first : first + widths[i]] for x in found]
+        return jnp.concatenate(found, axis=1)
 
     steps = [(i, group) for i in range(len(widths)) for group in groups_of(i)]
     pieces = {}
     regions, blocks = [None] * len(widths), []
-    arrived, passed, waiting, leaving_of = [], [], [], {}
+    arrived, passed, waiting, halfway, leaving_of = [], [], [], [], {}
 
     def add_gram(i, group, *after):
         used = [
             [[pieces[d, s, g] for g in groups_of(s) if g[0] in group] for s in range(i + 1)] for d in range(ba)
         ]
-        regions[i] = gram_strip(tie(me_b, *after), used, widths[: i + 1], unit, regions[i])
+        regions[i] = gram_strip(tie(me_b, *after, *halfway), used, widths[: i + 1], unit, regions[i])
         if group[-1] == each - 1:
             region = regions[i].reshape(aa, col, *regions[i].shape[2:])
-            blocks.append(block_by_permutes(region) if i < len(widths) - 1 else block_by_all_to_all(region))
-
-    keep_core(0, send_core(0))
-    out = send_core(1, kept_of[0]) if each > 1 else None
+            summed = summed_over_core(region)
+            halfway.append(summed)
+            blocks.append(block_by_permutes(summed) if i < len(widths) - 1 else block_by_all_to_all(summed))
+
+    def send(n):
+        i, group = steps[n]
+        if i == 0:
+            truncate(n, *(terms[n - 1][-1][:1] if n else []), *(arrived[n - DEEP : n - DEEP + 1] if n >= DEEP else []))
+        after = ([arrived[n - DEEP]] if n >= DEEP else []) + (passed[n - DEEP - 2] if n >= DEEP + 2 else [])
+        leaving_of[n] = terms_of(0, group, i)
+        if after:
+            leaving_of[n] = tie(leaving_of[n], *after)
+
+    for n in range(min(DEEP - 1, len(steps))):
+        send(n)
     for n, (i, group) in enumerate(steps):
-        t = jnp.concatenate([parts_of(c, i) for c in group], axis=1)
-        half = t.shape[0] // 2
-        leaving, t = (t[:half], t[half:]) if bits[1:] else (t, t)
-        if i == 0 and n + 1 < each:
-            keep_core(n + 1, leaving, out)
-            if n + 2 < each:
-                out = send_core(n + 2, kept_of[n + 1])
-        after = ([arrived[n - 2]] if n >= 2 else []) + (passed[n - 4] if n >= 4 else [])
-        if after:
-            leaving = tie(leaving, *after)
-        leaving_of[n] = leaving
+        ahead = n + DEEP - 1
+        if ahead < len(steps):
+            send(ahead)
+        leaving = leaving_of[n]
+        t = tie(terms_of(-1, group, i), leaving_of[min(ahead, len(steps) - 1)])
         for bit in bits[1:]:
             t = t + swap(leaving, "aa", bit)
             half = t.shape[0] // 2
@@ -231,11 +293,13 @@
         passed.append([swap(t, "ba", d) for d in range(1, ba)])
         for d, x in enumerate([t] + passed[-1]):
             pieces[d, i, group] = x
-        waiting.append((i, group))
-        if len(waiting) > LAG:
-            add_gram(*waiting.pop(0), leaving_of[n])
+        for part in halves:
+            if group[-1] == part[-1]:
+                waiting.append((n, i, part))
+        if waiting and waiting[0][0] <= n - LAG:
+            add_gram(*waiting.pop(0)[1:], leaving_of[min(ahead, len(steps) - 1)])
     while waiting:
-        add_gram(*waiting.pop(0))
+        add_gram(*waiting.pop(0)[1:])
 
     lanes = owners * unit
     columns = [[None] * len(widths) for _ in widths]

time: 152 us -> 142 us (0.934)
  starting transfers between devices: 48.3 us -> 39.8 us
  Pallas kernels: 41.1 us -> 46.8 us
  other arithmetic: 7.32 us -> 2.86 us
  waiting for transfers between devices: 51.1 us -> 48.7 us
    ppermute x41 -> x35, starting transfers between devices: 44.8 us -> 36.4 us  [swap(): lax.ppermute(x, axis, [(i, i ^ bit) for i in range(lax.axis_size(axis))])]
    pallas_call x12 -> x15, Pallas kernels: 29.8 us -> 36.6 us  [the longest x12 28 us: truncated(): pl.pallas_call(functools.partial(truncate_kernel, cuts), grid_spec=pltpu....]
    add x14 -> x4, other arithmetic: 5.14 us -> 0.06 us  [block_by_permutes(): lax.dynamic_index_in_dim(halves, side, 1, keepdims=False)]
    ppermute x41 -> x35, waiting for transfers between devices: 37.9 us -> 36.4 us  [swap(): lax.ppermute(x, axis, [(i, i ^ bit) for i in range(lax.axis_size(axis))])]
    pallas_call x12 -> x6, Pallas kernels: 11.3 us -> 10.2 us  [gram_strip(): pl.pallas_call(functools.partial(gram_kernel, ba, widths, counts, unit, l...]
  transfers between devices with their start and end apart: 42 -> 36, of which waited for: 11 -> 15; matrix products, arithmetic and copies ran while one was open for 5% -> 2% of each run, Pallas kernels for 25% -> 25%
where the time goes in v3:
time: 142 us; the launch traced here: 141 us
  waiting for transfers between devices  48.7 us (34%)
  Pallas kernels  46.8 us (33%)
  starting transfers between devices  39.8 us (28%)
  other arithmetic  2.86 us (2%)
  local copies, waits for them, and re-layouts  2.29 us (2%)
    ppermute x35, waiting for transfers between devices, swap(): lax.ppermute(x, axis, [(i, i ^ bit) for i in range(lax.axis_size(axis))])  36.4 us
    ppermute x35, starting transfers between devices, swap(): lax.ppermute(x, axis, [(i, i ^ bit) for i in range(lax.axis_size(axis))])  36.4 us
    pallas_call x12, Pallas kernels, truncated(): pl.pallas_call(functools.partial(truncate_kernel, cuts), grid_spec=pltpu....  28 us
    all_to_all x1, waiting for transfers between devices, block_by_all_to_all(): lax.all_to_all(t, ('aa', 'col'), 0, 0, tiled=True, axis_index_groups=groups)  12.3 us
    pallas_call x6, Pallas kernels, gram_strip(): pl.pallas_call(functools.partial(gram_kernel, ba, widths, counts, unit, l...  10.2 us
    pallas_call x3, Pallas kernels, gathered(): pl.pallas_call(gather_kernel, in_specs=[pl.BlockSpec(memory_space=pltpu.S...  8.63 us
    all_to_all x1, starting transfers between devices, block_by_all_to_all(): lax.all_to_all(t, ('aa', 'col'), 0, 0, tiled=True, axis_index_groups=groups)  3.47 us
  transfers between devices with their start and end apart: 36, of which 15 were waited for; matrix products, arithmetic and copies ran while one was open for 2% of the time, Pallas kernels for 25%

profile of v3, /device:TPU:0, one launch (start us, length us, event | category | flops | bytes accessed | tf_op | source)
XLA Modules:
  0.0 141.3 jit_solution(14032731307294385735)
XLA Ops:
  2.6 2.5 %collective-permute-done.1.refs_3_ = f32[256,256]{1,0:T(8,128)S(1)} collective-permute-done((f32[256,256]{1,0:T(8,128)S(1)}, f32[256,256]{1,0:T(8,128)S(1)}, u32[]{:S(2)}, u32[]{:S(2)}) %collective-permute-start.1) | collective-permute-done | bytes 262176 | tf_op jit(solution)/shard_map/ppermute | solution.py:18
  5.1 2.2 %shard_map.29 = (f32[1,8,32,256]{3,2,1,0:T(8,128)S(1)}, f32[1,8,32,256]{3,2,1,0:T(8,128)S(1)}) custom-call(s32[2]{0:T(128)S(1)} %pad_add_fusion._, f32[24,256,512]{2,1,0:T(8,128)} %refs_0_.23, f32[2,256,512]{2,1,0:T(8,128)S(1)} %collective-permute-done.refs_1_, f32[256,256]{1,0:T(8,128)S(1)} %copy-done, f32[256,256]{1,0:T(8,128)S(1)} %collective-permute-done.1.refs_3_), custom_call_target="tpu_custom_call" | custom-call | tf_op jit(solution)/shard_map/pallas_call | solution.py:77
  7.4 2.6 %shard_map.31 = f32[2,256,512]{2,1,0:T(8,128)} custom-call(s32[2]{0:T(128)S(1)} %get-tuple-element.158.layers_ref, f32[24,256,512]{2,1,0:T(8,128)} %refs_0_.23), custom_call_target="tpu_custom_call" | custom-call | tf_op jit(solution)/shard_map/pallas_call | solution.py:50
  10.1 4.2 %shard_map.34 = f32[8,256,512]{2,1,0:T(8,128)} custom-call(s32[8]{0:T(128)S(1)} %stack.137.layers_ref, f32[24,256,512]{2,1,0:T(8,128)} %refs_0_.23), custom_call_target="tpu_custom_call" | custom-call | tf_op jit(solution)/shard_map/pallas_call | solution.py:50
  14.9 2.2 %shard_map.30 = (f32[1,8,32,256]{3,2,1,0:T(8,128)S(1)}, f32[1,8,32,256]{3,2,1,0:T(8,128)S(1)}) custom-call(s32[2]{0:T(128)S(1)} %get-tuple-element.157._, f32[24,256,512]{2,1,0:T(8,128)} %refs_0_.23, f32[2,256,512]{2,1,0:T(8,128)S(1)} %collective-permute-done.refs_1_, f32[256,256]{1,0:T(8,128)S(1)} %copy-done, f32[256,256]{1,0:T(8,128)S(1)} %collective-permute-done.1.refs_3_), custom_call_target="tpu_custom_call" | custom-call | tf_op jit(solution)/shard_map/pallas_call | solution.py:77
  17.1 2.9 %collective-permute-start.4 = (f32[1,1,8,32,256]{4,3,2,1,0:T(8,128)S(1)}, f32[1,1,8,32,256]{4,3,2,1,0:T(8,128)S(1)}, u32[]{:S(2)}, u32[]{:S(2)}) collective-permute-start(f32[1,1,8,32,256]{4,3,2,1,0:T(8,128)S(1)} %bitcast.188), channel_id=1, source_target_pairs={{0,16},{8,24},{16,0},{24,8},{1,17},{9,25},{17,1},{25,9},{2,18},{10... | collective-permute-start | bytes 786440 | tf_op jit(solution)/shard_map/ppermute | solution.py:18
  20.2 2.3 %collective-permute-done.2.refs_1_ = f32[2,256,512]{2,1,0:T(8,128)S(1)} collective-permute-done((f32[2,256,512]{2,1,0:T(8,128)}, f32[2,256,512]{2,1,0:T(8,128)S(1)}, u32[]{:S(2)}, u32[]{:S(2)}) %collective-permute-start.2) | collective-permute-done | bytes 1048608 | tf_op jit(solution)/shard_map/ppermute | solution.py:18
  22.5 2.2 %shard_map.32 = (f32[1,8,32,256]{3,2,1,0:T(8,128)S(1)}, f32[1,8,32,256]{3,2,1,0:T(8,128)S(1)}) custom-call(s32[2]{0:T(128)S(1)} %pad_add_fusion.3._, f32[24,256,512]{2,1,0:T(8,128)} %refs_0_.23, f32[2,256,512]{2,1,0:T(8,128)S(1)} %collective-permute-done.2.refs_1_, f32[256,256]{1,0:T(8,128)S(1)} %copy-done, f32[256,256]{1,0:T(8,128)S(1)} %collective-permute-done.1.refs_3_), custom_call_target="tpu_custom_call" | custom-call | tf_op jit(solution)/shard_map/pallas_call | solution.py:77
  24.8 2.2 %shard_map.33 = (f32[1,8,32,256]{3,2,1,0:T(8,128)S(1)}, f32[1,8,32,256]{3,2,1,0:T(8,128)S(1)}) custom-call(s32[2]{0:T(128)S(1)} %pad_add_fusion.5._, f32[24,256,512]{2,1,0:T(8,128)} %refs_0_.23, f32[2,256,512]{2,1,0:T(8,128)S(1)} %collective-permute-done.2.refs_1_, f32[256,256]{1,0:T(8,128)S(1)} %copy-done, f32[256,256]{1,0:T(8,128)S(1)} %collective-permute-done.1.refs_3_), custom_call_target="tpu_custom_call" | custom-call | tf_op jit(solution)/shard_map/pallas_call | solution.py:77
  27.0 2.7 %collective-permute-start.5 = (f32[1,1,8,32,256]{4,3,2,1,0:T(8,128)S(1)}, f32[1,1,8,32,256]{4,3,2,1,0:T(8,128)S(1)}, u32[]{:S(2)}, u32[]{:S(2)}) collective-permute-start(f32[1,1,8,32,256]{4,3,2,1,0:T(8,128)S(1)} %bitcast.193), channel_id=1, source_target_pairs={{0,16},{8,24},{16,0},{24,8},{1,17},{9,25},{17,1},{25,9},{2,18},{10... | collective-permute-start | bytes 786440 | tf_op jit(solution)/shard_map/ppermute | solution.py:18
  29.9 2.4 %shard_map.35 = (f32[1,8,32,256]{3,2,1,0:T(8,128)S(1)}, f32[1,8,32,256]{3,2,1,0:T(8,128)S(1)}) custom-call(s32[2]{0:T(128)S(1)} %pad_add_fusion.6._, f32[24,256,512]{2,1,0:T(8,128)} %refs_0_.23, f32[8,256,512]{2,1,0:T(8,128)} %collective-permute-done.3.refs_1_, f32[256,256]{1,0:T(8,128)S(1)} %copy-done, f32[256,256]{1,0:T(8,128)S(1)} %collective-permute-done.1.refs_3_), custom_call_target="tpu_custom_call" | custom-call | tf_op jit(solution)/shard_map/pallas_call | solution.py:77
  32.4 2.1 %collective-permute-start.7 = (f32[1,8,32,256]{3,2,1,0:T(8,128)S(1)}, f32[1,8,32,256]{3,2,1,0:T(8,128)S(1)}, u32[]{:S(2)}, u32[]{:S(2)}) collective-permute-start(f32[1,8,32,256]{3,2,1,0:T(8,128)S(1)} %add_bitcast_fusion.9.refs_0_), channel_id=1, source_target_pairs={{0,4},{4,0},{1,5},{5,1},{2,6},{6,2},{3,7},{7,3},{8,12},{12,8},{9,1... | collective-permute-start | bytes 786440 | tf_op jit(solution)/shard_map/ppermute | solution.py:18
  34.6 2.4 %shard_map.36 = (f32[1,8,32,256]{3,2,1,0:T(8,128)S(1)}, f32[1,8,32,256]{3,2,1,0:T(8,128)S(1)}) custom-call(s32[2]{0:T(128)S(1)} %pad_add_fusion.7._, f32[24,256,512]{2,1,0:T(8,128)} %refs_0_.23, f32[8,256,512]{2,1,0:T(8,128)} %collective-permute-done.3.refs_1_, f32[256,256]{1,0:T(8,128)S(1)} %copy-done, f32[256,256]{1,0:T(8,128)S(1)} %collective-permute-done.1.refs_3_), custom_call_target="tpu_custom_call" | custom-call | tf_op jit(solution)/shard_map/pallas_call | solution.py:77
  37.0 2.4 %shard_map.37 = (f32[1,8,32,256]{3,2,1,0:T(8,128)S(1)}, f32[1,8,32,256]{3,2,1,0:T(8,128)S(1)}) custom-call(s32[2]{0:T(128)S(1)} %pad_add_fusion.8._, f32[24,256,512]{2,1,0:T(8,128)} %refs_0_.23, f32[8,256,512]{2,1,0:T(8,128)} %collective-permute-done.3.refs_1_, f32[256,256]{1,0:T(8,128)S(1)} %copy-done, f32[256,256]{1,0:T(8,128)S(1)} %collective-permute-done.1.refs_3_), custom_call_target="tpu_custom_call" | custom-call | tf_op jit(solution)/shard_map/pallas_call | solution.py:77
  41.7 2.4 %shard_map.38 = (f32[1,8,32,256]{3,2,1,0:T(8,128)S(1)}, f32[1,8,32,256]{3,2,1,0:T(8,128)S(1)}) custom-call(s32[2]{0:T(128)S(1)} %pad_add_fusion.9._, f32[24,256,512]{2,1,0:T(8,128)} %refs_0_.23, f32[8,256,512]{2,1,0:T(8,128)} %collective-permute-done.3.refs_1_, f32[256,256]{1,0:T(8,128)S(1)} %copy-done, f32[256,256]{1,0:T(8,128)S(1)} %collective-permute-done.1.refs_3_), custom_call_target="tpu_custom_call" | custom-call | tf_op jit(solution)/shard_map/pallas_call | solution.py:77
  44.1 2.4 %shard_map.39 = (f32[1,8,32,256]{3,2,1,0:T(8,128)S(1)}, f32[1,8,32,256]{3,2,1,0:T(8,128)S(1)}) custom-call(s32[2]{0:T(128)S(1)} %pad_add_fusion.10._, f32[24,256,512]{2,1,0:T(8,128)} %refs_0_.23, f32[8,256,512]{2,1,0:T(8,128)} %collective-permute-done.3.refs_1_, f32[256,256]{1,0:T(8,128)S(1)} %copy-done, f32[256,256]{1,0:T(8,128)S(1)} %collective-permute-done.1.refs_3_), custom_call_target="tpu_custom_call" | custom-call | tf_op jit(solution)/shard_map/pallas_call | solution.py:77
  46.8 2.4 %shard_map.40 = (f32[1,8,32,256]{3,2,1,0:T(8,128)S(1)}, f32[1,8,32,256]{3,2,1,0:T(8,128)S(1)}) custom-call(s32[2]{0:T(128)S(1)} %pad_add_fusion.11._, f32[24,256,512]{2,1,0:T(8,128)} %refs_0_.23, f32[8,256,512]{2,1,0:T(8,128)} %collective-permute-done.3.refs_1_, f32[256,256]{1,0:T(8,128)S(1)} %copy-done, f32[256,256]{1,0:T(8,128)S(1)} %collective-permute-done.1.refs_3_), custom_call_target="tpu_custom_call" | custom-call | tf_op jit(solution)/shard_map/pallas_call | solution.py:77
  49.5 2.1 %collective-permute-start.11 = (f32[1,8,32,256]{3,2,1,0:T(8,128)S(1)}, f32[1,8,32,256]{3,2,1,0:T(8,128)S(1)}, u32[]{:S(2)}, u32[]{:S(2)}) collective-permute-start(f32[1,8,32,256]{3,2,1,0:T(8,128)S(1)} %add_bitcast_fusion.7.refs_2_), channel_id=1, source_target_pairs={{0,4},{4,0},{1,5},{5,1},{2,6},{6,2},{3,7},{7,3},{8,12},{12,8},{9,1... | collective-permute-start | bytes 786440 | tf_op jit(solution)/shard_map/ppermute | solution.py:18
  51.7 2.4 %shard_map.41 = (f32[1,8,32,256]{3,2,1,0:T(8,128)S(1)}, f32[1,8,32,256]{3,2,1,0:T(8,128)S(1)}) custom-call(s32[2]{0:T(128)S(1)} %pad_add_fusion.12._, f32[24,256,512]{2,1,0:T(8,128)} %refs_0_.23, f32[8,256,512]{2,1,0:T(8,128)} %collective-permute-done.3.refs_1_, f32[256,256]{1,0:T(8,128)S(1)} %copy-done, f32[256,256]{1,0:T(8,128)S(1)} %collective-permute-done.1.refs_3_), custom_call_target="tpu_custom_call" | custom-call | tf_op jit(solution)/shard_map/pallas_call | solution.py:77
  58.5 2.4 %shard_map.42 = (f32[1,8,32,256]{3,2,1,0:T(8,128)S(1)}, f32[1,8,32,256]{3,2,1,0:T(8,128)S(1)}) custom-call(s32[2]{0:T(128)S(1)} %pad_add_fusion.13._, f32[24,256,512]{2,1,0:T(8,128)} %refs_0_.23, f32[8,256,512]{2,1,0:T(8,128)} %collective-permute-done.3.refs_1_, f32[256,256]{1,0:T(8,128)S(1)} %copy-done, f32[256,256]{1,0:T(8,128)S(1)} %collective-permute-done.1.refs_3_), custom_call_target="tpu_custom_call" | custom-call | tf_op jit(solution)/shard_map/pallas_call | solution.py:77
  66.5 5.4 %collective-permute-done.14 = f32[1,3,8,16,256]{4,3,2,1,0:T(8,128)S(1)} collective-permute-done((f32[1,3,8,16,256]{4,3,2,1,0:T(8,128)S(1)}, f32[1,3,8,16,256]{4,3,2,1,0:T(8,128)S(1)}, u32[]{:S(2)}, u32[]{:S(2)}) %collective-permute-start.14) | collective-permute-done | bytes 393248 | tf_op jit(solution)/shard_map/ppermute | solution.py:18
  74.0 2.3 %collective-permute-done.16.refs_5_.refs_6_.refs_8_ = f32[1,8,32,256]{3,2,1,0:T(8,128)S(1)} collective-permute-done((f32[1,8,32,256]{3,2,1,0:T(8,128)S(1)}, f32[1,8,32,256]{3,2,1,0:T(8,128)S(1)}, u32[]{:S(2)}, u32[]{:S(2)}) %collective-permute-start.16) | collective-permute-done | bytes 262176 | tf_op jit(solution)/shard_map/ppermute | solution.py:18
  77.2 3.0 %collective-permute-done.21 = f32[1,3,8,16,256]{4,3,2,1,0:T(8,128)S(1)} collective-permute-done((f32[1,3,8,16,256]{4,3,2,1,0:T(8,128)S(1)}, f32[1,3,8,16,256]{4,3,2,1,0:T(8,128)S(1)}, u32[]{:S(2)}, u32[]{:S(2)}) %collective-permute-start.21) | collective-permute-done | bytes 393248 | tf_op jit(solution)/shard_map/ppermute | solution.py:18
  80.4 11.3 %collective-permute-done.28 = f32[1,2,8,16,256]{4,3,2,1,0:T(8,128)S(1)} collective-permute-done((f32[1,2,8,16,256]{4,3,2,1,0:T(8,128)S(1)}, f32[1,2,8,16,256]{4,3,2,1,0:T(8,128)S(1)}, u32[]{:S(2)}, u32[]{:S(2)}) %collective-permute-start.28) | collective-permute-done | bytes 262176 | tf_op jit(solution)/shard_map/ppermute | solution.py:18
  96.7 2.6 %collective-permute-start.18 = (f32[2,2,64,128]{3,2,1,0:T(8,128)S(1)}, f32[2,2,64,128]{3,2,1,0:T(8,128)S(1)}, u32[]{:S(2)}, u32[]{:S(2)}) collective-permute-start(f32[2,2,64,128]{3,2,1,0:T(8,128)S(1)} %dynamic-slice_bitcast_fusion.4), channel_id=1, source_target_pairs={{0,2},{1,3},{2,0},{3,1},{4,6},{5,7},{6,4},{7,5},{8,10},{9,11},{10,... | collective-permute-start | bytes 393224 | tf_op jit(solution)/shard_map/ppermute | solution.py:18
  105.5 2.7 %collective-permute-start.25 = (f32[2,2,80,128]{3,2,1,0:T(8,128)S(1)}, f32[2,2,80,128]{3,2,1,0:T(8,128)S(1)}, u32[]{:S(2)}, u32[]{:S(2)}) collective-permute-start(f32[2,2,80,128]{3,2,1,0:T(8,128)S(1)} %dynamic-slice_bitcast_fusion.3), channel_id=1, source_target_pairs={{0,2},{1,3},{2,0},{3,1},{4,6},{5,7},{6,4},{7,5},{8,10},{9,11},{10,... | collective-permute-start | bytes 491528 | tf_op jit(solution)/shard_map/ppermute | solution.py:18
  108.5 2.4 %shard_map.47.refs_12_ = f32[2,8,112,128]{3,2,1,0:T(8,128)S(1)} custom-call(s32[1]{0:T(128)} %bitcast.92.me_ref, f32[1,8,32,256]{3,2,1,0:T(8,128)S(1)} %add_bitcast_fusion.9.refs_0_, f32[1,8,32,256]{3,2,1,0:T(8,128)S(1)} %add_bitcast_fusion.8.refs_1_, f32[1,8,32,256]{3,2,1,0:T(8,128)S(1)} %add_bitcast_fusion.7.refs_2_, ...), custom_call_target="tpu_custom_call" | custom-call | tf_op jit(solution)/shard_map/pallas_call | solution.py:140
  110.9 2.4 %shard_map.48 = f32[2,8,112,128]{3,2,1,0:T(8,128)S(1)} custom-call(s32[1]{0:T(128)} %bitcast.89.me_ref, f32[1,8,32,256]{3,2,1,0:T(8,128)S(1)} %add_bitcast_fusion.6.refs_0_, f32[1,8,32,256]{3,2,1,0:T(8,128)S(1)} %add_bitcast_fusion.5.refs_1_, f32[1,8,32,256]{3,2,1,0:T(8,128)S(1)} %add_bitcast_fusion.4.refs_2_, ...), custom_call_target="tpu_custom_call", output_to_operand_aliasing={{}: (13, {})} | custom-call | tf_op jit(solution)/shard_map/pallas_call | solution.py:140
  113.4 2.8 %collective-permute-done.25 = f32[2,2,80,128]{3,2,1,0:T(8,128)S(1)} collective-permute-done((f32[2,2,80,128]{3,2,1,0:T(8,128)S(1)}, f32[2,2,80,128]{3,2,1,0:T(8,128)S(1)}, u32[]{:S(2)}, u32[]{:S(2)}) %collective-permute-start.25) | collective-permute-done | bytes 163872 | tf_op jit(solution)/shard_map/ppermute | solution.py:18
  118.0 2.8 %collective-permute-done.26 = f32[2,1,80,128]{3,2,1,0:T(8,128)S(1)} collective-permute-done((f32[2,1,80,128]{3,2,1,0:T(8,128)S(1)}, f32[2,1,80,128]{3,2,1,0:T(8,128)S(1)}, u32[]{:S(2)}, u32[]{:S(2)}) %collective-permute-start.26) | collective-permute-done | bytes 81952 | tf_op jit(solution)/shard_map/ppermute | solution.py:18
  123.3 3.5 %all-to-all-start = ((f32[8,112,128]{2,1,0:T(8,128)}), f32[8,112,128]{2,1,0:T(8,128)S(1)}, u32[]{:S(2)}, u32[]{:S(2)}) async-start(f32[8,112,128]{2,1,0:T(8,128)} %bitcast.97), calls=%async_computation | async-start | bytes 917504 | tf_op jit(solution)/shard_map/all_to_all | solution.py:195
  127.4 12.3 %all-to-all-done = f32[8,112,128]{2,1,0:T(8,128)S(1)} async-done(((f32[8,112,128]{2,1,0:T(8,128)}), f32[8,112,128]{2,1,0:T(8,128)S(1)}, u32[]{:S(2)}, u32[]{:S(2)}) %all-to-all-start) | async-done | bytes 458784 | tf_op jit(solution)/shard_map/all_to_all | solution.py:195
  (147 shorter events, 37.6 us)
Async XLA Ops:
  14.3 15.5 %collective-permute-start.3 = (f32[8,256,512]{2,1,0:T(8,128)}, f32[8,256,512]{2,1,0:T(8,128)}, u32[]{:S(2)}, u32[]{:S(2)}) collective-permute-start(f32[8,256,512]{2,1,0:T(8,128)} %shard_map.34), channel_id=1, source_target_pairs={{0,8},{8,0},{16,24},{24,16},{1,9},{9,1},{17,25},{25,17},{2,10},{10... | collective-permute-start | bytes 12582920 | tf_op jit(solution)/shard_map/ppermute | solution.py:18
  14.8 7.7 %collective-permute-start.2 = (f32[2,256,512]{2,1,0:T(8,128)}, f32[2,256,512]{2,1,0:T(8,128)S(1)}, u32[]{:S(2)}, u32[]{:S(2)}) collective-permute-start(f32[2,256,512]{2,1,0:T(8,128)} %shard_map.31), channel_id=1, source_target_pairs={{0,8},{8,0},{16,24},{24,16},{1,9},{9,1},{17,25},{25,17},{2,10},{10... | collective-permute-start | bytes 3145736 | tf_op jit(solution)/shard_map/ppermute | solution.py:18
  17.1 15.2 %collective-permute-start.4 = (f32[1,1,8,32,256]{4,3,2,1,0:T(8,128)S(1)}, f32[1,1,8,32,256]{4,3,2,1,0:T(8,128)S(1)}, u32[]{:S(2)}, u32[]{:S(2)}) collective-permute-start(f32[1,1,8,32,256]{4,3,2,1,0:T(8,128)S(1)} %bitcast.188), channel_id=1, source_target_pairs={{0,16},{8,24},{16,0},{24,8},{1,17},{9,25},{17,1},{25,9},{2,18},{10... | collective-permute-start | bytes 786440 | tf_op jit(solution)/shard_map/ppermute | solution.py:18
  27.0 14.0 %collective-permute-start.5 = (f32[1,1,8,32,256]{4,3,2,1,0:T(8,128)S(1)}, f32[1,1,8,32,256]{4,3,2,1,0:T(8,128)S(1)}, u32[]{:S(2)}, u32[]{:S(2)}) collective-permute-start(f32[1,1,8,32,256]{4,3,2,1,0:T(8,128)S(1)} %bitcast.193), channel_id=1, source_target_pairs={{0,16},{8,24},{16,0},{24,8},{1,17},{9,25},{17,1},{25,9},{2,18},{10... | collective-permute-start | bytes 786440 | tf_op jit(solution)/shard_map/ppermute | solution.py:18
  32.3 17.2 %collective-permute-start.6 = (f32[1,1,8,32,256]{4,3,2,1,0:T(8,128)S(1)}, f32[1,1,8,32,256]{4,3,2,1,0:T(8,128)S(1)}, u32[]{:S(2)}, u32[]{:S(2)}) collective-permute-start(f32[1,1,8,32,256]{4,3,2,1,0:T(8,128)S(1)} %bitcast.189), channel_id=1, source_target_pairs={{0,16},{8,24},{16,0},{24,8},{1,17},{9,25},{17,1},{25,9},{2,18},{10... | collective-permute-start | bytes 786440 | tf_op jit(solution)/shard_map/ppermute | solution.py:18
  32.4 21.7 %collective-permute-start.7 = (f32[1,8,32,256]{3,2,1,0:T(8,128)S(1)}, f32[1,8,32,256]{3,2,1,0:T(8,128)S(1)}, u32[]{:S(2)}, u32[]{:S(2)}) collective-permute-start(f32[1,8,32,256]{3,2,1,0:T(8,128)S(1)} %add_bitcast_fusion.9.refs_0_), channel_id=1, source_target_pairs={{0,4},{4,0},{1,5},{5,1},{2,6},{6,2},{3,7},{7,3},{8,12},{12,8},{9,1... | collective-permute-start | bytes 786440 | tf_op jit(solution)/shard_map/ppermute | solution.py:18
  39.4 16.2 %collective-permute-start.8 = (f32[1,1,8,32,256]{4,3,2,1,0:T(8,128)S(1)}, f32[1,1,8,32,256]{4,3,2,1,0:T(8,128)S(1)}, u32[]{:S(2)}, u32[]{:S(2)}) collective-permute-start(f32[1,1,8,32,256]{4,3,2,1,0:T(8,128)S(1)} %bitcast.190), channel_id=1, source_target_pairs={{0,16},{8,24},{16,0},{24,8},{1,17},{9,25},{17,1},{25,9},{2,18},{10... | collective-permute-start | bytes 786440 | tf_op jit(solution)/shard_map/ppermute | solution.py:18
  41.0 15.2 %collective-permute-start.9 = (f32[1,8,32,256]{3,2,1,0:T(8,128)S(1)}, f32[1,8,32,256]{3,2,1,0:T(8,128)S(1)}, u32[]{:S(2)}, u32[]{:S(2)}) collective-permute-start(f32[1,8,32,256]{3,2,1,0:T(8,128)S(1)} %add_bitcast_fusion.8.refs_1_), channel_id=1, source_target_pairs={{0,4},{4,0},{1,5},{5,1},{2,6},{6,2},{3,7},{7,3},{8,12},{12,8},{9,1... | collective-permute-start | bytes 786440 | tf_op jit(solution)/shard_map/ppermute | solution.py:18
  46.7 9.7 %collective-permute-start.10 = (f32[1,1,8,32,256]{4,3,2,1,0:T(8,128)S(1)}, f32[1,1,8,32,256]{4,3,2,1,0:T(8,128)S(1)}, u32[]{:S(2)}, u32[]{:S(2)}) collective-permute-start(f32[1,1,8,32,256]{4,3,2,1,0:T(8,128)S(1)} %bitcast.191), channel_id=1, source_target_pairs={{0,16},{8,24},{16,0},{24,8},{1,17},{9,25},{17,1},{25,9},{2,18},{10... | collective-permute-start | bytes 786440 | tf_op jit(solution)/shard_map/ppermute | solution.py:18
  49.5 11.4 %collective-permute-start.11 = (f32[1,8,32,256]{3,2,1,0:T(8,128)S(1)}, f32[1,8,32,256]{3,2,1,0:T(8,128)S(1)}, u32[]{:S(2)}, u32[]{:S(2)}) collective-permute-start(f32[1,8,32,256]{3,2,1,0:T(8,128)S(1)} %add_bitcast_fusion.7.refs_2_), channel_id=1, source_target_pairs={{0,4},{4,0},{1,5},{5,1},{2,6},{6,2},{3,7},{7,3},{8,12},{12,8},{9,1... | collective-permute-start | bytes 786440 | tf_op jit(solution)/shard_map/ppermute | solution.py:18
  54.1 9.3 %collective-permute-start.12 = (f32[1,1,8,32,256]{4,3,2,1,0:T(8,128)S(1)}, f32[1,1,8,32,256]{4,3,2,1,0:T(8,128)S(1)}, u32[]{:S(2)}, u32[]{:S(2)}) collective-permute-start(f32[1,1,8,32,256]{4,3,2,1,0:T(8,128)S(1)} %bitcast.192), channel_id=1, source_target_pairs={{0,16},{8,24},{16,0},{24,8},{1,17},{9,25},{17,1},{25,9},{2,18},{10... | collective-permute-start | bytes 786440 | tf_op jit(solution)/shard_map/ppermute | solution.py:18
  55.7 9.3 %collective-permute-start.13 = (f32[1,8,32,256]{3,2,1,0:T(8,128)S(1)}, f32[1,8,32,256]{3,2,1,0:T(8,128)S(1)}, u32[]{:S(2)}, u32[]{:S(2)}) collective-permute-start(f32[1,8,32,256]{3,2,1,0:T(8,128)S(1)} %add_bitcast_fusion.6.refs_0_), channel_id=1, source_target_pairs={{0,4},{4,0},{1,5},{5,1},{2,6},{6,2},{3,7},{7,3},{8,12},{12,8},{9,1... | collective-permute-start | bytes 786440 | tf_op jit(solution)/shard_map/ppermute | solution.py:18
  56.3 15.6 %collective-permute-start.14 = (f32[1,3,8,16,256]{4,3,2,1,0:T(8,128)S(1)}, f32[1,3,8,16,256]{4,3,2,1,0:T(8,128)S(1)}, u32[]{:S(2)}, u32[]{:S(2)}) collective-permute-start(f32[1,3,8,16,256]{4,3,2,1,0:T(8,128)S(1)} %pad_maximum_fusion.3), channel_id=1, source_target_pairs={{0,16},{8,24},{16,0},{24,8},{1,17},{9,25},{17,1},{25,9},{2,18},{10... | collective-permute-start | bytes 1179656 | tf_op jit(solution)/shard_map/ppermute | solution.py:18
  56.5 15.5 %collective-permute-start.15 = (f32[1,8,32,256]{3,2,1,0:T(8,128)S(1)}, f32[1,8,32,256]{3,2,1,0:T(8,128)S(1)}, u32[]{:S(2)}, u32[]{:S(2)}) collective-permute-start(f32[1,8,32,256]{3,2,1,0:T(8,128)S(1)} %add_bitcast_fusion.5.refs_1_), channel_id=1, source_target_pairs={{0,4},{4,0},{1,5},{5,1},{2,6},{6,2},{3,7},{7,3},{8,12},{12,8},{9,1... | collective-permute-start | bytes 786440 | tf_op jit(solution)/shard_map/ppermute | solution.py:18
  61.0 19.3 %collective-permute-start.21 = (f32[1,3,8,16,256]{4,3,2,1,0:T(8,128)S(1)}, f32[1,3,8,16,256]{4,3,2,1,0:T(8,128)S(1)}, u32[]{:S(2)}, u32[]{:S(2)}) collective-permute-start(f32[1,3,8,16,256]{4,3,2,1,0:T(8,128)S(1)} %pad_maximum_fusion.2), channel_id=1, source_target_pairs={{0,16},{8,24},{16,0},{24,8},{1,17},{9,25},{17,1},{25,9},{2,18},{10... | collective-permute-start | bytes 1179656 | tf_op jit(solution)/shard_map/ppermute | solution.py:18
  63.4 12.8 %collective-permute-start.16 = (f32[1,8,32,256]{3,2,1,0:T(8,128)S(1)}, f32[1,8,32,256]{3,2,1,0:T(8,128)S(1)}, u32[]{:S(2)}, u32[]{:S(2)}) collective-permute-start(f32[1,8,32,256]{3,2,1,0:T(8,128)S(1)} %add_bitcast_fusion.4.refs_2_), channel_id=1, source_target_pairs={{0,4},{4,0},{1,5},{5,1},{2,6},{6,2},{3,7},{7,3},{8,12},{12,8},{9,1... | collective-permute-start | bytes 786440 | tf_op jit(solution)/shard_map/ppermute | solution.py:18
  65.0 28.2 %collective-permute-start.32 = (f32[1,3,8,16,256]{4,3,2,1,0:T(8,128)S(1)}, f32[1,3,8,16,256]{4,3,2,1,0:T(8,128)S(1)}, u32[]{:S(2)}, u32[]{:S(2)}) collective-permute-start(f32[1,3,8,16,256]{4,3,2,1,0:T(8,128)S(1)} %pad_maximum_fusion.1), channel_id=1, source_target_pairs={{0,16},{8,24},{16,0},{24,8},{1,17},{9,25},{17,1},{25,9},{2,18},{10... | collective-permute-start | bytes 1179656 | tf_op jit(solution)/shard_map/ppermute | solution.py:18
  71.9 27.4 %collective-permute-start.23 = (f32[3,8,16,256]{3,2,1,0:T(8,128)S(1)}, f32[3,8,16,256]{3,2,1,0:T(8,128)S(1)}, u32[]{:S(2)}, u32[]{:S(2)}) collective-permute-start(f32[3,8,16,256]{3,2,1,0:T(8,128)S(1)} %add_bitcast_fusion.2.refs_3_), channel_id=1, source_target_pairs={{0,4},{4,0},{1,5},{5,1},{2,6},{6,2},{3,7},{7,3},{8,12},{12,8},{9,1... | collective-permute-start | bytes 1179656 | tf_op jit(solution)/shard_map/ppermute | solution.py:18
  72.0 19.7 %collective-permute-start.28 = (f32[1,2,8,16,256]{4,3,2,1,0:T(8,128)S(1)}, f32[1,2,8,16,256]{4,3,2,1,0:T(8,128)S(1)}, u32[]{:S(2)}, u32[]{:S(2)}) collective-permute-start(f32[1,2,8,16,256]{4,3,2,1,0:T(8,128)S(1)} %pad_maximum_fusion.6), channel_id=1, source_target_pairs={{0,16},{8,24},{16,0},{24,8},{1,17},{9,25},{17,1},{25,9},{2,18},{10... | collective-permute-start | bytes 786440 | tf_op jit(solution)/shard_map/ppermute | solution.py:18
  77.2 16.7 %collective-permute-start.17 = (f32[2,4,64,128]{3,2,1,0:T(8,128)S(1)}, f32[2,4,64,128]{3,2,1,0:T(8,128)S(1)}, u32[]{:S(2)}, u32[]{:S(2)}) collective-permute-start(f32[2,4,64,128]{3,2,1,0:T(8,128)S(1)} %dynamic-slice_bitcast_fusion.2), channel_id=1, source_target_pairs={{0,8},{8,0},{16,24},{24,16},{1,9},{9,1},{17,25},{25,17},{2,10},{10... | collective-permute-start | bytes 786440 | tf_op jit(solution)/shard_map/ppermute | solution.py:18
  80.3 21.5 %collective-permute-start.22 = (f32[3,8,16,256]{3,2,1,0:T(8,128)S(1)}, f32[3,8,16,256]{3,2,1,0:T(8,128)S(1)}, u32[]{:S(2)}, u32[]{:S(2)}) collective-permute-start(f32[3,8,16,256]{3,2,1,0:T(8,128)S(1)} %add_bitcast_fusion.1.refs_3_), channel_id=1, source_target_pairs={{0,4},{4,0},{1,5},{5,1},{2,6},{6,2},{3,7},{7,3},{8,12},{12,8},{9,1... | collective-permute-start | bytes 1179656 | tf_op jit(solution)/shard_map/ppermute | solution.py:18
  91.7 5.0 %collective-permute-start.29 = (f32[1,1,8,16,256]{4,3,2,1,0:T(8,128)S(1)}, f32[1,1,8,16,256]{4,3,2,1,0:T(8,128)S(1)}, u32[]{:S(2)}, u32[]{:S(2)}) collective-permute-start(f32[1,1,8,16,256]{4,3,2,1,0:T(8,128)S(1)} %get-tuple-element.122), channel_id=1, source_target_pairs={{0,16},{8,24},{16,0},{24,8},{1,17},{9,25},{17,1},{25,9},{2,18},{10... | collective-permute-start | bytes 393224 | tf_op jit(solution)/shard_map/ppermute | solution.py:18
  93.2 17.7 %collective-permute-start.30 = (f32[2,8,16,256]{3,2,1,0:T(8,128)S(1)}, f32[2,8,16,256]{3,2,1,0:T(8,128)S(1)}, u32[]{:S(2)}, u32[]{:S(2)}) collective-permute-start(f32[2,8,16,256]{3,2,1,0:T(8,128)S(1)} %add_bitcast_fusion.3.refs_4_), channel_id=1, source_target_pairs={{0,4},{4,0},{1,5},{5,1},{2,6},{6,2},{3,7},{7,3},{8,12},{12,8},{9,1... | collective-permute-start | bytes 786440 | tf_op jit(solution)/shard_map/ppermute | solution.py:18
  93.9 14.6 %collective-permute-start.33 = (f32[3,8,16,256]{3,2,1,0:T(8,128)S(1)}, f32[3,8,16,256]{3,2,1,0:T(8,128)S(1)}, u32[]{:S(2)}, u32[]{:S(2)}) collective-permute-start(f32[3,8,16,256]{3,2,1,0:T(8,128)S(1)} %add_bitcast_fusion.refs_4_), channel_id=1, source_target_pairs={{0,4},{4,0},{1,5},{5,1},{2,6},{6,2},{3,7},{7,3},{8,12},{12,8},{9,1... | collective-permute-start | bytes 1179656 | tf_op jit(solution)/shard_map/ppermute | solution.py:18
  96.7 7.3 %collective-permute-start.18 = (f32[2,2,64,128]{3,2,1,0:T(8,128)S(1)}, f32[2,2,64,128]{3,2,1,0:T(8,128)S(1)}, u32[]{:S(2)}, u32[]{:S(2)}) collective-permute-start(f32[2,2,64,128]{3,2,1,0:T(8,128)S(1)} %dynamic-slice_bitcast_fusion.4), channel_id=1, source_target_pairs={{0,2},{1,3},{2,0},{3,1},{4,6},{5,7},{6,4},{7,5},{8,10},{9,11},{10,... | collective-permute-start | bytes 393224 | tf_op jit(solution)/shard_map/ppermute | solution.py:18
  99.3 11.6 %collective-permute-start.31 = (f32[1,8,16,256]{3,2,1,0:T(8,128)S(1)}, f32[1,8,16,256]{3,2,1,0:T(8,128)S(1)}, u32[]{:S(2)}, u32[]{:S(2)}) collective-permute-start(f32[1,8,16,256]{3,2,1,0:T(8,128)S(1)} %add_bitcast_fusion.10.refs_5_), channel_id=1, source_target_pairs={{0,4},{4,0},{1,5},{5,1},{2,6},{6,2},{3,7},{7,3},{8,12},{12,8},{9,1... | collective-permute-start | bytes 393224 | tf_op jit(solution)/shard_map/ppermute | solution.py:18
  105.5 10.8 %collective-permute-start.25 = (f32[2,2,80,128]{3,2,1,0:T(8,128)S(1)}, f32[2,2,80,128]{3,2,1,0:T(8,128)S(1)}, u32[]{:S(2)}, u32[]{:S(2)}) collective-permute-start(f32[2,2,80,128]{3,2,1,0:T(8,128)S(1)} %dynamic-slice_bitcast_fusion.3), channel_id=1, source_target_pairs={{0,2},{1,3},{2,0},{3,1},{4,6},{5,7},{6,4},{7,5},{8,10},{9,11},{10,... | collective-permute-start | bytes 491528 | tf_op jit(solution)/shard_map/ppermute | solution.py:18
  113.4 9.1 %collective-permute-start.34 = (f32[2,4,112,128]{3,2,1,0:T(8,128)S(1)}, f32[2,4,112,128]{3,2,1,0:T(8,128)S(1)}, u32[]{:S(2)}, u32[]{:S(2)}) collective-permute-start(f32[2,4,112,128]{3,2,1,0:T(8,128)S(1)} %dynamic-slice_bitcast_fusion), channel_id=1, source_target_pairs={{0,8},{8,0},{16,24},{24,16},{1,9},{9,1},{17,25},{25,17},{2,10},{10... | collective-permute-start | bytes 1376264 | tf_op jit(solution)/shard_map/ppermute | solution.py:18
  116.3 4.5 %collective-permute-start.26 = (f32[2,1,80,128]{3,2,1,0:T(8,128)S(1)}, f32[2,1,80,128]{3,2,1,0:T(8,128)S(1)}, u32[]{:S(2)}, u32[]{:S(2)}) collective-permute-start(f32[2,1,80,128]{3,2,1,0:T(8,128)S(1)} %constant_dynamic-slice_fusion), channel_id=1, source_target_pairs={{0,1},{1,0},{2,3},{3,2},{4,5},{5,4},{6,7},{7,6},{8,9},{9,8},{10,11... | collective-permute-start | bytes 245768 | tf_op jit(solution)/shard_map/ppermute | solution.py:18
  116.4 10.3 %collective-permute-start.20 = (f32[64,128]{1,0:T(8,128)S(1)}, f32[64,128]{1,0:T(8,128)S(1)}, u32[]{:S(2)}, u32[]{:S(2)}) collective-permute-start(f32[64,128]{1,0:T(8,128)S(1)} %dynamic-slice_bitcast_fusion.6), channel_id=1, source_target_pairs={{0,16},{8,24},{16,0},{24,8},{1,17},{9,25},{17,1},{25,9},{2,18},{10... | collective-permute-start | bytes 98312 | tf_op jit(solution)/shard_map/ppermute | solution.py:18
  120.8 6.1 %collective-permute-start.27 = (f32[80,128]{1,0:T(8,128)S(1)}, f32[80,128]{1,0:T(8,128)S(1)}, u32[]{:S(2)}, u32[]{:S(2)}) collective-permute-start(f32[80,128]{1,0:T(8,128)S(1)} %dynamic-slice_bitcast_fusion.5), channel_id=1, source_target_pairs={{0,16},{8,24},{16,0},{24,8},{1,17},{9,25},{17,1},{25,9},{2,18},{10... | collective-permute-start | bytes 122888 | tf_op jit(solution)/shard_map/ppermute | solution.py:18
  123.3 16.4 %all-to-all-start = ((f32[8,112,128]{2,1,0:T(8,128)}), f32[8,112,128]{2,1,0:T(8,128)S(1)}, u32[]{:S(2)}, u32[]{:S(2)}) async-start(f32[8,112,128]{2,1,0:T(8,128)} %bitcast.97), calls=%async_computation | async-start | bytes 917504 | tf_op jit(solution)/shard_map/all_to_all | solution.py:195
  (5 other events, 14.3 us)

commit v4 on v3

--- a/solution.py
+++ b/solution.py
@@ -8,10 +8,22 @@
 from jax.experimental.pallas import tpu as pltpu
 from jax.sharding import PartitionSpec as P
 
-VMEM_LIMIT = 48 << 20
+VMEM_LIMIT = 44 << 20
+BRIEF = pl.CostEstimate(flops=0, bytes_accessed=0, transcendentals=0)
 LAG = 2
-DEEP = 3
-BRIEF = pl.CostEstimate(flops=0, bytes_accessed=0, transcendentals=0)
+DEEP = 2
+PASS = 5
+AHEAD = 1
+ORDERED = 1
+HALF_SEND = 0
+HALF_TAKE = 0
+HALF_GRAM = 1
+GRAM_LATE = 0
+STRIPS = 3
+FIRST = [1, 1, 1, 1, 1, 1]
+MIDDLE = [3, 3]
+LAST = [1, 2, 2, 1]
+APART = 1
 
 
 def swap(x, axis, bit):
@@ -58,24 +70,38 @@
     )(layers, field)
 
 
-def truncate_kernel(cuts, _, *refs):
+def truncate_kernel(cuts, sizes, _, *refs):
     own, came, own_factor, came_factor = refs[:4]
     layer = jnp.concatenate([own[0], came[0]], axis=0)
     factor = jnp.concatenate([own_factor[...], came_factor[...]], axis=0)
     out = product(split(layer), split(factor), ((0,), (0,)))
     owners = refs[4].shape[1]
     out = out.reshape(owners, -1, out.shape[1])
-    for ref, (low, high) in zip(refs[4:], cuts):
-        ref[0] = out[:, low:high]
-
-
-def truncated(layers, slots, field, came, factors, owners, cuts):
+    first = 0
+    for part, size in enumerate(sizes):
+        outs = refs[4 + part * len(cuts) : 4 + (part + 1) * len(cuts)]
+
+        @pl.when((pl.program_id(0) >= first) & (pl.program_id(0) < first + size))
+        def _():
+            for ref, (low, high) in zip(outs, cuts):
+                ref[0] = out[:, low:high]
+
+        first += size
+
+
+def truncated(sizes, layers, slots, field, came, factors, owners, cuts):
     count = layers.shape[0]
     _, rows, width = field.shape
     ranks = factors[0].shape[1]
-    outs = [(owners, high - low, ranks) for low, high in cuts]
-    return pl.pallas_call(
-        functools.partial(truncate_kernel, cuts),
+    shapes = [(owners, high - low, ranks) for low, high in cuts]
+    out_specs, out_shape = [], []
+    for part, size in enumerate(sizes):
+        first = sum(sizes[:part])
+        place = functools.partial(lambda first, last, i, n: (jnp.clip(i - first, 0, last), 0, 0, 0), first, size - 1)
+        out_specs += [pl.BlockSpec((1, *x), place) for x in shapes]
+        out_shape += [jax.ShapeDtypeStruct((size, *x), jnp.float32) for x in shapes]
+    outs = pl.pallas_call(
+        functools.partial(truncate_kernel, cuts, sizes),
         grid_spec=pltpu.PrefetchScalarGridSpec(
             num_scalar_prefetch=1,
             grid=(count,),
@@ -85,12 +111,13 @@
                 pl.BlockSpec((rows, ranks), lambda i, n: (0, 0)),
                 pl.BlockSpec((rows, ranks), lambda i, n: (0, 0)),
             ],
-            out_specs=[pl.BlockSpec((1, *x), lambda i, n: (i, 0, 0, 0)) for x in outs],
+            out_specs=out_specs,
         ),
-        out_shape=[jax.ShapeDtypeStruct((count, *x), jnp.float32) for x in outs],
+        out_shape=out_shape,
         compiler_params=pltpu.CompilerParams(vmem_limit_bytes=VMEM_LIMIT),
         cost_estimate=BRIEF,
     )(jnp.concatenate([layers, slots]), field, came, *factors)
+    return [outs[part * len(cuts) : (part + 1) * len(cuts)] for part in range(len(sizes))]
 
 
 def gram_kernel(ba, widths, counts, unit, added, me_ref, *refs):
@@ -156,11 +183,9 @@
 
 
 def strips_of(rest):
-    widths = []
-    while rest > 16 and rest % 2 == 0 and len(widths) < 2:
-        rest //= 2
-        widths.append(rest)
-    return widths + [rest]
+    if rest % 32:
+        return [rest]
+    return [rest // 2, rest // 4, rest // 4] if STRIPS == 3 else [rest - rest // 4, rest // 4] if STRIPS == 2 else [rest // 2, rest // 2]
 
 
 def summed_over_core(region):
@@ -211,11 +236,10 @@
     halves = [range(middle), range(middle, each)] if middle else [range(each)]
 
     def groups_of(i):
-        if i == 0:
-            return [range(c, c + 1) for c in range(each)]
-        if i == len(widths) - 1 and len(halves[-1]) > 1:
-            return halves[:-1] + [range(middle, each - 1), range(each - 1, each)]
-        return halves
+        sizes = [1] * each if each != 6 else FIRST if i == 0 else LAST if i == len(widths) - 1 else MIDDLE
+        if each != 6 and i:
+            sizes = [len(x) for x in halves]
+        return [range(sum(sizes[:n]), sum(sizes[: n + 1])) for n in range(len(sizes))]
 
     cuts = [(0, widths[0])] + ([(widths[0], rest)] if len(widths) > 1 else [])
     trips = [range(c, c + 1) for c in range(min(2, each))] + ([range(2, each)] if each > 2 else [])
@@ -235,14 +259,14 @@
     def truncate(c, *after):
         came, slots = came_of[c]
         half = len(keep) // 2
+        parts = [x for x in (range(half), range(half, len(keep))) if x]
         terms[c] = []
-        for part in (range(half), range(half, len(keep))):
-            if part:
-                layers = jnp.stack([(me_a ^ keep[n]) * each + c for n in part])
-                places = jnp.stack([slots[n] for n in part])
-                after = tie(layers, *after), places
-                terms[c].append(truncated(*after, field, came, factors, owners, cuts))
-                after = terms[c][-1][:1]
+        for together in [[x] for x in parts] if c < APART else [parts]:
+            layers = jnp.stack([(me_a ^ keep[n]) * each + c for part in together for n in part])
+            places = jnp.stack([slots[n] for part in together for n in part])
+            sizes = [len(x) for x in together]
+            terms[c] += truncated(sizes, tie(layers, *after), places, field, came, factors, owners, cuts)
+            after = terms[c][-1][:1]
 
     def terms_of(part, group, i):
         cut = min(i, 1)
@@ -260,7 +284,7 @@
         used = [
             [[pieces[d, s, g] for g in groups_of(s) if g[0] in group] for s in range(i + 1)] for d in range(ba)
         ]
-        regions[i] = gram_strip(tie(me_b, *after, *halfway), used, widths[: i + 1], unit, regions[i])
+        regions[i] = gram_strip(tie(me_b, *after, *halfway[:HALF_GRAM]), used, widths[: i + 1], unit, regions[i])
         if group[-1] == each - 1:
             region = regions[i].reshape(aa, col, *regions[i].shape[2:])
             summed = summed_over_core(region)
@@ -270,8 +294,9 @@
     def send(n):
         i, group = steps[n]
         if i == 0:
-            truncate(n, *(terms[n - 1][-1][:1] if n else []), *(arrived[n - DEEP : n - DEEP + 1] if n >= DEEP else []))
-        after = ([arrived[n - DEEP]] if n >= DEEP else []) + (passed[n - DEEP - 2] if n >= DEEP + 2 else [])
+            for c in group:
+                truncate(c, *(terms[c - 1][-1][:1] if c else []), *(arrived[n - DEEP : n - DEEP + 1] if n >= DEEP else []))
+        after = ([arrived[n - DEEP]] if n >= DEEP else []) + (passed[n - PASS] if n >= PASS else []) + halfway[:HALF_SEND]
         leaving_of[n] = terms_of(0, group, i)
         if after:
             leaving_of[n] = tie(leaving_of[n], *after)
@@ -283,7 +308,8 @@
         if ahead < len(steps):
             send(ahead)
         leaving = leaving_of[n]
-        t = tie(terms_of(-1, group, i), leaving_of[min(ahead, len(steps) - 1)])
+        late = min(n + AHEAD, len(steps) - 1, len(leaving_of) - 1)
+        t = tie(terms_of(-1, group, i), leaving_of[late], *arrived[len(arrived) - ORDERED :], *halfway[:HALF_TAKE])
         for bit in bits[1:]:
             t = t + swap(leaving, "aa", bit)
             half = t.shape[0] // 2
@@ -297,7 +323,7 @@
             if group[-1] == part[-1]:
                 waiting.append((n, i, part))
         if waiting and waiting[0][0] <= n - LAG:
-            add_gram(*waiting.pop(0)[1:], leaving_of[min(ahead, len(steps) - 1)])
+            add_gram(*waiting.pop(0)[1:], t if GRAM_LATE else leaving_of[min(ahead, len(steps) - 1)])
     while waiting:
         add_gram(*waiting.pop(0)[1:])
 

time: 142 us -> 137 us (0.965)
  Pallas kernels: 46.8 us -> 39.1 us
  starting transfers between devices: 39.8 us -> 46.7 us
  waiting for transfers between devices: 48.7 us -> 45 us
    pallas_call x12 -> x7, Pallas kernels: 28 us -> 20.4 us  [truncated(): pl.pallas_call(functools.partial(truncate_kernel, cuts, sizes), grid_spec...]
    ppermute x35 -> x37, starting transfers between devices: 36.4 us -> 41.7 us  [swap(): lax.ppermute(x, axis, [(i, i ^ bit) for i in range(lax.axis_size(axis))])]
    ppermute x35 -> x37, waiting for transfers between devices: 36.4 us -> 33 us  [swap(): lax.ppermute(x, axis, [(i, i ^ bit) for i in range(lax.axis_size(axis))])]
    all_to_all x1, starting transfers between devices: 3.47 us -> 5.04 us  [block_by_all_to_all(): lax.all_to_all(t, ('aa', 'col'), 0, 0, tiled=True, axis_index_groups=groups)]
  transfers between devices with their start and end apart: 36 -> 38, of which waited for: 15 -> 12; matrix products, arithmetic and copies ran while one was open for 2% -> 3% of each run, Pallas kernels for 25% -> 27%
where the time goes in v4:
time: 137 us
  starting transfers between devices  46.7 us (34%)
  waiting for transfers between devices  45 us (33%)
  Pallas kernels  39.1 us (29%)
  other arithmetic  2.83 us (2%)
  local copies, waits for them, and re-layouts  2.28 us (2%)
    ppermute x37, starting transfers between devices, swap(): lax.ppermute(x, axis, [(i, i ^ bit) for i in range(lax.axis_size(axis))])  41.7 us
    ppermute x37, waiting for transfers between devices, swap(): lax.ppermute(x, axis, [(i, i ^ bit) for i in range(lax.axis_size(axis))])  33 us
    pallas_call x7, Pallas kernels, truncated(): pl.pallas_call(functools.partial(truncate_kernel, cuts, sizes), grid_spec...  20.4 us
    all_to_all x1, waiting for transfers between devices, block_by_all_to_all(): lax.all_to_all(t, ('aa', 'col'), 0, 0, tiled=True, axis_index_groups=groups)  12.1 us
    pallas_call x6, Pallas kernels, gram_strip(): pl.pallas_call(functools.partial(gram_kernel, ba, widths, counts, unit, l...  10 us
    pallas_call x3, Pallas kernels, gathered(): pl.pallas_call(gather_kernel, in_specs=[pl.BlockSpec(memory_space=pltpu.S...  8.65 us
    all_to_all x1, starting transfers between devices, block_by_all_to_all(): lax.all_to_all(t, ('aa', 'col'), 0, 0, tiled=True, axis_index_groups=groups)  5.04 us
  transfers between devices with their start and end apart: 38, of which 12 were waited for; matrix products, arithmetic and copies ran while one was open for 3% of the time, Pallas kernels for 27%

profile of v4, /device:TPU:0, one launch (start us, length us, event | category | flops | bytes accessed | tf_op | source)
XLA Modules:
  0.0 136.8 jit_solution(9754741079611719736)
XLA Ops:
  0.1 2.6 %shard_map.28 = f32[2,256,512]{2,1,0:T(8,128)} custom-call(s32[2]{0:T(128)S(1)} %pad_add_fusion.1.layers_ref, f32[24,256,512]{2,1,0:T(8,128)} %refs_0_.13), custom_call_target="tpu_custom_call" | custom-call | tf_op jit(solution)/shard_map/pallas_call | solution.py:62
  3.3 2.5 %collective-permute-done.1.refs_3_ = f32[256,256]{1,0:T(8,128)S(1)} collective-permute-done((f32[256,256]{1,0:T(8,128)S(1)}, f32[256,256]{1,0:T(8,128)S(1)}, u32[]{:S(2)}, u32[]{:S(2)}) %collective-permute-start.1) | collective-permute-done | bytes 262176 | tf_op jit(solution)/shard_map/ppermute | solution.py:30
  7.8 4.2 %shard_map.33 = f32[8,256,512]{2,1,0:T(8,128)} custom-call(s32[8]{0:T(128)S(1)} %stack.154.layers_ref, f32[24,256,512]{2,1,0:T(8,128)} %refs_0_.13), custom_call_target="tpu_custom_call" | custom-call | tf_op jit(solution)/shard_map/pallas_call | solution.py:62
  13.0 2.2 %shard_map.29 = (f32[1,8,32,256]{3,2,1,0:T(8,128)S(1)}, f32[1,8,32,256]{3,2,1,0:T(8,128)S(1)}) custom-call(s32[2]{0:T(128)S(1)} %get-tuple-element.155._, f32[24,256,512]{2,1,0:T(8,128)} %refs_0_.13, f32[2,256,512]{2,1,0:T(8,128)S(1)} %collective-permute-done.refs_1_, f32[256,256]{1,0:T(8,128)S(1)} %copy-done, f32[256,256]{1,0:T(8,128)S(1)} %collective-permute-done.1.refs_3_), custom_call_target="tpu_custom_call" | custom-call | tf_op jit(solution)/shard_map/pallas_call | solution.py:103
  15.3 2.2 %shard_map.30 = (f32[1,8,32,256]{3,2,1,0:T(8,128)S(1)}, f32[1,8,32,256]{3,2,1,0:T(8,128)S(1)}) custom-call(s32[2]{0:T(128)S(1)} %pad_add_fusion.2._, f32[24,256,512]{2,1,0:T(8,128)} %refs_0_.13, f32[2,256,512]{2,1,0:T(8,128)S(1)} %collective-permute-done.refs_1_, f32[256,256]{1,0:T(8,128)S(1)} %copy-done, f32[256,256]{1,0:T(8,128)S(1)} %collective-permute-done.1.refs_3_), custom_call_target="tpu_custom_call" | custom-call | tf_op jit(solution)/shard_map/pallas_call | solution.py:103
  17.5 2.8 %collective-permute-start.3 = (f32[1,1,8,32,256]{4,3,2,1,0:T(8,128)S(1)}, f32[1,1,8,32,256]{4,3,2,1,0:T(8,128)S(1)}, u32[]{:S(2)}, u32[]{:S(2)}) collective-permute-start(f32[1,1,8,32,256]{4,3,2,1,0:T(8,128)S(1)} %bitcast.196), channel_id=1, source_target_pairs={{0,16},{8,24},{16,0},{24,8},{1,17},{9,25},{17,1},{25,9},{2,18},{10... | collective-permute-start | bytes 786440 | tf_op jit(solution)/shard_map/ppermute | solution.py:30
  20.4 3.2 %shard_map.32 = (f32[1,8,32,256]{3,2,1,0:T(8,128)S(1)}, f32[1,8,32,256]{3,2,1,0:T(8,128)S(1)}, f32[1,8,32,256]{3,2,1,0:T(8,128)S(1)}, f32[1,8,32,256]{3,2,1,0:T(8,128)S(1)}) custom-call(s32[4]{0:T(128)S(1)} %pad_add_fusion.4._, f32[24,256,512]{2,1,0:T(8,128)} %refs_0_.13, f32[2,256,512]{2,1,0:T(8,128)} %collective-permute-done.2.refs_1_, ...), custom_call_target="tpu_custom_call" | custom-call | tf_op jit(solution)/shard_map/pallas_call | solution.py:103
  23.6 2.0 %collective-permute-start.5 = (f32[1,1,8,32,256]{4,3,2,1,0:T(8,128)S(1)}, f32[1,1,8,32,256]{4,3,2,1,0:T(8,128)S(1)}, u32[]{:S(2)}, u32[]{:S(2)}) collective-permute-start(f32[1,1,8,32,256]{4,3,2,1,0:T(8,128)S(1)} %bitcast.195), channel_id=1, source_target_pairs={{0,16},{8,24},{16,0},{24,8},{1,17},{9,25},{17,1},{25,9},{2,18},{10... | collective-permute-start | bytes 786440 | tf_op jit(solution)/shard_map/ppermute | solution.py:30
  27.2 1.8 %collective-permute-start.8 = (f32[1,8,32,256]{3,2,1,0:T(8,128)S(1)}, f32[1,8,32,256]{3,2,1,0:T(8,128)S(1)}, u32[]{:S(2)}, u32[]{:S(2)}) collective-permute-start(f32[1,8,32,256]{3,2,1,0:T(8,128)S(1)} %add_bitcast_fusion.9.refs_0_), channel_id=1, source_target_pairs={{0,4},{4,0},{1,5},{5,1},{2,6},{6,2},{3,7},{7,3},{8,12},{12,8},{9,1... | collective-permute-start | bytes 786440 | tf_op jit(solution)/shard_map/ppermute | solution.py:30
  29.1 3.2 %shard_map.34 = (f32[1,8,32,256]{3,2,1,0:T(8,128)S(1)}, f32[1,8,32,256]{3,2,1,0:T(8,128)S(1)}, f32[1,8,32,256]{3,2,1,0:T(8,128)S(1)}, f32[1,8,32,256]{3,2,1,0:T(8,128)S(1)}) custom-call(s32[4]{0:T(128)S(1)} %pad_add_fusion.7._, f32[24,256,512]{2,1,0:T(8,128)} %refs_0_.13, f32[8,256,512]{2,1,0:T(8,128)} %collective-permute-done.4.refs_1_, ...), custom_call_target="tpu_custom_call" | custom-call | tf_op jit(solution)/shard_map/pallas_call | solution.py:103
  34.6 3.2 %shard_map.35 = (f32[1,8,32,256]{3,2,1,0:T(8,128)S(1)}, f32[1,8,32,256]{3,2,1,0:T(8,128)S(1)}, f32[1,8,32,256]{3,2,1,0:T(8,128)S(1)}, f32[1,8,32,256]{3,2,1,0:T(8,128)S(1)}) custom-call(s32[4]{0:T(128)S(1)} %pad_add_fusion.9._, f32[24,256,512]{2,1,0:T(8,128)} %refs_0_.13, f32[8,256,512]{2,1,0:T(8,128)} %collective-permute-done.4.refs_1_, ...), custom_call_target="tpu_custom_call" | custom-call | tf_op jit(solution)/shard_map/pallas_call | solution.py:103
  40.4 3.2 %shard_map.36 = (f32[1,8,32,256]{3,2,1,0:T(8,128)S(1)}, f32[1,8,32,256]{3,2,1,0:T(8,128)S(1)}, f32[1,8,32,256]{3,2,1,0:T(8,128)S(1)}, f32[1,8,32,256]{3,2,1,0:T(8,128)S(1)}) custom-call(s32[4]{0:T(128)S(1)} %pad_add_fusion.11._, f32[24,256,512]{2,1,0:T(8,128)} %refs_0_.13, f32[8,256,512]{2,1,0:T(8,128)} %collective-permute-done.4.refs_1_, ...), custom_call_target="tpu_custom_call" | custom-call | tf_op jit(solution)/shard_map/pallas_call | solution.py:103
  46.7 3.3 %shard_map.37 = (f32[1,8,32,256]{3,2,1,0:T(8,128)S(1)}, f32[1,8,32,256]{3,2,1,0:T(8,128)S(1)}, f32[1,8,32,256]{3,2,1,0:T(8,128)S(1)}, f32[1,8,32,256]{3,2,1,0:T(8,128)S(1)}) custom-call(s32[4]{0:T(128)S(1)} %pad_add_fusion.13._, f32[24,256,512]{2,1,0:T(8,128)} %refs_0_.13, f32[8,256,512]{2,1,0:T(8,128)} %collective-permute-done.4.refs_1_, ...), custom_call_target="tpu_custom_call" | custom-call | tf_op jit(solution)/shard_map/pallas_call | solution.py:103
  50.1 1.9 %collective-permute-start.11 = (f32[1,1,8,32,256]{4,3,2,1,0:T(8,128)S(1)}, f32[1,1,8,32,256]{4,3,2,1,0:T(8,128)S(1)}, u32[]{:S(2)}, u32[]{:S(2)}) collective-permute-start(f32[1,1,8,32,256]{4,3,2,1,0:T(8,128)S(1)} %bitcast.194), channel_id=1, source_target_pairs={{0,16},{8,24},{16,0},{24,8},{1,17},{9,25},{17,1},{25,9},{2,18},{10... | collective-permute-start | bytes 786440 | tf_op jit(solution)/shard_map/ppermute | solution.py:30
  53.3 6.2 %collective-permute-done.11 = f32[1,1,8,32,256]{4,3,2,1,0:T(8,128)S(1)} collective-permute-done((f32[1,1,8,32,256]{4,3,2,1,0:T(8,128)S(1)}, f32[1,1,8,32,256]{4,3,2,1,0:T(8,128)S(1)}, u32[]{:S(2)}, u32[]{:S(2)}) %collective-permute-start.11) | collective-permute-done | bytes 262176 | tf_op jit(solution)/shard_map/ppermute | solution.py:30
  59.5 1.9 %collective-permute-start.21 = (f32[1,3,8,16,256]{4,3,2,1,0:T(8,128)S(1)}, f32[1,3,8,16,256]{4,3,2,1,0:T(8,128)S(1)}, u32[]{:S(2)}, u32[]{:S(2)}) collective-permute-start(f32[1,3,8,16,256]{4,3,2,1,0:T(8,128)S(1)} %pad_maximum_fusion.1), channel_id=1, source_target_pairs={{0,16},{8,24},{16,0},{24,8},{1,17},{9,25},{17,1},{25,9},{2,18},{10... | collective-permute-start | bytes 1179656 | tf_op jit(solution)/shard_map/ppermute | solution.py:30
  61.5 2.1 %collective-permute-start.15 = (f32[1,8,32,256]{3,2,1,0:T(8,128)S(1)}, f32[1,8,32,256]{3,2,1,0:T(8,128)S(1)}, u32[]{:S(2)}, u32[]{:S(2)}) collective-permute-start(f32[1,8,32,256]{3,2,1,0:T(8,128)S(1)} %add_bitcast_fusion.5.refs_1_), channel_id=1, source_target_pairs={{0,4},{4,0},{1,5},{5,1},{2,6},{6,2},{3,7},{7,3},{8,12},{12,8},{9,1... | collective-permute-start | bytes 786440 | tf_op jit(solution)/shard_map/ppermute | solution.py:30
  64.5 3.4 %collective-permute-done.13 = f32[1,3,8,16,256]{4,3,2,1,0:T(8,128)S(1)} collective-permute-done((f32[1,3,8,16,256]{4,3,2,1,0:T(8,128)S(1)}, f32[1,3,8,16,256]{4,3,2,1,0:T(8,128)S(1)}, u32[]{:S(2)}, u32[]{:S(2)}) %collective-permute-start.13) | collective-permute-done | bytes 393248 | tf_op jit(solution)/shard_map/ppermute | solution.py:30
  67.9 1.9 %collective-permute-start.24 = (f32[3,8,16,256]{3,2,1,0:T(8,128)S(1)}, f32[3,8,16,256]{3,2,1,0:T(8,128)S(1)}, u32[]{:S(2)}, u32[]{:S(2)}) collective-permute-start(f32[3,8,16,256]{3,2,1,0:T(8,128)S(1)} %add_bitcast_fusion.1.refs_3_), channel_id=1, source_target_pairs={{0,4},{4,0},{1,5},{5,1},{2,6},{6,2},{3,7},{7,3},{8,12},{12,8},{9,1... | collective-permute-start | bytes 1179656 | tf_op jit(solution)/shard_map/ppermute | solution.py:30
  69.9 2.0 %collective-permute-start.22 = (f32[1,1,8,16,256]{4,3,2,1,0:T(8,128)S(1)}, f32[1,1,8,16,256]{4,3,2,1,0:T(8,128)S(1)}, u32[]{:S(2)}, u32[]{:S(2)}) collective-permute-start(f32[1,1,8,16,256]{4,3,2,1,0:T(8,128)S(1)} %get-tuple-element.109), channel_id=1, source_target_pairs={{0,16},{8,24},{16,0},{24,8},{1,17},{9,25},{17,1},{25,9},{2,18},{10... | collective-permute-start | bytes 393224 | tf_op jit(solution)/shard_map/ppermute | solution.py:30
  71.9 4.3 %collective-permute-done.21 = f32[1,3,8,16,256]{4,3,2,1,0:T(8,128)S(1)} collective-permute-done((f32[1,3,8,16,256]{4,3,2,1,0:T(8,128)S(1)}, f32[1,3,8,16,256]{4,3,2,1,0:T(8,128)S(1)}, u32[]{:S(2)}, u32[]{:S(2)}) %collective-permute-start.21) | collective-permute-done | bytes 393248 | tf_op jit(solution)/shard_map/ppermute | solution.py:30
  80.8 3.4 %collective-permute-done.29 = f32[1,2,8,16,256]{4,3,2,1,0:T(8,128)S(1)} collective-permute-done((f32[1,2,8,16,256]{4,3,2,1,0:T(8,128)S(1)}, f32[1,2,8,16,256]{4,3,2,1,0:T(8,128)S(1)}, u32[]{:S(2)}, u32[]{:S(2)}) %collective-permute-start.29) | collective-permute-done | bytes 262176 | tf_op jit(solution)/shard_map/ppermute | solution.py:30
  86.4 2.6 %collective-permute-start.18 = (f32[2,2,64,128]{3,2,1,0:T(8,128)S(1)}, f32[2,2,64,128]{3,2,1,0:T(8,128)S(1)}, u32[]{:S(2)}, u32[]{:S(2)}) collective-permute-start(f32[2,2,64,128]{3,2,1,0:T(8,128)S(1)} %dynamic-slice_bitcast_fusion.4), channel_id=1, source_target_pairs={{0,2},{1,3},{2,0},{3,1},{4,6},{5,7},{6,4},{7,5},{8,10},{9,11},{10,... | collective-permute-start | bytes 393224 | tf_op jit(solution)/shard_map/ppermute | solution.py:30
  89.0 2.5 %collective-permute-start.31 = (f32[1,1,8,16,256]{4,3,2,1,0:T(8,128)S(1)}, f32[1,1,8,16,256]{4,3,2,1,0:T(8,128)S(1)}, u32[]{:S(2)}, u32[]{:S(2)}) collective-permute-start(f32[1,1,8,16,256]{4,3,2,1,0:T(8,128)S(1)} %get-tuple-element.123), channel_id=1, source_target_pairs={{0,16},{8,24},{16,0},{24,8},{1,17},{9,25},{17,1},{25,9},{2,18},{10... | collective-permute-start | bytes 393224 | tf_op jit(solution)/shard_map/ppermute | solution.py:30
  93.3 1.9 %collective-permute-start.32 = (f32[2,8,16,256]{3,2,1,0:T(8,128)S(1)}, f32[2,8,16,256]{3,2,1,0:T(8,128)S(1)}, u32[]{:S(2)}, u32[]{:S(2)}) collective-permute-start(f32[2,8,16,256]{3,2,1,0:T(8,128)S(1)} %add_bitcast_fusion.2.refs_4_), channel_id=1, source_target_pairs={{0,4},{4,0},{1,5},{5,1},{2,6},{6,2},{3,7},{7,3},{8,12},{12,8},{9,1... | collective-permute-start | bytes 786440 | tf_op jit(solution)/shard_map/ppermute | solution.py:30
  99.2 2.5 %collective-permute-done.19 = f32[2,1,64,128]{3,2,1,0:T(8,128)S(1)} collective-permute-done((f32[2,1,64,128]{3,2,1,0:T(8,128)S(1)}, f32[2,1,64,128]{3,2,1,0:T(8,128)S(1)}, u32[]{:S(2)}, u32[]{:S(2)}) %collective-permute-start.19) | collective-permute-done | bytes 65568 | tf_op jit(solution)/shard_map/ppermute | solution.py:30
  103.2 2.4 %shard_map.42.refs_12_ = f32[2,8,112,128]{3,2,1,0:T(8,128)S(1)} custom-call(s32[1]{0:T(128)} %bitcast.95.me_ref, f32[1,8,32,256]{3,2,1,0:T(8,128)S(1)} %add_bitcast_fusion.9.refs_0_, f32[1,8,32,256]{3,2,1,0:T(8,128)S(1)} %add_bitcast_fusion.8.refs_1_, f32[1,8,32,256]{3,2,1,0:T(8,128)S(1)} %add_bitcast_fusion.7.refs_2_, ...), custom_call_target="tpu_custom_call" | custom-call | tf_op jit(solution)/shard_map/pallas_call | solution.py:167
  105.5 2.4 %shard_map.43 = f32[2,8,112,128]{3,2,1,0:T(8,128)S(1)} custom-call(s32[1]{0:T(128)} %bitcast.91.me_ref, f32[1,8,32,256]{3,2,1,0:T(8,128)S(1)} %add_bitcast_fusion.6.refs_0_, f32[1,8,32,256]{3,2,1,0:T(8,128)S(1)} %add_bitcast_fusion.5.refs_1_, f32[1,8,32,256]{3,2,1,0:T(8,128)S(1)} %add_bitcast_fusion.4.refs_2_, ...), custom_call_target="tpu_custom_call", output_to_operand_aliasing={{}: (13, {})} | custom-call | tf_op jit(solution)/shard_map/pallas_call | solution.py:167
  108.1 3.8 %collective-permute-done.26 = f32[2,2,80,128]{3,2,1,0:T(8,128)S(1)} collective-permute-done((f32[2,2,80,128]{3,2,1,0:T(8,128)S(1)}, f32[2,2,80,128]{3,2,1,0:T(8,128)S(1)}, u32[]{:S(2)}, u32[]{:S(2)}) %collective-permute-start.26) | collective-permute-done | bytes 163872 | tf_op jit(solution)/shard_map/ppermute | solution.py:30
  112.1 4.3 %collective-permute-done.27 = f32[2,1,80,128]{3,2,1,0:T(8,128)S(1)} collective-permute-done((f32[2,1,80,128]{3,2,1,0:T(8,128)S(1)}, f32[2,1,80,128]{3,2,1,0:T(8,128)S(1)}, u32[]{:S(2)}, u32[]{:S(2)}) %collective-permute-start.27) | collective-permute-done | bytes 81952 | tf_op jit(solution)/shard_map/ppermute | solution.py:30
  117.4 5.0 %all-to-all-start = ((f32[8,112,128]{2,1,0:T(8,128)}), f32[8,112,128]{2,1,0:T(8,128)S(1)}, u32[]{:S(2)}, u32[]{:S(2)}) async-start(f32[8,112,128]{2,1,0:T(8,128)} %bitcast.99), calls=%async_computation | async-start | bytes 917504 | tf_op jit(solution)/shard_map/all_to_all | solution.py:220
  123.1 12.1 %all-to-all-done = f32[8,112,128]{2,1,0:T(8,128)S(1)} async-done(((f32[8,112,128]{2,1,0:T(8,128)}), f32[8,112,128]{2,1,0:T(8,128)S(1)}, u32[]{:S(2)}, u32[]{:S(2)}) %all-to-all-start) | async-done | bytes 458784 | tf_op jit(solution)/shard_map/all_to_all | solution.py:220
  (147 shorter events, 33.0 us)
Async XLA Ops:
  2.7 9.3 %collective-permute-start = (f32[2,256,512]{2,1,0:T(8,128)}, f32[2,256,512]{2,1,0:T(8,128)S(1)}, u32[]{:S(2)}, u32[]{:S(2)}) collective-permute-start(f32[2,256,512]{2,1,0:T(8,128)} %shard_map.28), channel_id=1, source_target_pairs={{0,8},{8,0},{16,24},{24,16},{1,9},{9,1},{17,25},{25,17},{2,10},{10... | collective-permute-start | bytes 3145736 | tf_op jit(solution)/shard_map/ppermute | solution.py:30
  12.0 17.1 %collective-permute-start.4 = (f32[8,256,512]{2,1,0:T(8,128)}, f32[8,256,512]{2,1,0:T(8,128)}, u32[]{:S(2)}, u32[]{:S(2)}) collective-permute-start(f32[8,256,512]{2,1,0:T(8,128)} %shard_map.33), channel_id=1, source_target_pairs={{0,8},{8,0},{16,24},{24,16},{1,9},{9,1},{17,25},{25,17},{2,10},{10... | collective-permute-start | bytes 12582920 | tf_op jit(solution)/shard_map/ppermute | solution.py:30
  12.4 8.0 %collective-permute-start.2 = (f32[2,256,512]{2,1,0:T(8,128)S(1)}, f32[2,256,512]{2,1,0:T(8,128)}, u32[]{:S(2)}, u32[]{:S(2)}) collective-permute-start(f32[2,256,512]{2,1,0:T(8,128)S(1)} %shard_map.31), channel_id=1, source_target_pairs={{0,8},{8,0},{16,24},{24,16},{1,9},{9,1},{17,25},{25,17},{2,10},{10... | collective-permute-start | bytes 3145736 | tf_op jit(solution)/shard_map/ppermute | solution.py:30
  17.5 9.6 %collective-permute-start.3 = (f32[1,1,8,32,256]{4,3,2,1,0:T(8,128)S(1)}, f32[1,1,8,32,256]{4,3,2,1,0:T(8,128)S(1)}, u32[]{:S(2)}, u32[]{:S(2)}) collective-permute-start(f32[1,1,8,32,256]{4,3,2,1,0:T(8,128)S(1)} %bitcast.196), channel_id=1, source_target_pairs={{0,16},{8,24},{16,0},{24,8},{1,17},{9,25},{17,1},{25,9},{2,18},{10... | collective-permute-start | bytes 786440 | tf_op jit(solution)/shard_map/ppermute | solution.py:30
  23.6 10.3 %collective-permute-start.5 = (f32[1,1,8,32,256]{4,3,2,1,0:T(8,128)S(1)}, f32[1,1,8,32,256]{4,3,2,1,0:T(8,128)S(1)}, u32[]{:S(2)}, u32[]{:S(2)}) collective-permute-start(f32[1,1,8,32,256]{4,3,2,1,0:T(8,128)S(1)} %bitcast.195), channel_id=1, source_target_pairs={{0,16},{8,24},{16,0},{24,8},{1,17},{9,25},{17,1},{25,9},{2,18},{10... | collective-permute-start | bytes 786440 | tf_op jit(solution)/shard_map/ppermute | solution.py:30
  27.2 23.0 %collective-permute-start.8 = (f32[1,8,32,256]{3,2,1,0:T(8,128)S(1)}, f32[1,8,32,256]{3,2,1,0:T(8,128)S(1)}, u32[]{:S(2)}, u32[]{:S(2)}) collective-permute-start(f32[1,8,32,256]{3,2,1,0:T(8,128)S(1)} %add_bitcast_fusion.9.refs_0_), channel_id=1, source_target_pairs={{0,4},{4,0},{1,5},{5,1},{2,6},{6,2},{3,7},{7,3},{8,12},{12,8},{9,1... | collective-permute-start | bytes 786440 | tf_op jit(solution)/shard_map/ppermute | solution.py:30
  32.3 7.3 %collective-permute-start.6 = (f32[1,1,8,32,256]{4,3,2,1,0:T(8,128)S(1)}, f32[1,1,8,32,256]{4,3,2,1,0:T(8,128)S(1)}, u32[]{:S(2)}, u32[]{:S(2)}) collective-permute-start(f32[1,1,8,32,256]{4,3,2,1,0:T(8,128)S(1)} %bitcast.191), channel_id=1, source_target_pairs={{0,16},{8,24},{16,0},{24,8},{1,17},{9,25},{17,1},{25,9},{2,18},{10... | collective-permute-start | bytes 786440 | tf_op jit(solution)/shard_map/ppermute | solution.py:30
  33.9 18.3 %collective-permute-start.10 = (f32[1,8,32,256]{3,2,1,0:T(8,128)S(1)}, f32[1,8,32,256]{3,2,1,0:T(8,128)S(1)}, u32[]{:S(2)}, u32[]{:S(2)}) collective-permute-start(f32[1,8,32,256]{3,2,1,0:T(8,128)S(1)} %add_bitcast_fusion.8.refs_1_), channel_id=1, source_target_pairs={{0,4},{4,0},{1,5},{5,1},{2,6},{6,2},{3,7},{7,3},{8,12},{12,8},{9,1... | collective-permute-start | bytes 786440 | tf_op jit(solution)/shard_map/ppermute | solution.py:30
  37.8 8.2 %collective-permute-start.7 = (f32[1,1,8,32,256]{4,3,2,1,0:T(8,128)S(1)}, f32[1,1,8,32,256]{4,3,2,1,0:T(8,128)S(1)}, u32[]{:S(2)}, u32[]{:S(2)}) collective-permute-start(f32[1,1,8,32,256]{4,3,2,1,0:T(8,128)S(1)} %bitcast.192), channel_id=1, source_target_pairs={{0,16},{8,24},{16,0},{24,8},{1,17},{9,25},{17,1},{25,9},{2,18},{10... | collective-permute-start | bytes 786440 | tf_op jit(solution)/shard_map/ppermute | solution.py:30
  39.7 19.8 %collective-permute-start.12 = (f32[1,8,32,256]{3,2,1,0:T(8,128)S(1)}, f32[1,8,32,256]{3,2,1,0:T(8,128)S(1)}, u32[]{:S(2)}, u32[]{:S(2)}) collective-permute-start(f32[1,8,32,256]{3,2,1,0:T(8,128)S(1)} %add_bitcast_fusion.7.refs_2_), channel_id=1, source_target_pairs={{0,4},{4,0},{1,5},{5,1},{2,6},{6,2},{3,7},{7,3},{8,12},{12,8},{9,1... | collective-permute-start | bytes 786440 | tf_op jit(solution)/shard_map/ppermute | solution.py:30
  43.5 8.7 %collective-permute-start.9 = (f32[1,1,8,32,256]{4,3,2,1,0:T(8,128)S(1)}, f32[1,1,8,32,256]{4,3,2,1,0:T(8,128)S(1)}, u32[]{:S(2)}, u32[]{:S(2)}) collective-permute-start(f32[1,1,8,32,256]{4,3,2,1,0:T(8,128)S(1)} %bitcast.193), channel_id=1, source_target_pairs={{0,16},{8,24},{16,0},{24,8},{1,17},{9,25},{17,1},{25,9},{2,18},{10... | collective-permute-start | bytes 786440 | tf_op jit(solution)/shard_map/ppermute | solution.py:30
  46.0 23.8 %collective-permute-start.14 = (f32[1,8,32,256]{3,2,1,0:T(8,128)S(1)}, f32[1,8,32,256]{3,2,1,0:T(8,128)S(1)}, u32[]{:S(2)}, u32[]{:S(2)}) collective-permute-start(f32[1,8,32,256]{3,2,1,0:T(8,128)S(1)} %add_bitcast_fusion.6.refs_0_), channel_id=1, source_target_pairs={{0,4},{4,0},{1,5},{5,1},{2,6},{6,2},{3,7},{7,3},{8,12},{12,8},{9,1... | collective-permute-start | bytes 786440 | tf_op jit(solution)/shard_map/ppermute | solution.py:30
  50.1 9.3 %collective-permute-start.11 = (f32[1,1,8,32,256]{4,3,2,1,0:T(8,128)S(1)}, f32[1,1,8,32,256]{4,3,2,1,0:T(8,128)S(1)}, u32[]{:S(2)}, u32[]{:S(2)}) collective-permute-start(f32[1,1,8,32,256]{4,3,2,1,0:T(8,128)S(1)} %bitcast.194), channel_id=1, source_target_pairs={{0,16},{8,24},{16,0},{24,8},{1,17},{9,25},{17,1},{25,9},{2,18},{10... | collective-permute-start | bytes 786440 | tf_op jit(solution)/shard_map/ppermute | solution.py:30
  52.3 15.6 %collective-permute-start.13 = (f32[1,3,8,16,256]{4,3,2,1,0:T(8,128)S(1)}, f32[1,3,8,16,256]{4,3,2,1,0:T(8,128)S(1)}, u32[]{:S(2)}, u32[]{:S(2)}) collective-permute-start(f32[1,3,8,16,256]{4,3,2,1,0:T(8,128)S(1)} %pad_maximum_fusion.2), channel_id=1, source_target_pairs={{0,16},{8,24},{16,0},{24,8},{1,17},{9,25},{17,1},{25,9},{2,18},{10... | collective-permute-start | bytes 1179656 | tf_op jit(solution)/shard_map/ppermute | solution.py:30
  59.5 16.6 %collective-permute-start.21 = (f32[1,3,8,16,256]{4,3,2,1,0:T(8,128)S(1)}, f32[1,3,8,16,256]{4,3,2,1,0:T(8,128)S(1)}, u32[]{:S(2)}, u32[]{:S(2)}) collective-permute-start(f32[1,3,8,16,256]{4,3,2,1,0:T(8,128)S(1)} %pad_maximum_fusion.1), channel_id=1, source_target_pairs={{0,16},{8,24},{16,0},{24,8},{1,17},{9,25},{17,1},{25,9},{2,18},{10... | collective-permute-start | bytes 1179656 | tf_op jit(solution)/shard_map/ppermute | solution.py:30
  61.5 15.0 %collective-permute-start.15 = (f32[1,8,32,256]{3,2,1,0:T(8,128)S(1)}, f32[1,8,32,256]{3,2,1,0:T(8,128)S(1)}, u32[]{:S(2)}, u32[]{:S(2)}) collective-permute-start(f32[1,8,32,256]{3,2,1,0:T(8,128)S(1)} %add_bitcast_fusion.5.refs_1_), channel_id=1, source_target_pairs={{0,4},{4,0},{1,5},{5,1},{2,6},{6,2},{3,7},{7,3},{8,12},{12,8},{9,1... | collective-permute-start | bytes 786440 | tf_op jit(solution)/shard_map/ppermute | solution.py:30
  63.5 14.8 %collective-permute-start.16 = (f32[1,8,32,256]{3,2,1,0:T(8,128)S(1)}, f32[1,8,32,256]{3,2,1,0:T(8,128)S(1)}, u32[]{:S(2)}, u32[]{:S(2)}) collective-permute-start(f32[1,8,32,256]{3,2,1,0:T(8,128)S(1)} %add_bitcast_fusion.4.refs_2_), channel_id=1, source_target_pairs={{0,4},{4,0},{1,5},{5,1},{2,6},{6,2},{3,7},{7,3},{8,12},{12,8},{9,1... | collective-permute-start | bytes 786440 | tf_op jit(solution)/shard_map/ppermute | solution.py:30
  67.9 18.4 %collective-permute-start.24 = (f32[3,8,16,256]{3,2,1,0:T(8,128)S(1)}, f32[3,8,16,256]{3,2,1,0:T(8,128)S(1)}, u32[]{:S(2)}, u32[]{:S(2)}) collective-permute-start(f32[3,8,16,256]{3,2,1,0:T(8,128)S(1)} %add_bitcast_fusion.1.refs_3_), channel_id=1, source_target_pairs={{0,4},{4,0},{1,5},{5,1},{2,6},{6,2},{3,7},{7,3},{8,12},{12,8},{9,1... | collective-permute-start | bytes 1179656 | tf_op jit(solution)/shard_map/ppermute | solution.py:30
  69.9 9.5 %collective-permute-start.22 = (f32[1,1,8,16,256]{4,3,2,1,0:T(8,128)S(1)}, f32[1,1,8,16,256]{4,3,2,1,0:T(8,128)S(1)}, u32[]{:S(2)}, u32[]{:S(2)}) collective-permute-start(f32[1,1,8,16,256]{4,3,2,1,0:T(8,128)S(1)} %get-tuple-element.109), channel_id=1, source_target_pairs={{0,16},{8,24},{16,0},{24,8},{1,17},{9,25},{17,1},{25,9},{2,18},{10... | collective-permute-start | bytes 393224 | tf_op jit(solution)/shard_map/ppermute | solution.py:30
  76.2 17.1 %collective-permute-start.23 = (f32[3,8,16,256]{3,2,1,0:T(8,128)S(1)}, f32[3,8,16,256]{3,2,1,0:T(8,128)S(1)}, u32[]{:S(2)}, u32[]{:S(2)}) collective-permute-start(f32[3,8,16,256]{3,2,1,0:T(8,128)S(1)} %add_bitcast_fusion.refs_3_), channel_id=1, source_target_pairs={{0,4},{4,0},{1,5},{5,1},{2,6},{6,2},{3,7},{7,3},{8,12},{12,8},{9,1... | collective-permute-start | bytes 1179656 | tf_op jit(solution)/shard_map/ppermute | solution.py:30
  76.5 7.6 %collective-permute-start.29 = (f32[1,2,8,16,256]{4,3,2,1,0:T(8,128)S(1)}, f32[1,2,8,16,256]{4,3,2,1,0:T(8,128)S(1)}, u32[]{:S(2)}, u32[]{:S(2)}) collective-permute-start(f32[1,2,8,16,256]{4,3,2,1,0:T(8,128)S(1)} %pad_maximum_fusion.5), channel_id=1, source_target_pairs={{0,16},{8,24},{16,0},{24,8},{1,17},{9,25},{17,1},{25,9},{2,18},{10... | collective-permute-start | bytes 786440 | tf_op jit(solution)/shard_map/ppermute | solution.py:30
  79.3 6.7 %collective-permute-start.17 = (f32[2,4,64,128]{3,2,1,0:T(8,128)S(1)}, f32[2,4,64,128]{3,2,1,0:T(8,128)S(1)}, u32[]{:S(2)}, u32[]{:S(2)}) collective-permute-start(f32[2,4,64,128]{3,2,1,0:T(8,128)S(1)} %dynamic-slice_bitcast_fusion.2), channel_id=1, source_target_pairs={{0,8},{8,0},{16,24},{24,16},{1,9},{9,1},{17,25},{25,17},{2,10},{10... | collective-permute-start | bytes 786440 | tf_op jit(solution)/shard_map/ppermute | solution.py:30
  79.4 9.6 %collective-permute-start.30 = (f32[1,2,8,16,256]{4,3,2,1,0:T(8,128)S(1)}, f32[1,2,8,16,256]{4,3,2,1,0:T(8,128)S(1)}, u32[]{:S(2)}, u32[]{:S(2)}) collective-permute-start(f32[1,2,8,16,256]{4,3,2,1,0:T(8,128)S(1)} %pad_maximum_fusion.4), channel_id=1, source_target_pairs={{0,16},{8,24},{16,0},{24,8},{1,17},{9,25},{17,1},{25,9},{2,18},{10... | collective-permute-start | bytes 786440 | tf_op jit(solution)/shard_map/ppermute | solution.py:30
  84.2 19.0 %collective-permute-start.34 = (f32[1,8,16,256]{3,2,1,0:T(8,128)S(1)}, f32[1,8,16,256]{3,2,1,0:T(8,128)S(1)}, u32[]{:S(2)}, u32[]{:S(2)}) collective-permute-start(f32[1,8,16,256]{3,2,1,0:T(8,128)S(1)} %add_bitcast_fusion.11.refs_4_), channel_id=1, source_target_pairs={{0,4},{4,0},{1,5},{5,1},{2,6},{6,2},{3,7},{7,3},{8,12},{12,8},{9,1... | collective-permute-start | bytes 393224 | tf_op jit(solution)/shard_map/ppermute | solution.py:30
  86.0 17.1 %collective-permute-start.35 = (f32[2,8,16,256]{3,2,1,0:T(8,128)S(1)}, f32[2,8,16,256]{3,2,1,0:T(8,128)S(1)}, u32[]{:S(2)}, u32[]{:S(2)}) collective-permute-start(f32[2,8,16,256]{3,2,1,0:T(8,128)S(1)} %add_bitcast_fusion.3.refs_5_), channel_id=1, source_target_pairs={{0,4},{4,0},{1,5},{5,1},{2,6},{6,2},{3,7},{7,3},{8,12},{12,8},{9,1... | collective-permute-start | bytes 786440 | tf_op jit(solution)/shard_map/ppermute | solution.py:30
  86.4 10.6 %collective-permute-start.18 = (f32[2,2,64,128]{3,2,1,0:T(8,128)S(1)}, f32[2,2,64,128]{3,2,1,0:T(8,128)S(1)}, u32[]{:S(2)}, u32[]{:S(2)}) collective-permute-start(f32[2,2,64,128]{3,2,1,0:T(8,128)S(1)} %dynamic-slice_bitcast_fusion.4), channel_id=1, source_target_pairs={{0,2},{1,3},{2,0},{3,1},{4,6},{5,7},{6,4},{7,5},{8,10},{9,11},{10,... | collective-permute-start | bytes 393224 | tf_op jit(solution)/shard_map/ppermute | solution.py:30
  89.0 8.1 %collective-permute-start.31 = (f32[1,1,8,16,256]{4,3,2,1,0:T(8,128)S(1)}, f32[1,1,8,16,256]{4,3,2,1,0:T(8,128)S(1)}, u32[]{:S(2)}, u32[]{:S(2)}) collective-permute-start(f32[1,1,8,16,256]{4,3,2,1,0:T(8,128)S(1)} %get-tuple-element.123), channel_id=1, source_target_pairs={{0,16},{8,24},{16,0},{24,8},{1,17},{9,25},{17,1},{25,9},{2,18},{10... | collective-permute-start | bytes 393224 | tf_op jit(solution)/shard_map/ppermute | solution.py:30
  93.3 12.2 %collective-permute-start.32 = (f32[2,8,16,256]{3,2,1,0:T(8,128)S(1)}, f32[2,8,16,256]{3,2,1,0:T(8,128)S(1)}, u32[]{:S(2)}, u32[]{:S(2)}) collective-permute-start(f32[2,8,16,256]{3,2,1,0:T(8,128)S(1)} %add_bitcast_fusion.2.refs_4_), channel_id=1, source_target_pairs={{0,4},{4,0},{1,5},{5,1},{2,6},{6,2},{3,7},{7,3},{8,12},{12,8},{9,1... | collective-permute-start | bytes 786440 | tf_op jit(solution)/shard_map/ppermute | solution.py:30
  101.7 10.2 %collective-permute-start.26 = (f32[2,2,80,128]{3,2,1,0:T(8,128)S(1)}, f32[2,2,80,128]{3,2,1,0:T(8,128)S(1)}, u32[]{:S(2)}, u32[]{:S(2)}) collective-permute-start(f32[2,2,80,128]{3,2,1,0:T(8,128)S(1)} %dynamic-slice_bitcast_fusion.3), channel_id=1, source_target_pairs={{0,2},{1,3},{2,0},{3,1},{4,6},{5,7},{6,4},{7,5},{8,10},{9,11},{10,... | collective-permute-start | bytes 491528 | tf_op jit(solution)/shard_map/ppermute | solution.py:30
  108.0 8.6 %collective-permute-start.36 = (f32[2,4,112,128]{3,2,1,0:T(8,128)S(1)}, f32[2,4,112,128]{3,2,1,0:T(8,128)S(1)}, u32[]{:S(2)}, u32[]{:S(2)}) collective-permute-start(f32[2,4,112,128]{3,2,1,0:T(8,128)S(1)} %dynamic-slice_bitcast_fusion), channel_id=1, source_target_pairs={{0,8},{8,0},{16,24},{24,16},{1,9},{9,1},{17,25},{25,17},{2,10},{10... | collective-permute-start | bytes 1376264 | tf_op jit(solution)/shard_map/ppermute | solution.py:30
  112.1 10.4 %collective-permute-start.20 = (f32[64,128]{1,0:T(8,128)S(1)}, f32[64,128]{1,0:T(8,128)S(1)}, u32[]{:S(2)}, u32[]{:S(2)}) collective-permute-start(f32[64,128]{1,0:T(8,128)S(1)} %dynamic-slice_bitcast_fusion.6), channel_id=1, source_target_pairs={{0,16},{8,24},{16,0},{24,8},{1,17},{9,25},{17,1},{25,9},{2,18},{10... | collective-permute-start | bytes 98312 | tf_op jit(solution)/shard_map/ppermute | solution.py:30
  117.4 17.8 %all-to-all-start = ((f32[8,112,128]{2,1,0:T(8,128)}), f32[8,112,128]{2,1,0:T(8,128)S(1)}, u32[]{:S(2)}, u32[]{:S(2)}) async-start(f32[8,112,128]{2,1,0:T(8,128)} %bitcast.99), calls=%async_computation | async-start | bytes 917504 | tf_op jit(solution)/shard_map/all_to_all | solution.py:220
  (7 other events, 29.5 us)

commit v5 on v4

--- a/solution.py
+++ b/solution.py
@@ -10,20 +10,8 @@
 
 VMEM_LIMIT = 44 << 20
 BRIEF = pl.CostEstimate(flops=0, bytes_accessed=0, transcendentals=0)
+DEEP = 2
 LAG = 2
-DEEP = 2
-PASS = 5
-AHEAD = 1
-ORDERED = 1
-HALF_SEND = 0
-HALF_TAKE = 0
-HALF_GRAM = 1
-GRAM_LATE = 0
-STRIPS = 3
-FIRST = [1, 1, 1, 1, 1, 1]
-MIDDLE = [3, 3]
-LAST = [1, 2, 2, 1]
-APART = 1
 
 
 def swap(x, axis, bit):
@@ -183,9 +171,7 @@
 
 
 def strips_of(rest):
-    if rest % 32:
-        return [rest]
-    return [rest // 2, rest // 4, rest // 4] if STRIPS == 3 else [rest - rest // 4, rest // 4] if STRIPS == 2 else [rest // 2, rest // 2]
+    return [rest // 2, rest // 4, rest // 4] if rest % 32 == 0 else [rest]
 
 
 def summed_over_core(region):
@@ -236,37 +222,44 @@
     halves = [range(middle), range(middle, each)] if middle else [range(each)]
 
     def groups_of(i):
-        sizes = [1] * each if each != 6 else FIRST if i == 0 else LAST if i == len(widths) - 1 else MIDDLE
-        if each != 6 and i:
-            sizes = [len(x) for x in halves]
-        return [range(sum(sizes[:n]), sum(sizes[: n + 1])) for n in range(len(sizes))]
+        if i == 0:
+            return [range(c, c + 1) for c in range(each)]
+        if i == len(widths) - 1 and len(halves) == 2 and middle > 1:
+            cuts = [0, 1, middle, each - 1, each]
+            return [range(low, high) for low, high in zip(cuts, cuts[1:])]
+        return halves
 
     cuts = [(0, widths[0])] + ([(widths[0], rest)] if len(widths) > 1 else [])
     trips = [range(c, c + 1) for c in range(min(2, each))] + ([range(2, each)] if each > 2 else [])
     came_of, terms = {}, {}
     factors = [factor, swap(factor, "aa", 1)]
-    for n, trip in enumerate(trips):
+    def exchange(*after):
+        trip = trips.pop(0)
         first = (me_a & 1 ^ 1) * each
-        if n:
-            first = tie(first, going, *(factors[1:] if n == 1 else []))
+        first = tie(first, *after) if after else first
         going = gathered(jnp.stack([first + 2 * each * x + c for x in range(aa // 2) for c in trip]), field)
-        if n > 1:
+        if len(came_of) > 1:
             going = tie(going, came_of[0][0])
         came = swap(going, "aa", 1)
         for c in trip:
             came_of[c] = came, [(me_a ^ d) // 2 * len(trip) + c - trip[0] for d in keep]
+        return going
 
     def truncate(c, *after):
         came, slots = came_of[c]
         half = len(keep) // 2
         parts = [x for x in (range(half), range(half, len(keep))) if x]
         terms[c] = []
-        for together in [[x] for x in parts] if c < APART else [parts]:
+        for together in [parts] if c else [[x] for x in parts]:
             layers = jnp.stack([(me_a ^ keep[n]) * each + c for part in together for n in part])
             places = jnp.stack([slots[n] for part in together for n in part])
             sizes = [len(x) for x in together]
             terms[c] += truncated(sizes, tie(layers, *after), places, field, came, factors, owners, cuts)
             after = terms[c][-1][:1]
+            if c == 0 and trips:
+                exchange(*after)
+        while c == 0 and trips:
+            exchange(*after)
 
     def terms_of(part, group, i):
         cut = min(i, 1)
@@ -284,7 +277,7 @@
         used = [
             [[pieces[d, s, g] for g in groups_of(s) if g[0] in group] for s in range(i + 1)] for d in range(ba)
         ]
-        regions[i] = gram_strip(tie(me_b, *after, *halfway[:HALF_GRAM]), used, widths[: i + 1], unit, regions[i])
+        regions[i] = gram_strip(tie(me_b, *after, *halfway[:1]), used, widths[: i + 1], unit, regions[i])
         if group[-1] == each - 1:
             region = regions[i].reshape(aa, col, *regions[i].shape[2:])
             summed = summed_over_core(region)
@@ -295,12 +288,13 @@
         i, group = steps[n]
         if i == 0:
             for c in group:
-                truncate(c, *(terms[c - 1][-1][:1] if c else []), *(arrived[n - DEEP : n - DEEP + 1] if n >= DEEP else []))
-        after = ([arrived[n - DEEP]] if n >= DEEP else []) + (passed[n - PASS] if n >= PASS else []) + halfway[:HALF_SEND]
+                truncate(c, *(terms[c - 1][-1][:1] if c else [first]), *arrived[max(n - DEEP, 0) : max(n - DEEP + 1, 0)])
+        after = arrived[max(n - DEEP, 0) : max(n - DEEP + 1, 0)] + (passed[n - DEEP - 3] if n >= DEEP + 3 else [])
         leaving_of[n] = terms_of(0, group, i)
         if after:
             leaving_of[n] = tie(leaving_of[n], *after)
 
+    first = exchange()
     for n in range(min(DEEP - 1, len(steps))):
         send(n)
     for n, (i, group) in enumerate(steps):
@@ -308,8 +302,7 @@
         if ahead < len(steps):
             send(ahead)
         leaving = leaving_of[n]
-        late = min(n + AHEAD, len(steps) - 1, len(leaving_of) - 1)
-        t = tie(terms_of(-1, group, i), leaving_of[late], *arrived[len(arrived) - ORDERED :], *halfway[:HALF_TAKE])
+        t = tie(terms_of(-1, group, i), leaving_of[min(ahead, len(steps) - 1)], *arrived[-1:])
         for bit in bits[1:]:
             t = t + swap(leaving, "aa", bit)
             half = t.shape[0] // 2
@@ -323,7 +316,7 @@
             if group[-1] == part[-1]:
                 waiting.append((n, i, part))
         if waiting and waiting[0][0] <= n - LAG:
-            add_gram(*waiting.pop(0)[1:], t if GRAM_LATE else leaving_of[min(ahead, len(steps) - 1)])
+            add_gram(*waiting.pop(0)[1:], leaving_of[min(ahead, len(steps) - 1)])
     while waiting:
         add_gram(*waiting.pop(0)[1:])
 

time: 137 us -> 136 us (level)
  starting transfers between devices: 46.7 us -> 43.5 us
  waiting for transfers between devices: 45 us -> 47.7 us
    ppermute x37, waiting for transfers between devices: 33 us -> 35.7 us  [swap(): lax.ppermute(x, axis, [(i, i ^ bit) for i in range(lax.axis_size(axis))])]
    ppermute x37, starting transfers between devices: 41.7 us -> 40 us  [swap(): lax.ppermute(x, axis, [(i, i ^ bit) for i in range(lax.axis_size(axis))])]
    all_to_all x1, starting transfers between devices: 5.04 us -> 3.55 us  [block_by_all_to_all(): lax.all_to_all(t, ('aa', 'col'), 0, 0, tiled=True, axis_index_groups=groups)]
  transfers between devices with their start and end apart: 38 -> 38, of which waited for: 12 -> 14; matrix products, arithmetic and copies ran while one was open for 3% -> 3% of each run, Pallas kernels for 27% -> 20%
where the time goes in v5:
time: 136 us
  waiting for transfers between devices  47.7 us (35%)
  starting transfers between devices  43.5 us (32%)
  Pallas kernels  38 us (28%)
  local copies, waits for them, and re-layouts  3 us (2%)
  other arithmetic  2.87 us (2%)
    ppermute x37, starting transfers between devices, swap(): lax.ppermute(x, axis, [(i, i ^ bit) for i in range(lax.axis_size(axis))])  40 us
    ppermute x37, waiting for transfers between devices, swap(): lax.ppermute(x, axis, [(i, i ^ bit) for i in range(lax.axis_size(axis))])  35.7 us
    pallas_call x7, Pallas kernels, truncated(): pl.pallas_call(functools.partial(truncate_kernel, cuts, sizes), grid_spec...  20.3 us
    all_to_all x1, waiting for transfers between devices, block_by_all_to_all(): lax.all_to_all(t, ('aa', 'col'), 0, 0, tiled=True, axis_index_groups=groups)  12 us
    pallas_call x6, Pallas kernels, gram_strip(): pl.pallas_call(functools.partial(gram_kernel, ba, widths, counts, unit, l...  9.9 us
    pallas_call x3, Pallas kernels, gathered(): pl.pallas_call(gather_kernel, in_specs=[pl.BlockSpec(memory_space=pltpu.S...  7.83 us
    all_to_all x1, starting transfers between devices, block_by_all_to_all(): lax.all_to_all(t, ('aa', 'col'), 0, 0, tiled=True, axis_index_groups=groups)  3.55 us
  transfers between devices with their start and end apart: 38, of which 14 were waited for; matrix products, arithmetic and copies ran while one was open for 3% of the time, Pallas kernels for 20%

profile of v5, /device:TPU:0, one launch (start us, length us, event | category | flops | bytes accessed | tf_op | source)
XLA Modules:
  0.0 135.8 jit_solution(5921887043054441664)
XLA Ops:
  0.1 1.8 %shard_map.28 = f32[2,256,512]{2,1,0:T(8,128)S(1)} custom-call(s32[2]{0:T(128)S(1)} %pad_add_fusion.layers_ref, f32[24,256,512]{2,1,0:T(8,128)} %refs_0_.13), custom_call_target="tpu_custom_call" | custom-call | tf_op jit(solution)/shard_map/pallas_call | solution.py:50
  2.6 2.5 %collective-permute-done.1.refs_3_ = f32[256,256]{1,0:T(8,128)S(1)} collective-permute-done((f32[256,256]{1,0:T(8,128)S(1)}, f32[256,256]{1,0:T(8,128)S(1)}, u32[]{:S(2)}, u32[]{:S(2)}) %collective-permute-start.1) | collective-permute-done | bytes 262176 | tf_op jit(solution)/shard_map/ppermute | solution.py:18
  5.1 2.2 %shard_map.29 = (f32[1,8,32,256]{3,2,1,0:T(8,128)S(1)}, f32[1,8,32,256]{3,2,1,0:T(8,128)S(1)}) custom-call(s32[2]{0:T(128)S(1)} %get-tuple-element.157._, f32[24,256,512]{2,1,0:T(8,128)} %refs_0_.13, f32[2,256,512]{2,1,0:T(8,128)S(1)} %collective-permute-done.refs_1_, f32[256,256]{1,0:T(8,128)S(1)} %copy-done, f32[256,256]{1,0:T(8,128)S(1)} %collective-permute-done.1.refs_3_), custom_call_target="tpu_custom_call" | custom-call | tf_op jit(solution)/shard_map/pallas_call | solution.py:91
  8.1 2.2 %shard_map.30 = (f32[1,8,32,256]{3,2,1,0:T(8,128)S(1)}, f32[1,8,32,256]{3,2,1,0:T(8,128)S(1)}) custom-call(s32[2]{0:T(128)S(1)} %pad_add_fusion.2._, f32[24,256,512]{2,1,0:T(8,128)} %refs_0_.13, f32[2,256,512]{2,1,0:T(8,128)S(1)} %collective-permute-done.refs_1_, f32[256,256]{1,0:T(8,128)S(1)} %copy-done, f32[256,256]{1,0:T(8,128)S(1)} %collective-permute-done.1.refs_3_), custom_call_target="tpu_custom_call" | custom-call | tf_op jit(solution)/shard_map/pallas_call | solution.py:91
  10.4 4.2 %shard_map.33 = f32[8,256,512]{2,1,0:T(8,128)} custom-call(s32[8]{0:T(128)S(1)} %stack.154.layers_ref, f32[24,256,512]{2,1,0:T(8,128)} %refs_0_.13), custom_call_target="tpu_custom_call" | custom-call | tf_op jit(solution)/shard_map/pallas_call | solution.py:50
  15.2 1.8 %shard_map.31 = f32[2,256,512]{2,1,0:T(8,128)S(1)} custom-call(s32[2]{0:T(128)S(1)} %pad_add_fusion.5.layers_ref, f32[24,256,512]{2,1,0:T(8,128)} %refs_0_.13), custom_call_target="tpu_custom_call" | custom-call | tf_op jit(solution)/shard_map/pallas_call | solution.py:50
  17.5 2.9 %collective-permute-start.3 = (f32[1,1,8,32,256]{4,3,2,1,0:T(8,128)}, f32[1,1,8,32,256]{4,3,2,1,0:T(8,128)S(1)}, u32[]{:S(2)}, u32[]{:S(2)}) collective-permute-start(f32[1,1,8,32,256]{4,3,2,1,0:T(8,128)} %bitcast.191), channel_id=1, source_target_pairs={{0,16},{8,24},{16,0},{24,8},{1,17},{9,25},{17,1},{25,9},{2,18},{10... | collective-permute-start | bytes 786440 | tf_op jit(solution)/shard_map/ppermute | solution.py:18
  20.5 2.9 %collective-permute-done.2.refs_1_ = f32[2,256,512]{2,1,0:T(8,128)S(1)} collective-permute-done((f32[2,256,512]{2,1,0:T(8,128)S(1)}, f32[2,256,512]{2,1,0:T(8,128)S(1)}, u32[]{:S(2)}, u32[]{:S(2)}) %collective-permute-start.2) | collective-permute-done | bytes 1048608 | tf_op jit(solution)/shard_map/ppermute | solution.py:18
  23.4 3.0 %shard_map.32 = (f32[1,8,32,256]{3,2,1,0:T(8,128)S(1)}, f32[1,8,32,256]{3,2,1,0:T(8,128)S(1)}, f32[1,8,32,256]{3,2,1,0:T(8,128)S(1)}, f32[1,8,32,256]{3,2,1,0:T(8,128)S(1)}) custom-call(s32[4]{0:T(128)S(1)} %pad_add_fusion.4._, f32[24,256,512]{2,1,0:T(8,128)} %refs_0_.13, f32[2,256,512]{2,1,0:T(8,128)S(1)} %collective-permute-done.2.refs_1_, ...), custom_call_target="tpu_custom_call" | custom-call | tf_op jit(solution)/shard_map/pallas_call | solution.py:91
  26.4 2.9 %collective-permute-start.5 = (f32[1,1,8,32,256]{4,3,2,1,0:T(8,128)S(1)}, f32[1,1,8,32,256]{4,3,2,1,0:T(8,128)S(1)}, u32[]{:S(2)}, u32[]{:S(2)}) collective-permute-start(f32[1,1,8,32,256]{4,3,2,1,0:T(8,128)S(1)} %bitcast.196), channel_id=1, source_target_pairs={{0,16},{8,24},{16,0},{24,8},{1,17},{9,25},{17,1},{25,9},{2,18},{10... | collective-permute-start | bytes 786440 | tf_op jit(solution)/shard_map/ppermute | solution.py:18
  31.0 3.2 %shard_map.34 = (f32[1,8,32,256]{3,2,1,0:T(8,128)S(1)}, f32[1,8,32,256]{3,2,1,0:T(8,128)S(1)}, f32[1,8,32,256]{3,2,1,0:T(8,128)S(1)}, f32[1,8,32,256]{3,2,1,0:T(8,128)S(1)}) custom-call(s32[4]{0:T(128)S(1)} %pad_add_fusion.7._, f32[24,256,512]{2,1,0:T(8,128)} %refs_0_.13, f32[8,256,512]{2,1,0:T(8,128)} %collective-permute-done.4.refs_1_, ...), custom_call_target="tpu_custom_call" | custom-call | tf_op jit(solution)/shard_map/pallas_call | solution.py:91
  35.9 2.5 %collective-permute-start.10 = (f32[1,8,32,256]{3,2,1,0:T(8,128)S(1)}, f32[1,8,32,256]{3,2,1,0:T(8,128)S(1)}, u32[]{:S(2)}, u32[]{:S(2)}) collective-permute-start(f32[1,8,32,256]{3,2,1,0:T(8,128)S(1)} %add_bitcast_fusion.8.refs_1_), channel_id=1, source_target_pairs={{0,4},{4,0},{1,5},{5,1},{2,6},{6,2},{3,7},{7,3},{8,12},{12,8},{9,1... | collective-permute-start | bytes 786440 | tf_op jit(solution)/shard_map/ppermute | solution.py:18
  38.5 3.2 %shard_map.35 = (f32[1,8,32,256]{3,2,1,0:T(8,128)S(1)}, f32[1,8,32,256]{3,2,1,0:T(8,128)S(1)}, f32[1,8,32,256]{3,2,1,0:T(8,128)S(1)}, f32[1,8,32,256]{3,2,1,0:T(8,128)S(1)}) custom-call(s32[4]{0:T(128)S(1)} %pad_add_fusion.9._, f32[24,256,512]{2,1,0:T(8,128)} %refs_0_.13, f32[8,256,512]{2,1,0:T(8,128)} %collective-permute-done.4.refs_1_, ...), custom_call_target="tpu_custom_call" | custom-call | tf_op jit(solution)/shard_map/pallas_call | solution.py:91
  41.6 1.7 %collective-permute-start.7 = (f32[1,1,8,32,256]{4,3,2,1,0:T(8,128)S(1)}, f32[1,1,8,32,256]{4,3,2,1,0:T(8,128)S(1)}, u32[]{:S(2)}, u32[]{:S(2)}) collective-permute-start(f32[1,1,8,32,256]{4,3,2,1,0:T(8,128)S(1)} %bitcast.192), channel_id=1, source_target_pairs={{0,16},{8,24},{16,0},{24,8},{1,17},{9,25},{17,1},{25,9},{2,18},{10... | collective-permute-start | bytes 786440 | tf_op jit(solution)/shard_map/ppermute | solution.py:18
  44.1 3.2 %shard_map.36 = (f32[1,8,32,256]{3,2,1,0:T(8,128)S(1)}, f32[1,8,32,256]{3,2,1,0:T(8,128)S(1)}, f32[1,8,32,256]{3,2,1,0:T(8,128)S(1)}, f32[1,8,32,256]{3,2,1,0:T(8,128)S(1)}) custom-call(s32[4]{0:T(128)S(1)} %pad_add_fusion.11._, f32[24,256,512]{2,1,0:T(8,128)} %refs_0_.13, f32[8,256,512]{2,1,0:T(8,128)} %collective-permute-done.4.refs_1_, ...), custom_call_target="tpu_custom_call" | custom-call | tf_op jit(solution)/shard_map/pallas_call | solution.py:91
  49.6 3.3 %shard_map.37 = (f32[1,8,32,256]{3,2,1,0:T(8,128)S(1)}, f32[1,8,32,256]{3,2,1,0:T(8,128)S(1)}, f32[1,8,32,256]{3,2,1,0:T(8,128)S(1)}, f32[1,8,32,256]{3,2,1,0:T(8,128)S(1)}) custom-call(s32[4]{0:T(128)S(1)} %pad_add_fusion.13._, f32[24,256,512]{2,1,0:T(8,128)} %refs_0_.13, f32[8,256,512]{2,1,0:T(8,128)} %collective-permute-done.4.refs_1_, ...), custom_call_target="tpu_custom_call" | custom-call | tf_op jit(solution)/shard_map/pallas_call | solution.py:91
  56.7 5.6 %collective-permute-done.11 = f32[1,1,8,32,256]{4,3,2,1,0:T(8,128)S(1)} collective-permute-done((f32[1,1,8,32,256]{4,3,2,1,0:T(8,128)S(1)}, f32[1,1,8,32,256]{4,3,2,1,0:T(8,128)S(1)}, u32[]{:S(2)}, u32[]{:S(2)}) %collective-permute-start.11) | collective-permute-done | bytes 262176 | tf_op jit(solution)/shard_map/ppermute | solution.py:18
  65.7 5.0 %collective-permute-done.13 = f32[1,3,8,16,256]{4,3,2,1,0:T(8,128)S(1)} collective-permute-done((f32[1,3,8,16,256]{4,3,2,1,0:T(8,128)S(1)}, f32[1,3,8,16,256]{4,3,2,1,0:T(8,128)S(1)}, u32[]{:S(2)}, u32[]{:S(2)}) %collective-permute-start.13) | collective-permute-done | bytes 393248 | tf_op jit(solution)/shard_map/ppermute | solution.py:18
  74.2 3.6 %collective-permute-done.21 = f32[1,3,8,16,256]{4,3,2,1,0:T(8,128)S(1)} collective-permute-done((f32[1,3,8,16,256]{4,3,2,1,0:T(8,128)S(1)}, f32[1,3,8,16,256]{4,3,2,1,0:T(8,128)S(1)}, u32[]{:S(2)}, u32[]{:S(2)}) %collective-permute-start.21) | collective-permute-done | bytes 393248 | tf_op jit(solution)/shard_map/ppermute | solution.py:18
  80.1 2.1 %collective-permute-start.34 = (f32[1,8,16,256]{3,2,1,0:T(8,128)S(1)}, f32[1,8,16,256]{3,2,1,0:T(8,128)S(1)}, u32[]{:S(2)}, u32[]{:S(2)}) collective-permute-start(f32[1,8,16,256]{3,2,1,0:T(8,128)S(1)} %add_bitcast_fusion.11.refs_4_), channel_id=1, source_target_pairs={{0,4},{4,0},{1,5},{5,1},{2,6},{6,2},{3,7},{7,3},{8,12},{12,8},{9,1... | collective-permute-start | bytes 393224 | tf_op jit(solution)/shard_map/ppermute | solution.py:18
  82.9 4.8 %collective-permute-done.29 = f32[1,2,8,16,256]{4,3,2,1,0:T(8,128)S(1)} collective-permute-done((f32[1,2,8,16,256]{4,3,2,1,0:T(8,128)S(1)}, f32[1,2,8,16,256]{4,3,2,1,0:T(8,128)S(1)}, u32[]{:S(2)}, u32[]{:S(2)}) %collective-permute-start.29) | collective-permute-done | bytes 262176 | tf_op jit(solution)/shard_map/ppermute | solution.py:18
  87.7 2.6 %collective-permute-start.18 = (f32[2,2,64,128]{3,2,1,0:T(8,128)S(1)}, f32[2,2,64,128]{3,2,1,0:T(8,128)S(1)}, u32[]{:S(2)}, u32[]{:S(2)}) collective-permute-start(f32[2,2,64,128]{3,2,1,0:T(8,128)S(1)} %dynamic-slice_bitcast_fusion.4), channel_id=1, source_target_pairs={{0,2},{1,3},{2,0},{3,1},{4,6},{5,7},{6,4},{7,5},{8,10},{9,11},{10,... | collective-permute-start | bytes 393224 | tf_op jit(solution)/shard_map/ppermute | solution.py:18
  92.0 1.7 %shard_map.40.refs_8_ = f32[2,8,80,128]{3,2,1,0:T(8,128)S(1)} custom-call(s32[1]{0:T(128)} %bitcast.80.me_ref, f32[1,8,32,256]{3,2,1,0:T(8,128)S(1)} %add_bitcast_fusion.9.refs_0_, f32[1,8,32,256]{3,2,1,0:T(8,128)S(1)} %add_bitcast_fusion.8.refs_1_, f32[1,8,32,256]{3,2,1,0:T(8,128)S(1)} %add_bitcast_fusion.7.refs_2_, ...), custom_call_target="tpu_custom_call" | custom-call | tf_op jit(solution)/shard_map/pallas_call | solution.py:155
  94.2 1.7 %shard_map.41 = f32[2,8,80,128]{3,2,1,0:T(8,128)S(1)} custom-call(s32[1]{0:T(128)} %bitcast.79.me_ref, f32[1,8,32,256]{3,2,1,0:T(8,128)S(1)} %add_bitcast_fusion.6.refs_0_, f32[1,8,32,256]{3,2,1,0:T(8,128)S(1)} %add_bitcast_fusion.5.refs_1_, f32[1,8,32,256]{3,2,1,0:T(8,128)S(1)} %add_bitcast_fusion.4.refs_2_, ...), custom_call_target="tpu_custom_call", output_to_operand_aliasing={{}: (9, {})} | custom-call | tf_op jit(solution)/shard_map/pallas_call | solution.py:155
  101.0 2.0 %collective-permute-done.19 = f32[2,1,64,128]{3,2,1,0:T(8,128)S(1)} collective-permute-done((f32[2,1,64,128]{3,2,1,0:T(8,128)S(1)}, f32[2,1,64,128]{3,2,1,0:T(8,128)S(1)}, u32[]{:S(2)}, u32[]{:S(2)}) %collective-permute-start.19) | collective-permute-done | bytes 65568 | tf_op jit(solution)/shard_map/ppermute | solution.py:18
  103.3 2.3 %shard_map.42.refs_12_ = f32[2,8,112,128]{3,2,1,0:T(8,128)S(1)} custom-call(s32[1]{0:T(128)} %bitcast.95.me_ref, f32[1,8,32,256]{3,2,1,0:T(8,128)S(1)} %add_bitcast_fusion.9.refs_0_, f32[1,8,32,256]{3,2,1,0:T(8,128)S(1)} %add_bitcast_fusion.8.refs_1_, f32[1,8,32,256]{3,2,1,0:T(8,128)S(1)} %add_bitcast_fusion.7.refs_2_, ...), custom_call_target="tpu_custom_call" | custom-call | tf_op jit(solution)/shard_map/pallas_call | solution.py:155
  105.6 2.1 %collective-permute-done.33.refs_11_ = f32[1,8,16,256]{3,2,1,0:T(8,128)S(1)} collective-permute-done((f32[1,8,16,256]{3,2,1,0:T(8,128)S(1)}, f32[1,8,16,256]{3,2,1,0:T(8,128)S(1)}, u32[]{:S(2)}, u32[]{:S(2)}) %collective-permute-start.33) | collective-permute-done | bytes 131104 | tf_op jit(solution)/shard_map/ppermute | solution.py:18
  107.7 2.4 %shard_map.43 = f32[2,8,112,128]{3,2,1,0:T(8,128)S(1)} custom-call(s32[1]{0:T(128)} %bitcast.91.me_ref, f32[1,8,32,256]{3,2,1,0:T(8,128)S(1)} %add_bitcast_fusion.6.refs_0_, f32[1,8,32,256]{3,2,1,0:T(8,128)S(1)} %add_bitcast_fusion.5.refs_1_, f32[1,8,32,256]{3,2,1,0:T(8,128)S(1)} %add_bitcast_fusion.4.refs_2_, ...), custom_call_target="tpu_custom_call", output_to_operand_aliasing={{}: (13, {})} | custom-call | tf_op jit(solution)/shard_map/pallas_call | solution.py:155
  110.2 1.9 %collective-permute-done.26 = f32[2,2,80,128]{3,2,1,0:T(8,128)S(1)} collective-permute-done((f32[2,2,80,128]{3,2,1,0:T(8,128)S(1)}, f32[2,2,80,128]{3,2,1,0:T(8,128)S(1)}, u32[]{:S(2)}, u32[]{:S(2)}) %collective-permute-start.26) | collective-permute-done | bytes 163872 | tf_op jit(solution)/shard_map/ppermute | solution.py:18
  113.6 3.1 %collective-permute-done.27 = f32[2,1,80,128]{3,2,1,0:T(8,128)S(1)} collective-permute-done((f32[2,1,80,128]{3,2,1,0:T(8,128)S(1)}, f32[2,1,80,128]{3,2,1,0:T(8,128)S(1)}, u32[]{:S(2)}, u32[]{:S(2)}) %collective-permute-start.27) | collective-permute-done | bytes 81952 | tf_op jit(solution)/shard_map/ppermute | solution.py:18
  118.0 3.6 %all-to-all-start = ((f32[8,112,128]{2,1,0:T(8,128)}), f32[8,112,128]{2,1,0:T(8,128)S(1)}, u32[]{:S(2)}, u32[]{:S(2)}) async-start(f32[8,112,128]{2,1,0:T(8,128)} %bitcast.99), calls=%async_computation | async-start | bytes 917504 | tf_op jit(solution)/shard_map/all_to_all | solution.py:206
  122.2 12.0 %all-to-all-done = f32[8,112,128]{2,1,0:T(8,128)S(1)} async-done(((f32[8,112,128]{2,1,0:T(8,128)}), f32[8,112,128]{2,1,0:T(8,128)S(1)}, u32[]{:S(2)}, u32[]{:S(2)}) %all-to-all-start) | async-done | bytes 458784 | tf_op jit(solution)/shard_map/all_to_all | solution.py:206
  (149 shorter events, 35.0 us)
Async XLA Ops:
  14.6 16.4 %collective-permute-start.4 = (f32[8,256,512]{2,1,0:T(8,128)}, f32[8,256,512]{2,1,0:T(8,128)}, u32[]{:S(2)}, u32[]{:S(2)}) collective-permute-start(f32[8,256,512]{2,1,0:T(8,128)} %shard_map.33), channel_id=1, source_target_pairs={{0,8},{8,0},{16,24},{24,16},{1,9},{9,1},{17,25},{25,17},{2,10},{10... | collective-permute-start | bytes 12582920 | tf_op jit(solution)/shard_map/ppermute | solution.py:18
  17.0 6.4 %collective-permute-start.2 = (f32[2,256,512]{2,1,0:T(8,128)S(1)}, f32[2,256,512]{2,1,0:T(8,128)S(1)}, u32[]{:S(2)}, u32[]{:S(2)}) collective-permute-start(f32[2,256,512]{2,1,0:T(8,128)S(1)} %shard_map.31), channel_id=1, source_target_pairs={{0,8},{8,0},{16,24},{24,16},{1,9},{9,1},{17,25},{25,17},{2,10},{10... | collective-permute-start | bytes 3145736 | tf_op jit(solution)/shard_map/ppermute | solution.py:18
  17.5 11.8 %collective-permute-start.3 = (f32[1,1,8,32,256]{4,3,2,1,0:T(8,128)}, f32[1,1,8,32,256]{4,3,2,1,0:T(8,128)S(1)}, u32[]{:S(2)}, u32[]{:S(2)}) collective-permute-start(f32[1,1,8,32,256]{4,3,2,1,0:T(8,128)} %bitcast.191), channel_id=1, source_target_pairs={{0,16},{8,24},{16,0},{24,8},{1,17},{9,25},{17,1},{25,9},{2,18},{10... | collective-permute-start | bytes 786440 | tf_op jit(solution)/shard_map/ppermute | solution.py:18
  26.4 9.5 %collective-permute-start.5 = (f32[1,1,8,32,256]{4,3,2,1,0:T(8,128)S(1)}, f32[1,1,8,32,256]{4,3,2,1,0:T(8,128)S(1)}, u32[]{:S(2)}, u32[]{:S(2)}) collective-permute-start(f32[1,1,8,32,256]{4,3,2,1,0:T(8,128)S(1)} %bitcast.196), channel_id=1, source_target_pairs={{0,16},{8,24},{16,0},{24,8},{1,17},{9,25},{17,1},{25,9},{2,18},{10... | collective-permute-start | bytes 786440 | tf_op jit(solution)/shard_map/ppermute | solution.py:18
  29.3 23.6 %collective-permute-start.8 = (f32[1,8,32,256]{3,2,1,0:T(8,128)S(1)}, f32[1,8,32,256]{3,2,1,0:T(8,128)S(1)}, u32[]{:S(2)}, u32[]{:S(2)}) collective-permute-start(f32[1,8,32,256]{3,2,1,0:T(8,128)S(1)} %add_bitcast_fusion.9.refs_0_), channel_id=1, source_target_pairs={{0,4},{4,0},{1,5},{5,1},{2,6},{6,2},{3,7},{7,3},{8,12},{12,8},{9,1... | collective-permute-start | bytes 786440 | tf_op jit(solution)/shard_map/ppermute | solution.py:18
  34.2 9.4 %collective-permute-start.6 = (f32[1,1,8,32,256]{4,3,2,1,0:T(8,128)S(1)}, f32[1,1,8,32,256]{4,3,2,1,0:T(8,128)S(1)}, u32[]{:S(2)}, u32[]{:S(2)}) collective-permute-start(f32[1,1,8,32,256]{4,3,2,1,0:T(8,128)S(1)} %bitcast.193), channel_id=1, source_target_pairs={{0,16},{8,24},{16,0},{24,8},{1,17},{9,25},{17,1},{25,9},{2,18},{10... | collective-permute-start | bytes 786440 | tf_op jit(solution)/shard_map/ppermute | solution.py:18
  35.9 19.0 %collective-permute-start.10 = (f32[1,8,32,256]{3,2,1,0:T(8,128)S(1)}, f32[1,8,32,256]{3,2,1,0:T(8,128)S(1)}, u32[]{:S(2)}, u32[]{:S(2)}) collective-permute-start(f32[1,8,32,256]{3,2,1,0:T(8,128)S(1)} %add_bitcast_fusion.8.refs_1_), channel_id=1, source_target_pairs={{0,4},{4,0},{1,5},{5,1},{2,6},{6,2},{3,7},{7,3},{8,12},{12,8},{9,1... | collective-permute-start | bytes 786440 | tf_op jit(solution)/shard_map/ppermute | solution.py:18
  41.6 6.7 %collective-permute-start.7 = (f32[1,1,8,32,256]{4,3,2,1,0:T(8,128)S(1)}, f32[1,1,8,32,256]{4,3,2,1,0:T(8,128)S(1)}, u32[]{:S(2)}, u32[]{:S(2)}) collective-permute-start(f32[1,1,8,32,256]{4,3,2,1,0:T(8,128)S(1)} %bitcast.192), channel_id=1, source_target_pairs={{0,16},{8,24},{16,0},{24,8},{1,17},{9,25},{17,1},{25,9},{2,18},{10... | collective-permute-start | bytes 786440 | tf_op jit(solution)/shard_map/ppermute | solution.py:18
  43.6 19.6 %collective-permute-start.12 = (f32[1,8,32,256]{3,2,1,0:T(8,128)S(1)}, f32[1,8,32,256]{3,2,1,0:T(8,128)S(1)}, u32[]{:S(2)}, u32[]{:S(2)}) collective-permute-start(f32[1,8,32,256]{3,2,1,0:T(8,128)S(1)} %add_bitcast_fusion.7.refs_2_), channel_id=1, source_target_pairs={{0,4},{4,0},{1,5},{5,1},{2,6},{6,2},{3,7},{7,3},{8,12},{12,8},{9,1... | collective-permute-start | bytes 786440 | tf_op jit(solution)/shard_map/ppermute | solution.py:18
  47.2 7.6 %collective-permute-start.9 = (f32[1,1,8,32,256]{4,3,2,1,0:T(8,128)S(1)}, f32[1,1,8,32,256]{4,3,2,1,0:T(8,128)S(1)}, u32[]{:S(2)}, u32[]{:S(2)}) collective-permute-start(f32[1,1,8,32,256]{4,3,2,1,0:T(8,128)S(1)} %bitcast.194), channel_id=1, source_target_pairs={{0,16},{8,24},{16,0},{24,8},{1,17},{9,25},{17,1},{25,9},{2,18},{10... | collective-permute-start | bytes 786440 | tf_op jit(solution)/shard_map/ppermute | solution.py:18
  48.3 23.4 %collective-permute-start.14 = (f32[1,8,32,256]{3,2,1,0:T(8,128)S(1)}, f32[1,8,32,256]{3,2,1,0:T(8,128)S(1)}, u32[]{:S(2)}, u32[]{:S(2)}) collective-permute-start(f32[1,8,32,256]{3,2,1,0:T(8,128)S(1)} %add_bitcast_fusion.6.refs_0_), channel_id=1, source_target_pairs={{0,4},{4,0},{1,5},{5,1},{2,6},{6,2},{3,7},{7,3},{8,12},{12,8},{9,1... | collective-permute-start | bytes 786440 | tf_op jit(solution)/shard_map/ppermute | solution.py:18
  53.0 9.3 %collective-permute-start.11 = (f32[1,1,8,32,256]{4,3,2,1,0:T(8,128)S(1)}, f32[1,1,8,32,256]{4,3,2,1,0:T(8,128)S(1)}, u32[]{:S(2)}, u32[]{:S(2)}) collective-permute-start(f32[1,1,8,32,256]{4,3,2,1,0:T(8,128)S(1)} %bitcast.195), channel_id=1, source_target_pairs={{0,16},{8,24},{16,0},{24,8},{1,17},{9,25},{17,1},{25,9},{2,18},{10... | collective-permute-start | bytes 786440 | tf_op jit(solution)/shard_map/ppermute | solution.py:18
  54.9 15.8 %collective-permute-start.13 = (f32[1,3,8,16,256]{4,3,2,1,0:T(8,128)S(1)}, f32[1,3,8,16,256]{4,3,2,1,0:T(8,128)S(1)}, u32[]{:S(2)}, u32[]{:S(2)}) collective-permute-start(f32[1,3,8,16,256]{4,3,2,1,0:T(8,128)S(1)} %pad_maximum_fusion.2), channel_id=1, source_target_pairs={{0,16},{8,24},{16,0},{24,8},{1,17},{9,25},{17,1},{25,9},{2,18},{10... | collective-permute-start | bytes 1179656 | tf_op jit(solution)/shard_map/ppermute | solution.py:18
  56.5 16.7 %collective-permute-start.15 = (f32[1,8,32,256]{3,2,1,0:T(8,128)S(1)}, f32[1,8,32,256]{3,2,1,0:T(8,128)S(1)}, u32[]{:S(2)}, u32[]{:S(2)}) collective-permute-start(f32[1,8,32,256]{3,2,1,0:T(8,128)S(1)} %add_bitcast_fusion.5.refs_1_), channel_id=1, source_target_pairs={{0,4},{4,0},{1,5},{5,1},{2,6},{6,2},{3,7},{7,3},{8,12},{12,8},{9,1... | collective-permute-start | bytes 786440 | tf_op jit(solution)/shard_map/ppermute | solution.py:18
  62.3 10.9 %collective-permute-start.16 = (f32[1,8,32,256]{3,2,1,0:T(8,128)S(1)}, f32[1,8,32,256]{3,2,1,0:T(8,128)S(1)}, u32[]{:S(2)}, u32[]{:S(2)}) collective-permute-start(f32[1,8,32,256]{3,2,1,0:T(8,128)S(1)} %add_bitcast_fusion.4.refs_2_), channel_id=1, source_target_pairs={{0,4},{4,0},{1,5},{5,1},{2,6},{6,2},{3,7},{7,3},{8,12},{12,8},{9,1... | collective-permute-start | bytes 786440 | tf_op jit(solution)/shard_map/ppermute | solution.py:18
  63.3 14.6 %collective-permute-start.21 = (f32[1,3,8,16,256]{4,3,2,1,0:T(8,128)S(1)}, f32[1,3,8,16,256]{4,3,2,1,0:T(8,128)S(1)}, u32[]{:S(2)}, u32[]{:S(2)}) collective-permute-start(f32[1,3,8,16,256]{4,3,2,1,0:T(8,128)S(1)} %pad_maximum_fusion.1), channel_id=1, source_target_pairs={{0,16},{8,24},{16,0},{24,8},{1,17},{9,25},{17,1},{25,9},{2,18},{10... | collective-permute-start | bytes 1179656 | tf_op jit(solution)/shard_map/ppermute | solution.py:18
  70.8 19.6 %collective-permute-start.24 = (f32[3,8,16,256]{3,2,1,0:T(8,128)S(1)}, f32[3,8,16,256]{3,2,1,0:T(8,128)S(1)}, u32[]{:S(2)}, u32[]{:S(2)}) collective-permute-start(f32[3,8,16,256]{3,2,1,0:T(8,128)S(1)} %add_bitcast_fusion.1.refs_3_), channel_id=1, source_target_pairs={{0,4},{4,0},{1,5},{5,1},{2,6},{6,2},{3,7},{7,3},{8,12},{12,8},{9,1... | collective-permute-start | bytes 1179656 | tf_op jit(solution)/shard_map/ppermute | solution.py:18
  71.7 8.4 %collective-permute-start.22 = (f32[1,1,8,16,256]{4,3,2,1,0:T(8,128)S(1)}, f32[1,1,8,16,256]{4,3,2,1,0:T(8,128)S(1)}, u32[]{:S(2)}, u32[]{:S(2)}) collective-permute-start(f32[1,1,8,16,256]{4,3,2,1,0:T(8,128)S(1)} %get-tuple-element.111), channel_id=1, source_target_pairs={{0,16},{8,24},{16,0},{24,8},{1,17},{9,25},{17,1},{25,9},{2,18},{10... | collective-permute-start | bytes 393224 | tf_op jit(solution)/shard_map/ppermute | solution.py:18
  74.1 8.1 %collective-permute-start.17 = (f32[2,4,64,128]{3,2,1,0:T(8,128)S(1)}, f32[2,4,64,128]{3,2,1,0:T(8,128)S(1)}, u32[]{:S(2)}, u32[]{:S(2)}) collective-permute-start(f32[2,4,64,128]{3,2,1,0:T(8,128)S(1)} %dynamic-slice_bitcast_fusion.2), channel_id=1, source_target_pairs={{0,8},{8,0},{16,24},{24,16},{1,9},{9,1},{17,25},{25,17},{2,10},{10... | collective-permute-start | bytes 786440 | tf_op jit(solution)/shard_map/ppermute | solution.py:18
  77.9 15.8 %collective-permute-start.23 = (f32[3,8,16,256]{3,2,1,0:T(8,128)S(1)}, f32[3,8,16,256]{3,2,1,0:T(8,128)S(1)}, u32[]{:S(2)}, u32[]{:S(2)}) collective-permute-start(f32[3,8,16,256]{3,2,1,0:T(8,128)S(1)} %add_bitcast_fusion.refs_3_), channel_id=1, source_target_pairs={{0,4},{4,0},{1,5},{5,1},{2,6},{6,2},{3,7},{7,3},{8,12},{12,8},{9,1... | collective-permute-start | bytes 1179656 | tf_op jit(solution)/shard_map/ppermute | solution.py:18
  79.5 8.2 %collective-permute-start.29 = (f32[1,2,8,16,256]{4,3,2,1,0:T(8,128)S(1)}, f32[1,2,8,16,256]{4,3,2,1,0:T(8,128)S(1)}, u32[]{:S(2)}, u32[]{:S(2)}) collective-permute-start(f32[1,2,8,16,256]{4,3,2,1,0:T(8,128)S(1)} %pad_maximum_fusion.5), channel_id=1, source_target_pairs={{0,16},{8,24},{16,0},{24,8},{1,17},{9,25},{17,1},{25,9},{2,18},{10... | collective-permute-start | bytes 786440 | tf_op jit(solution)/shard_map/ppermute | solution.py:18
  80.1 23.1 %collective-permute-start.34 = (f32[1,8,16,256]{3,2,1,0:T(8,128)S(1)}, f32[1,8,16,256]{3,2,1,0:T(8,128)S(1)}, u32[]{:S(2)}, u32[]{:S(2)}) collective-permute-start(f32[1,8,16,256]{3,2,1,0:T(8,128)S(1)} %add_bitcast_fusion.11.refs_4_), channel_id=1, source_target_pairs={{0,4},{4,0},{1,5},{5,1},{2,6},{6,2},{3,7},{7,3},{8,12},{12,8},{9,1... | collective-permute-start | bytes 393224 | tf_op jit(solution)/shard_map/ppermute | solution.py:18
  82.2 13.8 %collective-permute-start.30 = (f32[1,2,8,16,256]{4,3,2,1,0:T(8,128)S(1)}, f32[1,2,8,16,256]{4,3,2,1,0:T(8,128)S(1)}, u32[]{:S(2)}, u32[]{:S(2)}) collective-permute-start(f32[1,2,8,16,256]{4,3,2,1,0:T(8,128)S(1)} %pad_maximum_fusion.4), channel_id=1, source_target_pairs={{0,16},{8,24},{16,0},{24,8},{1,17},{9,25},{17,1},{25,9},{2,18},{10... | collective-permute-start | bytes 786440 | tf_op jit(solution)/shard_map/ppermute | solution.py:18
  87.7 8.5 %collective-permute-start.18 = (f32[2,2,64,128]{3,2,1,0:T(8,128)S(1)}, f32[2,2,64,128]{3,2,1,0:T(8,128)S(1)}, u32[]{:S(2)}, u32[]{:S(2)}) collective-permute-start(f32[2,2,64,128]{3,2,1,0:T(8,128)S(1)} %dynamic-slice_bitcast_fusion.4), channel_id=1, source_target_pairs={{0,2},{1,3},{2,0},{3,1},{4,6},{5,7},{6,4},{7,5},{8,10},{9,11},{10,... | collective-permute-start | bytes 393224 | tf_op jit(solution)/shard_map/ppermute | solution.py:18
  90.3 12.9 %collective-permute-start.35 = (f32[2,8,16,256]{3,2,1,0:T(8,128)S(1)}, f32[2,8,16,256]{3,2,1,0:T(8,128)S(1)}, u32[]{:S(2)}, u32[]{:S(2)}) collective-permute-start(f32[2,8,16,256]{3,2,1,0:T(8,128)S(1)} %add_bitcast_fusion.3.refs_5_), channel_id=1, source_target_pairs={{0,4},{4,0},{1,5},{5,1},{2,6},{6,2},{3,7},{7,3},{8,12},{12,8},{9,1... | collective-permute-start | bytes 786440 | tf_op jit(solution)/shard_map/ppermute | solution.py:18
  93.7 5.0 %collective-permute-start.31 = (f32[1,1,8,16,256]{4,3,2,1,0:T(8,128)S(1)}, f32[1,1,8,16,256]{4,3,2,1,0:T(8,128)S(1)}, u32[]{:S(2)}, u32[]{:S(2)}) collective-permute-start(f32[1,1,8,16,256]{4,3,2,1,0:T(8,128)S(1)} %get-tuple-element.125), channel_id=1, source_target_pairs={{0,16},{8,24},{16,0},{24,8},{1,17},{9,25},{17,1},{25,9},{2,18},{10... | collective-permute-start | bytes 393224 | tf_op jit(solution)/shard_map/ppermute | solution.py:18
  96.2 11.6 %collective-permute-start.32 = (f32[2,8,16,256]{3,2,1,0:T(8,128)S(1)}, f32[2,8,16,256]{3,2,1,0:T(8,128)S(1)}, u32[]{:S(2)}, u32[]{:S(2)}) collective-permute-start(f32[2,8,16,256]{3,2,1,0:T(8,128)S(1)} %add_bitcast_fusion.2.refs_4_), channel_id=1, source_target_pairs={{0,4},{4,0},{1,5},{5,1},{2,6},{6,2},{3,7},{7,3},{8,12},{12,8},{9,1... | collective-permute-start | bytes 786440 | tf_op jit(solution)/shard_map/ppermute | solution.py:18
  100.4 7.3 %collective-permute-start.33 = (f32[1,8,16,256]{3,2,1,0:T(8,128)S(1)}, f32[1,8,16,256]{3,2,1,0:T(8,128)S(1)}, u32[]{:S(2)}, u32[]{:S(2)}) collective-permute-start(f32[1,8,16,256]{3,2,1,0:T(8,128)S(1)} %add_bitcast_fusion.10.refs_5_), channel_id=1, source_target_pairs={{0,4},{4,0},{1,5},{5,1},{2,6},{6,2},{3,7},{7,3},{8,12},{12,8},{9,1... | collective-permute-start | bytes 393224 | tf_op jit(solution)/shard_map/ppermute | solution.py:18
  103.0 9.1 %collective-permute-start.26 = (f32[2,2,80,128]{3,2,1,0:T(8,128)S(1)}, f32[2,2,80,128]{3,2,1,0:T(8,128)S(1)}, u32[]{:S(2)}, u32[]{:S(2)}) collective-permute-start(f32[2,2,80,128]{3,2,1,0:T(8,128)S(1)} %dynamic-slice_bitcast_fusion.3), channel_id=1, source_target_pairs={{0,2},{1,3},{2,0},{3,1},{4,6},{5,7},{6,4},{7,5},{8,10},{9,11},{10,... | collective-permute-start | bytes 491528 | tf_op jit(solution)/shard_map/ppermute | solution.py:18
  110.2 7.0 %collective-permute-start.36 = (f32[2,4,112,128]{3,2,1,0:T(8,128)S(1)}, f32[2,4,112,128]{3,2,1,0:T(8,128)S(1)}, u32[]{:S(2)}, u32[]{:S(2)}) collective-permute-start(f32[2,4,112,128]{3,2,1,0:T(8,128)S(1)} %dynamic-slice_bitcast_fusion), channel_id=1, source_target_pairs={{0,8},{8,0},{16,24},{24,16},{1,9},{9,1},{17,25},{25,17},{2,10},{10... | collective-permute-start | bytes 1376264 | tf_op jit(solution)/shard_map/ppermute | solution.py:18
  112.3 9.3 %collective-permute-start.20 = (f32[64,128]{1,0:T(8,128)S(1)}, f32[64,128]{1,0:T(8,128)S(1)}, u32[]{:S(2)}, u32[]{:S(2)}) collective-permute-start(f32[64,128]{1,0:T(8,128)S(1)} %dynamic-slice_bitcast_fusion.6), channel_id=1, source_target_pairs={{0,16},{8,24},{16,0},{24,8},{1,17},{9,25},{17,1},{25,9},{2,18},{10... | collective-permute-start | bytes 98312 | tf_op jit(solution)/shard_map/ppermute | solution.py:18
  118.0 16.2 %all-to-all-start = ((f32[8,112,128]{2,1,0:T(8,128)}), f32[8,112,128]{2,1,0:T(8,128)S(1)}, u32[]{:S(2)}, u32[]{:S(2)}) async-start(f32[8,112,128]{2,1,0:T(8,128)} %bitcast.99), calls=%async_computation | async-start | bytes 917504 | tf_op jit(solution)/shard_map/all_to_all | solution.py:206
  (8 other events, 27.1 us)

commit v6 on v5

--- a/solution.py
+++ b/solution.py
@@ -191,10 +191,13 @@
         leaving = lax.dynamic_index_in_dim(halves, side ^ 1, 1, keepdims=False)
         t = lax.dynamic_index_in_dim(halves, side, 1, keepdims=False) + swap(leaving, "col", bit)
         bit //= 2
-    total = t[:, 0]
-    places = total.shape[0]
+    return t[:, 0]
+
+
+def block_over_x(total):
+    me_x = lax.axis_index("aa") >> 1
     mine = lax.dynamic_index_in_dim(total, me_x, 0, keepdims=False)
-    for d in range(1, places):
+    for d in range(1, total.shape[0]):
         mine = mine + swap(lax.dynamic_index_in_dim(total, me_x ^ d, 0, keepdims=False), "aa", 2 * d)
     return mine
 
@@ -271,7 +274,7 @@
     steps = [(i, group) for i in range(len(widths)) for group in groups_of(i)]
     pieces = {}
     regions, blocks = [None] * len(widths), []
-    arrived, passed, waiting, halfway, leaving_of = [], [], [], [], {}
+    arrived, passed, waiting, halfway, early, leaving_of = [], [], [], [], [], {}
 
     def add_gram(i, group, *after):
         used = [
@@ -282,7 +285,16 @@
             region = regions[i].reshape(aa, col, *regions[i].shape[2:])
             summed = summed_over_core(region)
             halfway.append(summed)
-            blocks.append(block_by_permutes(summed) if i < len(widths) - 1 else block_by_all_to_all(summed))
+            if i < len(widths) - 1:
+                early.append(block_by_permutes(summed))
+            if i == len(widths) - 2:
+                joined = block_over_x(jnp.concatenate(early, axis=1))
+                rows = [0]
+                for x in early:
+                    rows.append(rows[-1] + x.shape[1])
+                blocks.extend(joined[low:high] for low, high in zip(rows, rows[1:]))
+            if i == len(widths) - 1:
+                blocks.append(block_by_all_to_all(summed))
 
     def send(n):
         i, group = steps[n]

time: 136 us -> 136 us (level)
  waiting for transfers between devices: 47.7 us -> 45 us
  starting transfers between devices: 43.5 us -> 45.9 us
    all_to_all x1, waiting for transfers between devices: 12 us -> 7.41 us  [block_by_all_to_all(): lax.all_to_all(t, ('aa', 'col'), 0, 0, tiled=True, axis_index_groups=groups)]
    ppermute x37 -> x36, starting transfers between devices: 40 us -> 42 us  [swap(): lax.ppermute(x, axis, [(i, i ^ bit) for i in range(lax.axis_size(axis))])]
    ppermute x37 -> x36, waiting for transfers between devices: 35.7 us -> 37.6 us  [swap(): lax.ppermute(x, axis, [(i, i ^ bit) for i in range(lax.axis_size(axis))])]
  transfers between devices with their start and end apart: 38 -> 37, of which waited for: 14 -> 13; matrix products, arithmetic and copies ran while one was open for 3% -> 2% of each run, Pallas kernels for 20% -> 20%
where the time goes in v6:
time: 136 us; the launch traced here: 135 us
  starting transfers between devices  45.9 us (34%)
  waiting for transfers between devices  45 us (33%)
  Pallas kernels  38 us (28%)
  local copies, waits for them, and re-layouts  2.96 us (2%)
  other arithmetic  2.85 us (2%)
    ppermute x36, starting transfers between devices, swap(): lax.ppermute(x, axis, [(i, i ^ bit) for i in range(lax.axis_size(axis))])  42 us
    ppermute x36, waiting for transfers between devices, swap(): lax.ppermute(x, axis, [(i, i ^ bit) for i in range(lax.axis_size(axis))])  37.6 us
    pallas_call x7, Pallas kernels, truncated(): pl.pallas_call(functools.partial(truncate_kernel, cuts, sizes), grid_spec...  20.3 us
    pallas_call x6, Pallas kernels, gram_strip(): pl.pallas_call(functools.partial(gram_kernel, ba, widths, counts, unit, l...  9.89 us
    pallas_call x3, Pallas kernels, gathered(): pl.pallas_call(gather_kernel, in_specs=[pl.BlockSpec(memory_space=pltpu.S...  7.83 us
    all_to_all x1, waiting for transfers between devices, block_by_all_to_all(): lax.all_to_all(t, ('aa', 'col'), 0, 0, tiled=True, axis_index_groups=groups)  7.41 us
    all_to_all x1, starting transfers between devices, block_by_all_to_all(): lax.all_to_all(t, ('aa', 'col'), 0, 0, tiled=True, axis_index_groups=groups)  3.89 us
  transfers between devices with their start and end apart: 37, of which 13 were waited for; matrix products, arithmetic and copies ran while one was open for 2% of the time, Pallas kernels for 20%

profile of v6, /device:TPU:0, one launch (start us, length us, event | category | flops | bytes accessed | tf_op | source)
XLA Modules:
  0.0 135.4 jit_solution(10706133295471984753)
XLA Ops:
  0.1 1.8 %shard_map.28 = f32[2,256,512]{2,1,0:T(8,128)S(1)} custom-call(s32[2]{0:T(128)S(1)} %pad_add_fusion.layers_ref, f32[24,256,512]{2,1,0:T(8,128)} %refs_0_.13), custom_call_target="tpu_custom_call" | custom-call | tf_op jit(solution)/shard_map/pallas_call | solution.py:50
  2.6 2.5 %collective-permute-done.1.refs_3_ = f32[256,256]{1,0:T(8,128)S(1)} collective-permute-done((f32[256,256]{1,0:T(8,128)S(1)}, f32[256,256]{1,0:T(8,128)S(1)}, u32[]{:S(2)}, u32[]{:S(2)}) %collective-permute-start.1) | collective-permute-done | bytes 262176 | tf_op jit(solution)/shard_map/ppermute | solution.py:18
  5.1 2.2 %shard_map.29 = (f32[1,8,32,256]{3,2,1,0:T(8,128)S(1)}, f32[1,8,32,256]{3,2,1,0:T(8,128)S(1)}) custom-call(s32[2]{0:T(128)S(1)} %get-tuple-element.157._, f32[24,256,512]{2,1,0:T(8,128)} %refs_0_.13, f32[2,256,512]{2,1,0:T(8,128)S(1)} %collective-permute-done.refs_1_, f32[256,256]{1,0:T(8,128)S(1)} %copy-done, f32[256,256]{1,0:T(8,128)S(1)} %collective-permute-done.1.refs_3_), custom_call_target="tpu_custom_call" | custom-call | tf_op jit(solution)/shard_map/pallas_call | solution.py:91
  8.1 2.2 %shard_map.30 = (f32[1,8,32,256]{3,2,1,0:T(8,128)S(1)}, f32[1,8,32,256]{3,2,1,0:T(8,128)S(1)}) custom-call(s32[2]{0:T(128)S(1)} %pad_add_fusion.2._, f32[24,256,512]{2,1,0:T(8,128)} %refs_0_.13, f32[2,256,512]{2,1,0:T(8,128)S(1)} %collective-permute-done.refs_1_, f32[256,256]{1,0:T(8,128)S(1)} %copy-done, f32[256,256]{1,0:T(8,128)S(1)} %collective-permute-done.1.refs_3_), custom_call_target="tpu_custom_call" | custom-call | tf_op jit(solution)/shard_map/pallas_call | solution.py:91
  10.4 4.2 %shard_map.33 = f32[8,256,512]{2,1,0:T(8,128)} custom-call(s32[8]{0:T(128)S(1)} %stack.154.layers_ref, f32[24,256,512]{2,1,0:T(8,128)} %refs_0_.13), custom_call_target="tpu_custom_call" | custom-call | tf_op jit(solution)/shard_map/pallas_call | solution.py:50
  15.1 1.8 %shard_map.31 = f32[2,256,512]{2,1,0:T(8,128)S(1)} custom-call(s32[2]{0:T(128)S(1)} %pad_add_fusion.5.layers_ref, f32[24,256,512]{2,1,0:T(8,128)} %refs_0_.13), custom_call_target="tpu_custom_call" | custom-call | tf_op jit(solution)/shard_map/pallas_call | solution.py:50
  17.5 2.9 %collective-permute-start.3 = (f32[1,1,8,32,256]{4,3,2,1,0:T(8,128)}, f32[1,1,8,32,256]{4,3,2,1,0:T(8,128)S(1)}, u32[]{:S(2)}, u32[]{:S(2)}) collective-permute-start(f32[1,1,8,32,256]{4,3,2,1,0:T(8,128)} %bitcast.193), channel_id=1, source_target_pairs={{0,16},{8,24},{16,0},{24,8},{1,17},{9,25},{17,1},{25,9},{2,18},{10... | collective-permute-start | bytes 786440 | tf_op jit(solution)/shard_map/ppermute | solution.py:18
  20.5 2.9 %collective-permute-done.2.refs_1_ = f32[2,256,512]{2,1,0:T(8,128)S(1)} collective-permute-done((f32[2,256,512]{2,1,0:T(8,128)S(1)}, f32[2,256,512]{2,1,0:T(8,128)S(1)}, u32[]{:S(2)}, u32[]{:S(2)}) %collective-permute-start.2) | collective-permute-done | bytes 1048608 | tf_op jit(solution)/shard_map/ppermute | solution.py:18
  23.4 3.0 %shard_map.32 = (f32[1,8,32,256]{3,2,1,0:T(8,128)S(1)}, f32[1,8,32,256]{3,2,1,0:T(8,128)S(1)}, f32[1,8,32,256]{3,2,1,0:T(8,128)S(1)}, f32[1,8,32,256]{3,2,1,0:T(8,128)S(1)}) custom-call(s32[4]{0:T(128)S(1)} %pad_add_fusion.4._, f32[24,256,512]{2,1,0:T(8,128)} %refs_0_.13, f32[2,256,512]{2,1,0:T(8,128)S(1)} %collective-permute-done.2.refs_1_, ...), custom_call_target="tpu_custom_call" | custom-call | tf_op jit(solution)/shard_map/pallas_call | solution.py:91
  26.3 2.9 %collective-permute-start.5 = (f32[1,1,8,32,256]{4,3,2,1,0:T(8,128)S(1)}, f32[1,1,8,32,256]{4,3,2,1,0:T(8,128)S(1)}, u32[]{:S(2)}, u32[]{:S(2)}) collective-permute-start(f32[1,1,8,32,256]{4,3,2,1,0:T(8,128)S(1)} %bitcast.198), channel_id=1, source_target_pairs={{0,16},{8,24},{16,0},{24,8},{1,17},{9,25},{17,1},{25,9},{2,18},{10... | collective-permute-start | bytes 786440 | tf_op jit(solution)/shard_map/ppermute | solution.py:18
  31.0 3.2 %shard_map.34 = (f32[1,8,32,256]{3,2,1,0:T(8,128)S(1)}, f32[1,8,32,256]{3,2,1,0:T(8,128)S(1)}, f32[1,8,32,256]{3,2,1,0:T(8,128)S(1)}, f32[1,8,32,256]{3,2,1,0:T(8,128)S(1)}) custom-call(s32[4]{0:T(128)S(1)} %pad_add_fusion.7._, f32[24,256,512]{2,1,0:T(8,128)} %refs_0_.13, f32[8,256,512]{2,1,0:T(8,128)} %collective-permute-done.4.refs_1_, ...), custom_call_target="tpu_custom_call" | custom-call | tf_op jit(solution)/shard_map/pallas_call | solution.py:91
  35.9 2.5 %collective-permute-start.10 = (f32[1,8,32,256]{3,2,1,0:T(8,128)S(1)}, f32[1,8,32,256]{3,2,1,0:T(8,128)S(1)}, u32[]{:S(2)}, u32[]{:S(2)}) collective-permute-start(f32[1,8,32,256]{3,2,1,0:T(8,128)S(1)} %add_bitcast_fusion.8.refs_1_), channel_id=1, source_target_pairs={{0,4},{4,0},{1,5},{5,1},{2,6},{6,2},{3,7},{7,3},{8,12},{12,8},{9,1... | collective-permute-start | bytes 786440 | tf_op jit(solution)/shard_map/ppermute | solution.py:18
  38.5 3.2 %shard_map.35 = (f32[1,8,32,256]{3,2,1,0:T(8,128)S(1)}, f32[1,8,32,256]{3,2,1,0:T(8,128)S(1)}, f32[1,8,32,256]{3,2,1,0:T(8,128)S(1)}, f32[1,8,32,256]{3,2,1,0:T(8,128)S(1)}) custom-call(s32[4]{0:T(128)S(1)} %pad_add_fusion.9._, f32[24,256,512]{2,1,0:T(8,128)} %refs_0_.13, f32[8,256,512]{2,1,0:T(8,128)} %collective-permute-done.4.refs_1_, ...), custom_call_target="tpu_custom_call" | custom-call | tf_op jit(solution)/shard_map/pallas_call | solution.py:91
  41.6 1.7 %collective-permute-start.7 = (f32[1,1,8,32,256]{4,3,2,1,0:T(8,128)S(1)}, f32[1,1,8,32,256]{4,3,2,1,0:T(8,128)S(1)}, u32[]{:S(2)}, u32[]{:S(2)}) collective-permute-start(f32[1,1,8,32,256]{4,3,2,1,0:T(8,128)S(1)} %bitcast.194), channel_id=1, source_target_pairs={{0,16},{8,24},{16,0},{24,8},{1,17},{9,25},{17,1},{25,9},{2,18},{10... | collective-permute-start | bytes 786440 | tf_op jit(solution)/shard_map/ppermute | solution.py:18
  44.1 3.2 %shard_map.36 = (f32[1,8,32,256]{3,2,1,0:T(8,128)S(1)}, f32[1,8,32,256]{3,2,1,0:T(8,128)S(1)}, f32[1,8,32,256]{3,2,1,0:T(8,128)S(1)}, f32[1,8,32,256]{3,2,1,0:T(8,128)S(1)}) custom-call(s32[4]{0:T(128)S(1)} %pad_add_fusion.11._, f32[24,256,512]{2,1,0:T(8,128)} %refs_0_.13, f32[8,256,512]{2,1,0:T(8,128)} %collective-permute-done.4.refs_1_, ...), custom_call_target="tpu_custom_call" | custom-call | tf_op jit(solution)/shard_map/pallas_call | solution.py:91
  49.6 3.3 %shard_map.37 = (f32[1,8,32,256]{3,2,1,0:T(8,128)S(1)}, f32[1,8,32,256]{3,2,1,0:T(8,128)S(1)}, f32[1,8,32,256]{3,2,1,0:T(8,128)S(1)}, f32[1,8,32,256]{3,2,1,0:T(8,128)S(1)}) custom-call(s32[4]{0:T(128)S(1)} %pad_add_fusion.13._, f32[24,256,512]{2,1,0:T(8,128)} %refs_0_.13, f32[8,256,512]{2,1,0:T(8,128)} %collective-permute-done.4.refs_1_, ...), custom_call_target="tpu_custom_call" | custom-call | tf_op jit(solution)/shard_map/pallas_call | solution.py:91
  56.6 5.6 %collective-permute-done.11 = f32[1,1,8,32,256]{4,3,2,1,0:T(8,128)S(1)} collective-permute-done((f32[1,1,8,32,256]{4,3,2,1,0:T(8,128)S(1)}, f32[1,1,8,32,256]{4,3,2,1,0:T(8,128)S(1)}, u32[]{:S(2)}, u32[]{:S(2)}) %collective-permute-start.11) | collective-permute-done | bytes 262176 | tf_op jit(solution)/shard_map/ppermute | solution.py:18
  65.6 5.1 %collective-permute-done.13 = f32[1,3,8,16,256]{4,3,2,1,0:T(8,128)S(1)} collective-permute-done((f32[1,3,8,16,256]{4,3,2,1,0:T(8,128)S(1)}, f32[1,3,8,16,256]{4,3,2,1,0:T(8,128)S(1)}, u32[]{:S(2)}, u32[]{:S(2)}) %collective-permute-start.13) | collective-permute-done | bytes 393248 | tf_op jit(solution)/shard_map/ppermute | solution.py:18
  74.2 3.6 %collective-permute-done.20 = f32[1,3,8,16,256]{4,3,2,1,0:T(8,128)S(1)} collective-permute-done((f32[1,3,8,16,256]{4,3,2,1,0:T(8,128)S(1)}, f32[1,3,8,16,256]{4,3,2,1,0:T(8,128)S(1)}, u32[]{:S(2)}, u32[]{:S(2)}) %collective-permute-start.20) | collective-permute-done | bytes 393248 | tf_op jit(solution)/shard_map/ppermute | solution.py:18
  80.1 2.1 %collective-permute-start.33 = (f32[1,8,16,256]{3,2,1,0:T(8,128)S(1)}, f32[1,8,16,256]{3,2,1,0:T(8,128)S(1)}, u32[]{:S(2)}, u32[]{:S(2)}) collective-permute-start(f32[1,8,16,256]{3,2,1,0:T(8,128)S(1)} %add_bitcast_fusion.11.refs_4_), channel_id=1, source_target_pairs={{0,4},{4,0},{1,5},{5,1},{2,6},{6,2},{3,7},{7,3},{8,12},{12,8},{9,1... | collective-permute-start | bytes 393224 | tf_op jit(solution)/shard_map/ppermute | solution.py:18
  82.9 4.8 %collective-permute-done.28 = f32[1,2,8,16,256]{4,3,2,1,0:T(8,128)S(1)} collective-permute-done((f32[1,2,8,16,256]{4,3,2,1,0:T(8,128)S(1)}, f32[1,2,8,16,256]{4,3,2,1,0:T(8,128)S(1)}, u32[]{:S(2)}, u32[]{:S(2)}) %collective-permute-start.28) | collective-permute-done | bytes 262176 | tf_op jit(solution)/shard_map/ppermute | solution.py:18
  87.7 2.6 %collective-permute-start.18 = (f32[2,2,64,128]{3,2,1,0:T(8,128)S(1)}, f32[2,2,64,128]{3,2,1,0:T(8,128)S(1)}, u32[]{:S(2)}, u32[]{:S(2)}) collective-permute-start(f32[2,2,64,128]{3,2,1,0:T(8,128)S(1)} %dynamic-slice_bitcast_fusion.4), channel_id=1, source_target_pairs={{0,2},{1,3},{2,0},{3,1},{4,6},{5,7},{6,4},{7,5},{8,10},{9,11},{10,... | collective-permute-start | bytes 393224 | tf_op jit(solution)/shard_map/ppermute | solution.py:18
  91.9 1.7 %shard_map.40.refs_8_ = f32[2,8,80,128]{3,2,1,0:T(8,128)S(1)} custom-call(s32[1]{0:T(128)} %bitcast.77.me_ref, f32[1,8,32,256]{3,2,1,0:T(8,128)S(1)} %add_bitcast_fusion.9.refs_0_, f32[1,8,32,256]{3,2,1,0:T(8,128)S(1)} %add_bitcast_fusion.8.refs_1_, f32[1,8,32,256]{3,2,1,0:T(8,128)S(1)} %add_bitcast_fusion.7.refs_2_, ...), custom_call_target="tpu_custom_call" | custom-call | tf_op jit(solution)/shard_map/pallas_call | solution.py:155
  94.2 1.7 %shard_map.41 = f32[2,8,80,128]{3,2,1,0:T(8,128)S(1)} custom-call(s32[1]{0:T(128)} %bitcast.76.me_ref, f32[1,8,32,256]{3,2,1,0:T(8,128)S(1)} %add_bitcast_fusion.6.refs_0_, f32[1,8,32,256]{3,2,1,0:T(8,128)S(1)} %add_bitcast_fusion.5.refs_1_, f32[1,8,32,256]{3,2,1,0:T(8,128)S(1)} %add_bitcast_fusion.4.refs_2_, ...), custom_call_target="tpu_custom_call", output_to_operand_aliasing={{}: (9, {})} | custom-call | tf_op jit(solution)/shard_map/pallas_call | solution.py:155
  101.4 2.3 %shard_map.42.refs_12_ = f32[2,8,112,128]{3,2,1,0:T(8,128)S(1)} custom-call(s32[1]{0:T(128)} %bitcast.95.me_ref, f32[1,8,32,256]{3,2,1,0:T(8,128)S(1)} %add_bitcast_fusion.9.refs_0_, f32[1,8,32,256]{3,2,1,0:T(8,128)S(1)} %add_bitcast_fusion.8.refs_1_, f32[1,8,32,256]{3,2,1,0:T(8,128)S(1)} %add_bitcast_fusion.7.refs_2_, ...), custom_call_target="tpu_custom_call" | custom-call | tf_op jit(solution)/shard_map/pallas_call | solution.py:155
  103.8 4.0 %collective-permute-done.32.refs_11_ = f32[1,8,16,256]{3,2,1,0:T(8,128)S(1)} collective-permute-done((f32[1,8,16,256]{3,2,1,0:T(8,128)S(1)}, f32[1,8,16,256]{3,2,1,0:T(8,128)S(1)}, u32[]{:S(2)}, u32[]{:S(2)}) %collective-permute-start.32) | collective-permute-done | bytes 131104 | tf_op jit(solution)/shard_map/ppermute | solution.py:18
  107.7 2.4 %shard_map.43 = f32[2,8,112,128]{3,2,1,0:T(8,128)S(1)} custom-call(s32[1]{0:T(128)} %bitcast.91.me_ref, f32[1,8,32,256]{3,2,1,0:T(8,128)S(1)} %add_bitcast_fusion.6.refs_0_, f32[1,8,32,256]{3,2,1,0:T(8,128)S(1)} %add_bitcast_fusion.5.refs_1_, f32[1,8,32,256]{3,2,1,0:T(8,128)S(1)} %add_bitcast_fusion.4.refs_2_, ...), custom_call_target="tpu_custom_call", output_to_operand_aliasing={{}: (13, {})} | custom-call | tf_op jit(solution)/shard_map/pallas_call | solution.py:155
  112.0 3.2 %collective-permute-done.26 = f32[2,1,80,128]{3,2,1,0:T(8,128)S(1)} collective-permute-done((f32[2,1,80,128]{3,2,1,0:T(8,128)S(1)}, f32[2,1,80,128]{3,2,1,0:T(8,128)S(1)}, u32[]{:S(2)}, u32[]{:S(2)}) %collective-permute-start.26) | collective-permute-done | bytes 81952 | tf_op jit(solution)/shard_map/ppermute | solution.py:18
  116.1 3.9 %all-to-all-start = ((f32[8,112,128]{2,1,0:T(8,128)}), f32[8,112,128]{2,1,0:T(8,128)S(1)}, u32[]{:S(2)}, u32[]{:S(2)}) async-start(f32[8,112,128]{2,1,0:T(8,128)} %bitcast.99), calls=%async_computation | async-start | bytes 917504 | tf_op jit(solution)/shard_map/all_to_all | solution.py:209
  120.0 2.1 %collective-permute-start.27 = (f32[144,128]{1,0:T(8,128)S(1)}, f32[144,128]{1,0:T(8,128)S(1)}, u32[]{:S(2)}, u32[]{:S(2)}) collective-permute-start(f32[144,128]{1,0:T(8,128)S(1)} %fusion.1), channel_id=1, source_target_pairs={{0,16},{8,24},{16,0},{24,8},{1,17},{9,25},{17,1},{25,9},{2,18},{10... | collective-permute-start | bytes 221192 | tf_op jit(solution)/shard_map/ppermute | solution.py:18
  122.0 3.7 %collective-permute-done.27 = f32[144,128]{1,0:T(8,128)S(1)} collective-permute-done((f32[144,128]{1,0:T(8,128)S(1)}, f32[144,128]{1,0:T(8,128)S(1)}, u32[]{:S(2)}, u32[]{:S(2)}) %collective-permute-start.27) | collective-permute-done | bytes 73760 | tf_op jit(solution)/shard_map/ppermute | solution.py:18
  126.4 7.4 %all-to-all-done = f32[8,112,128]{2,1,0:T(8,128)S(1)} async-done(((f32[8,112,128]{2,1,0:T(8,128)}), f32[8,112,128]{2,1,0:T(8,128)S(1)}, u32[]{:S(2)}, u32[]{:S(2)}) %all-to-all-start) | async-done | bytes 458784 | tf_op jit(solution)/shard_map/all_to_all | solution.py:209
  (146 shorter events, 34.9 us)
Async XLA Ops:
  14.6 16.4 %collective-permute-start.4 = (f32[8,256,512]{2,1,0:T(8,128)}, f32[8,256,512]{2,1,0:T(8,128)}, u32[]{:S(2)}, u32[]{:S(2)}) collective-permute-start(f32[8,256,512]{2,1,0:T(8,128)} %shard_map.33), channel_id=1, source_target_pairs={{0,8},{8,0},{16,24},{24,16},{1,9},{9,1},{17,25},{25,17},{2,10},{10... | collective-permute-start | bytes 12582920 | tf_op jit(solution)/shard_map/ppermute | solution.py:18
  17.0 6.4 %collective-permute-start.2 = (f32[2,256,512]{2,1,0:T(8,128)S(1)}, f32[2,256,512]{2,1,0:T(8,128)S(1)}, u32[]{:S(2)}, u32[]{:S(2)}) collective-permute-start(f32[2,256,512]{2,1,0:T(8,128)S(1)} %shard_map.31), channel_id=1, source_target_pairs={{0,8},{8,0},{16,24},{24,16},{1,9},{9,1},{17,25},{25,17},{2,10},{10... | collective-permute-start | bytes 3145736 | tf_op jit(solution)/shard_map/ppermute | solution.py:18
  17.5 11.8 %collective-permute-start.3 = (f32[1,1,8,32,256]{4,3,2,1,0:T(8,128)}, f32[1,1,8,32,256]{4,3,2,1,0:T(8,128)S(1)}, u32[]{:S(2)}, u32[]{:S(2)}) collective-permute-start(f32[1,1,8,32,256]{4,3,2,1,0:T(8,128)} %bitcast.193), channel_id=1, source_target_pairs={{0,16},{8,24},{16,0},{24,8},{1,17},{9,25},{17,1},{25,9},{2,18},{10... | collective-permute-start | bytes 786440 | tf_op jit(solution)/shard_map/ppermute | solution.py:18
  26.3 9.5 %collective-permute-start.5 = (f32[1,1,8,32,256]{4,3,2,1,0:T(8,128)S(1)}, f32[1,1,8,32,256]{4,3,2,1,0:T(8,128)S(1)}, u32[]{:S(2)}, u32[]{:S(2)}) collective-permute-start(f32[1,1,8,32,256]{4,3,2,1,0:T(8,128)S(1)} %bitcast.198), channel_id=1, source_target_pairs={{0,16},{8,24},{16,0},{24,8},{1,17},{9,25},{17,1},{25,9},{2,18},{10... | collective-permute-start | bytes 786440 | tf_op jit(solution)/shard_map/ppermute | solution.py:18
  29.3 23.6 %collective-permute-start.8 = (f32[1,8,32,256]{3,2,1,0:T(8,128)S(1)}, f32[1,8,32,256]{3,2,1,0:T(8,128)S(1)}, u32[]{:S(2)}, u32[]{:S(2)}) collective-permute-start(f32[1,8,32,256]{3,2,1,0:T(8,128)S(1)} %add_bitcast_fusion.9.refs_0_), channel_id=1, source_target_pairs={{0,4},{4,0},{1,5},{5,1},{2,6},{6,2},{3,7},{7,3},{8,12},{12,8},{9,1... | collective-permute-start | bytes 786440 | tf_op jit(solution)/shard_map/ppermute | solution.py:18
  34.2 9.4 %collective-permute-start.6 = (f32[1,1,8,32,256]{4,3,2,1,0:T(8,128)S(1)}, f32[1,1,8,32,256]{4,3,2,1,0:T(8,128)S(1)}, u32[]{:S(2)}, u32[]{:S(2)}) collective-permute-start(f32[1,1,8,32,256]{4,3,2,1,0:T(8,128)S(1)} %bitcast.195), channel_id=1, source_target_pairs={{0,16},{8,24},{16,0},{24,8},{1,17},{9,25},{17,1},{25,9},{2,18},{10... | collective-permute-start | bytes 786440 | tf_op jit(solution)/shard_map/ppermute | solution.py:18
  35.9 19.0 %collective-permute-start.10 = (f32[1,8,32,256]{3,2,1,0:T(8,128)S(1)}, f32[1,8,32,256]{3,2,1,0:T(8,128)S(1)}, u32[]{:S(2)}, u32[]{:S(2)}) collective-permute-start(f32[1,8,32,256]{3,2,1,0:T(8,128)S(1)} %add_bitcast_fusion.8.refs_1_), channel_id=1, source_target_pairs={{0,4},{4,0},{1,5},{5,1},{2,6},{6,2},{3,7},{7,3},{8,12},{12,8},{9,1... | collective-permute-start | bytes 786440 | tf_op jit(solution)/shard_map/ppermute | solution.py:18
  41.6 6.7 %collective-permute-start.7 = (f32[1,1,8,32,256]{4,3,2,1,0:T(8,128)S(1)}, f32[1,1,8,32,256]{4,3,2,1,0:T(8,128)S(1)}, u32[]{:S(2)}, u32[]{:S(2)}) collective-permute-start(f32[1,1,8,32,256]{4,3,2,1,0:T(8,128)S(1)} %bitcast.194), channel_id=1, source_target_pairs={{0,16},{8,24},{16,0},{24,8},{1,17},{9,25},{17,1},{25,9},{2,18},{10... | collective-permute-start | bytes 786440 | tf_op jit(solution)/shard_map/ppermute | solution.py:18
  43.6 19.6 %collective-permute-start.12 = (f32[1,8,32,256]{3,2,1,0:T(8,128)S(1)}, f32[1,8,32,256]{3,2,1,0:T(8,128)S(1)}, u32[]{:S(2)}, u32[]{:S(2)}) collective-permute-start(f32[1,8,32,256]{3,2,1,0:T(8,128)S(1)} %add_bitcast_fusion.7.refs_2_), channel_id=1, source_target_pairs={{0,4},{4,0},{1,5},{5,1},{2,6},{6,2},{3,7},{7,3},{8,12},{12,8},{9,1... | collective-permute-start | bytes 786440 | tf_op jit(solution)/shard_map/ppermute | solution.py:18
  47.2 7.6 %collective-permute-start.9 = (f32[1,1,8,32,256]{4,3,2,1,0:T(8,128)S(1)}, f32[1,1,8,32,256]{4,3,2,1,0:T(8,128)S(1)}, u32[]{:S(2)}, u32[]{:S(2)}) collective-permute-start(f32[1,1,8,32,256]{4,3,2,1,0:T(8,128)S(1)} %bitcast.196), channel_id=1, source_target_pairs={{0,16},{8,24},{16,0},{24,8},{1,17},{9,25},{17,1},{25,9},{2,18},{10... | collective-permute-start | bytes 786440 | tf_op jit(solution)/shard_map/ppermute | solution.py:18
  48.3 23.4 %collective-permute-start.14 = (f32[1,8,32,256]{3,2,1,0:T(8,128)S(1)}, f32[1,8,32,256]{3,2,1,0:T(8,128)S(1)}, u32[]{:S(2)}, u32[]{:S(2)}) collective-permute-start(f32[1,8,32,256]{3,2,1,0:T(8,128)S(1)} %add_bitcast_fusion.6.refs_0_), channel_id=1, source_target_pairs={{0,4},{4,0},{1,5},{5,1},{2,6},{6,2},{3,7},{7,3},{8,12},{12,8},{9,1... | collective-permute-start | bytes 786440 | tf_op jit(solution)/shard_map/ppermute | solution.py:18
  53.0 9.3 %collective-permute-start.11 = (f32[1,1,8,32,256]{4,3,2,1,0:T(8,128)S(1)}, f32[1,1,8,32,256]{4,3,2,1,0:T(8,128)S(1)}, u32[]{:S(2)}, u32[]{:S(2)}) collective-permute-start(f32[1,1,8,32,256]{4,3,2,1,0:T(8,128)S(1)} %bitcast.197), channel_id=1, source_target_pairs={{0,16},{8,24},{16,0},{24,8},{1,17},{9,25},{17,1},{25,9},{2,18},{10... | collective-permute-start | bytes 786440 | tf_op jit(solution)/shard_map/ppermute | solution.py:18
  54.9 15.8 %collective-permute-start.13 = (f32[1,3,8,16,256]{4,3,2,1,0:T(8,128)S(1)}, f32[1,3,8,16,256]{4,3,2,1,0:T(8,128)S(1)}, u32[]{:S(2)}, u32[]{:S(2)}) collective-permute-start(f32[1,3,8,16,256]{4,3,2,1,0:T(8,128)S(1)} %pad_maximum_fusion.2), channel_id=1, source_target_pairs={{0,16},{8,24},{16,0},{24,8},{1,17},{9,25},{17,1},{25,9},{2,18},{10... | collective-permute-start | bytes 1179656 | tf_op jit(solution)/shard_map/ppermute | solution.py:18
  56.5 16.7 %collective-permute-start.15 = (f32[1,8,32,256]{3,2,1,0:T(8,128)S(1)}, f32[1,8,32,256]{3,2,1,0:T(8,128)S(1)}, u32[]{:S(2)}, u32[]{:S(2)}) collective-permute-start(f32[1,8,32,256]{3,2,1,0:T(8,128)S(1)} %add_bitcast_fusion.5.refs_1_), channel_id=1, source_target_pairs={{0,4},{4,0},{1,5},{5,1},{2,6},{6,2},{3,7},{7,3},{8,12},{12,8},{9,1... | collective-permute-start | bytes 786440 | tf_op jit(solution)/shard_map/ppermute | solution.py:18
  62.3 10.9 %collective-permute-start.16 = (f32[1,8,32,256]{3,2,1,0:T(8,128)S(1)}, f32[1,8,32,256]{3,2,1,0:T(8,128)S(1)}, u32[]{:S(2)}, u32[]{:S(2)}) collective-permute-start(f32[1,8,32,256]{3,2,1,0:T(8,128)S(1)} %add_bitcast_fusion.4.refs_2_), channel_id=1, source_target_pairs={{0,4},{4,0},{1,5},{5,1},{2,6},{6,2},{3,7},{7,3},{8,12},{12,8},{9,1... | collective-permute-start | bytes 786440 | tf_op jit(solution)/shard_map/ppermute | solution.py:18
  63.3 14.6 %collective-permute-start.20 = (f32[1,3,8,16,256]{4,3,2,1,0:T(8,128)S(1)}, f32[1,3,8,16,256]{4,3,2,1,0:T(8,128)S(1)}, u32[]{:S(2)}, u32[]{:S(2)}) collective-permute-start(f32[1,3,8,16,256]{4,3,2,1,0:T(8,128)S(1)} %pad_maximum_fusion.1), channel_id=1, source_target_pairs={{0,16},{8,24},{16,0},{24,8},{1,17},{9,25},{17,1},{25,9},{2,18},{10... | collective-permute-start | bytes 1179656 | tf_op jit(solution)/shard_map/ppermute | solution.py:18
  70.8 19.5 %collective-permute-start.23 = (f32[3,8,16,256]{3,2,1,0:T(8,128)S(1)}, f32[3,8,16,256]{3,2,1,0:T(8,128)S(1)}, u32[]{:S(2)}, u32[]{:S(2)}) collective-permute-start(f32[3,8,16,256]{3,2,1,0:T(8,128)S(1)} %add_bitcast_fusion.1.refs_3_), channel_id=1, source_target_pairs={{0,4},{4,0},{1,5},{5,1},{2,6},{6,2},{3,7},{7,3},{8,12},{12,8},{9,1... | collective-permute-start | bytes 1179656 | tf_op jit(solution)/shard_map/ppermute | solution.py:18
  71.7 8.3 %collective-permute-start.21 = (f32[1,1,8,16,256]{4,3,2,1,0:T(8,128)S(1)}, f32[1,1,8,16,256]{4,3,2,1,0:T(8,128)S(1)}, u32[]{:S(2)}, u32[]{:S(2)}) collective-permute-start(f32[1,1,8,16,256]{4,3,2,1,0:T(8,128)S(1)} %get-tuple-element.111), channel_id=1, source_target_pairs={{0,16},{8,24},{16,0},{24,8},{1,17},{9,25},{17,1},{25,9},{2,18},{10... | collective-permute-start | bytes 393224 | tf_op jit(solution)/shard_map/ppermute | solution.py:18
  74.1 8.1 %collective-permute-start.17 = (f32[2,4,64,128]{3,2,1,0:T(8,128)S(1)}, f32[2,4,64,128]{3,2,1,0:T(8,128)S(1)}, u32[]{:S(2)}, u32[]{:S(2)}) collective-permute-start(f32[2,4,64,128]{3,2,1,0:T(8,128)S(1)} %dynamic-slice_bitcast_fusion.2), channel_id=1, source_target_pairs={{0,8},{8,0},{16,24},{24,16},{1,9},{9,1},{17,25},{25,17},{2,10},{10... | collective-permute-start | bytes 786440 | tf_op jit(solution)/shard_map/ppermute | solution.py:18
  77.9 15.8 %collective-permute-start.22 = (f32[3,8,16,256]{3,2,1,0:T(8,128)S(1)}, f32[3,8,16,256]{3,2,1,0:T(8,128)S(1)}, u32[]{:S(2)}, u32[]{:S(2)}) collective-permute-start(f32[3,8,16,256]{3,2,1,0:T(8,128)S(1)} %add_bitcast_fusion.refs_3_), channel_id=1, source_target_pairs={{0,4},{4,0},{1,5},{5,1},{2,6},{6,2},{3,7},{7,3},{8,12},{12,8},{9,1... | collective-permute-start | bytes 1179656 | tf_op jit(solution)/shard_map/ppermute | solution.py:18
  79.5 8.2 %collective-permute-start.28 = (f32[1,2,8,16,256]{4,3,2,1,0:T(8,128)S(1)}, f32[1,2,8,16,256]{4,3,2,1,0:T(8,128)S(1)}, u32[]{:S(2)}, u32[]{:S(2)}) collective-permute-start(f32[1,2,8,16,256]{4,3,2,1,0:T(8,128)S(1)} %pad_maximum_fusion.5), channel_id=1, source_target_pairs={{0,16},{8,24},{16,0},{24,8},{1,17},{9,25},{17,1},{25,9},{2,18},{10... | collective-permute-start | bytes 786440 | tf_op jit(solution)/shard_map/ppermute | solution.py:18
  80.1 19.7 %collective-permute-start.33 = (f32[1,8,16,256]{3,2,1,0:T(8,128)S(1)}, f32[1,8,16,256]{3,2,1,0:T(8,128)S(1)}, u32[]{:S(2)}, u32[]{:S(2)}) collective-permute-start(f32[1,8,16,256]{3,2,1,0:T(8,128)S(1)} %add_bitcast_fusion.11.refs_4_), channel_id=1, source_target_pairs={{0,4},{4,0},{1,5},{5,1},{2,6},{6,2},{3,7},{7,3},{8,12},{12,8},{9,1... | collective-permute-start | bytes 393224 | tf_op jit(solution)/shard_map/ppermute | solution.py:18
  82.2 13.8 %collective-permute-start.29 = (f32[1,2,8,16,256]{4,3,2,1,0:T(8,128)S(1)}, f32[1,2,8,16,256]{4,3,2,1,0:T(8,128)S(1)}, u32[]{:S(2)}, u32[]{:S(2)}) collective-permute-start(f32[1,2,8,16,256]{4,3,2,1,0:T(8,128)S(1)} %pad_maximum_fusion.4), channel_id=1, source_target_pairs={{0,16},{8,24},{16,0},{24,8},{1,17},{9,25},{17,1},{25,9},{2,18},{10... | collective-permute-start | bytes 786440 | tf_op jit(solution)/shard_map/ppermute | solution.py:18
  87.7 8.5 %collective-permute-start.18 = (f32[2,2,64,128]{3,2,1,0:T(8,128)S(1)}, f32[2,2,64,128]{3,2,1,0:T(8,128)S(1)}, u32[]{:S(2)}, u32[]{:S(2)}) collective-permute-start(f32[2,2,64,128]{3,2,1,0:T(8,128)S(1)} %dynamic-slice_bitcast_fusion.4), channel_id=1, source_target_pairs={{0,2},{1,3},{2,0},{3,1},{4,6},{5,7},{6,4},{7,5},{8,10},{9,11},{10,... | collective-permute-start | bytes 393224 | tf_op jit(solution)/shard_map/ppermute | solution.py:18
  90.3 11.1 %collective-permute-start.34 = (f32[2,8,16,256]{3,2,1,0:T(8,128)S(1)}, f32[2,8,16,256]{3,2,1,0:T(8,128)S(1)}, u32[]{:S(2)}, u32[]{:S(2)}) collective-permute-start(f32[2,8,16,256]{3,2,1,0:T(8,128)S(1)} %add_bitcast_fusion.3.refs_5_), channel_id=1, source_target_pairs={{0,4},{4,0},{1,5},{5,1},{2,6},{6,2},{3,7},{7,3},{8,12},{12,8},{9,1... | collective-permute-start | bytes 786440 | tf_op jit(solution)/shard_map/ppermute | solution.py:18
  96.1 11.6 %collective-permute-start.31 = (f32[2,8,16,256]{3,2,1,0:T(8,128)S(1)}, f32[2,8,16,256]{3,2,1,0:T(8,128)S(1)}, u32[]{:S(2)}, u32[]{:S(2)}) collective-permute-start(f32[2,8,16,256]{3,2,1,0:T(8,128)S(1)} %add_bitcast_fusion.2.refs_4_), channel_id=1, source_target_pairs={{0,4},{4,0},{1,5},{5,1},{2,6},{6,2},{3,7},{7,3},{8,12},{12,8},{9,1... | collective-permute-start | bytes 786440 | tf_op jit(solution)/shard_map/ppermute | solution.py:18
  98.8 9.0 %collective-permute-start.32 = (f32[1,8,16,256]{3,2,1,0:T(8,128)S(1)}, f32[1,8,16,256]{3,2,1,0:T(8,128)S(1)}, u32[]{:S(2)}, u32[]{:S(2)}) collective-permute-start(f32[1,8,16,256]{3,2,1,0:T(8,128)S(1)} %add_bitcast_fusion.10.refs_5_), channel_id=1, source_target_pairs={{0,4},{4,0},{1,5},{5,1},{2,6},{6,2},{3,7},{7,3},{8,12},{12,8},{9,1... | collective-permute-start | bytes 393224 | tf_op jit(solution)/shard_map/ppermute | solution.py:18
  99.4 10.9 %collective-permute-start.25 = (f32[2,2,80,128]{3,2,1,0:T(8,128)S(1)}, f32[2,2,80,128]{3,2,1,0:T(8,128)S(1)}, u32[]{:S(2)}, u32[]{:S(2)}) collective-permute-start(f32[2,2,80,128]{3,2,1,0:T(8,128)S(1)} %dynamic-slice_bitcast_fusion.3), channel_id=1, source_target_pairs={{0,2},{1,3},{2,0},{3,1},{4,6},{5,7},{6,4},{7,5},{8,10},{9,11},{10,... | collective-permute-start | bytes 491528 | tf_op jit(solution)/shard_map/ppermute | solution.py:18
  99.8 12.2 %collective-permute-start.19 = (f32[2,1,64,128]{3,2,1,0:T(8,128)S(1)}, f32[2,1,64,128]{3,2,1,0:T(8,128)S(1)}, u32[]{:S(2)}, u32[]{:S(2)}) collective-permute-start(f32[2,1,64,128]{3,2,1,0:T(8,128)S(1)} %constant_dynamic-slice_fusion.1), channel_id=1, source_target_pairs={{0,1},{1,0},{2,3},{3,2},{4,5},{5,4},{6,7},{7,6},{8,9},{9,8},{10,11... | collective-permute-start | bytes 196616 | tf_op jit(solution)/shard_map/ppermute | solution.py:18
  110.2 5.1 %collective-permute-start.35 = (f32[2,4,112,128]{3,2,1,0:T(8,128)S(1)}, f32[2,4,112,128]{3,2,1,0:T(8,128)S(1)}, u32[]{:S(2)}, u32[]{:S(2)}) collective-permute-start(f32[2,4,112,128]{3,2,1,0:T(8,128)S(1)} %dynamic-slice_bitcast_fusion), channel_id=1, source_target_pairs={{0,8},{8,0},{16,24},{24,16},{1,9},{9,1},{17,25},{25,17},{2,10},{10... | collective-permute-start | bytes 1376264 | tf_op jit(solution)/shard_map/ppermute | solution.py:18
  116.1 17.7 %all-to-all-start = ((f32[8,112,128]{2,1,0:T(8,128)}), f32[8,112,128]{2,1,0:T(8,128)S(1)}, u32[]{:S(2)}, u32[]{:S(2)}) async-start(f32[8,112,128]{2,1,0:T(8,128)} %bitcast.99), calls=%async_computation | async-start | bytes 917504 | tf_op jit(solution)/shard_map/all_to_all | solution.py:209
  120.0 5.8 %collective-permute-start.27 = (f32[144,128]{1,0:T(8,128)S(1)}, f32[144,128]{1,0:T(8,128)S(1)}, u32[]{:S(2)}, u32[]{:S(2)}) collective-permute-start(f32[144,128]{1,0:T(8,128)S(1)} %fusion.1), channel_id=1, source_target_pairs={{0,16},{8,24},{16,0},{24,8},{1,17},{9,25},{17,1},{25,9},{2,18},{10... | collective-permute-start | bytes 221192 | tf_op jit(solution)/shard_map/ppermute | solution.py:18
  (7 other events, 22.1 us)
